TPU v7x, 32 devices: a whole 2x2x4 slice. The times are simulated.
32 devices in a mesh: lat: 4 (over y, x), lon: 8 (over z, core).
Axes of the slice: x: 2, y: 2, z: 4, core: 2. Of those that a mesh axis runs over, the one named last changes fastest.
Arguments:
- prior_state: bfloat16 [2, 4, 80, 32, 1024], P(None, None, None, 'lat', 'lon'), may hold values from -6 to 6
- courant: float32 [2, 4, 32, 1024], P(None, None, 'lat', 'lon'), may hold values from -0.45 to 0.45
- obs_tile: int32 [64], replicated, may hold values from 0 to 31, as said below
- obs_site: int32 [64], replicated, may hold values from 0 to 8191
- obs_value: float32 [64], replicated, may hold values from -6 to 6
- obs_var: float32 [64], replicated, may hold values from 0.2 to 2
- loc_bits: int32 [64, 2], replicated, may hold values from 0 to 1073741823
- batch_order: int32 [4], replicated, may hold values from 0 to 3, each once
Outputs:
- analysis: bfloat16 [2, 4, 80, 32, 1024], P(None, None, None, 'lat', 'lon')
Inputs may be any that keep to these rules, and one draw needn't show every extreme that they name: `obs_tile`: in each batch of 16 consecutive observations one tile owns exactly 4 observations and every other tile at most one. `loc_bits`: bits of tiles numbered 32 or more are not read.
All inputs are finite; a program needn't handle non-finite values.
Results may differ from a plain program's by a relative error of at most 0.0013.
Values may be sent and summed in bfloat16 or wider, within the bound.
No kernel may reach another device: no remote copies, remote signals or barrier semaphores. Data moves between devices by JAX's collectives and lax.ppermute only.
A program may use at most 64 MiB of HBM per device.

v0:
```python
import jax
import jax.numpy as jnp
from jax import lax
from jax.sharding import PartitionSpec as P

OBSERVED_BATCH = 16
BATCHES = 4
CAP = 4


EPSILON = 1e-05
HIGHEST_PRECISE = lax.Precision.HIGHEST


def padded(cells, sides, width, closed):
    for axis, dim in sides:
        count = lax.axis_size(axis)
        ends = count if closed else count - 1
        head = lax.slice_in_dim(cells, 0, width, axis=dim)
        tail = lax.slice_in_dim(cells, cells.shape[dim] - width, cells.shape[dim], axis=dim)
        cells = jnp.concatenate(
            [
                lax.ppermute(tail, axis, [(i, (i + 1) % count) for i in range(ends)]),
                cells,
                lax.ppermute(head, axis, [((i + 1) % count, i) for i in range(ends)]),
            ],
            axis=dim,
        )
    return cells


def upwind_transport(center_value, west, east, south, north, along_lon, along_lat):
    return (
        center_value
        - jnp.maximum(along_lon, 0.0) * (center_value - west)
        - jnp.minimum(along_lon, 0.0) * (east - center_value)
        - jnp.maximum(along_lat, 0.0) * (center_value - south)
        - jnp.minimum(along_lat, 0.0) * (north - center_value)
    )


def tile_bits(loc_bits, tile_ids):
    bit_words = jnp.take(loc_bits, tile_ids // 30, axis=1)
    return jnp.bitwise_and(jnp.right_shift(bit_words, (tile_ids % 30)[None, :]), 1).astype(
        jnp.float32
    )


def eakf_step(prior_row, obs_val, obs_err, member_list):
    mean_prior = jnp.mean(prior_row)
    anomaly = prior_row - mean_prior
    spread = jnp.sum(anomaly * anomaly) / (member_list - 1) + EPSILON
    post_var = spread * obs_err / (spread + obs_err)
    post_mean = post_var * (mean_prior / spread + obs_val / obs_err)
    factor = jnp.sqrt(obs_err / (spread + obs_err))
    increment = factor * anomaly + post_mean - prior_row
    weights = anomaly / ((member_list - 1) * spread)
    return (increment, weights)


def per_device(prior_state, courant, obs_tile, obs_site, obs_value, obs_var, loc_bits, batch_order):
    field_stack, level_list, member_list, rows_dev, cols_dev = prior_state.shape
    count_of_cells = rows_dev * cols_dev
    south_north = padded(prior_state, (("lat", 3),), 1, False)
    west_east = padded(prior_state, (("lon", 4),), 1, True)
    prediction = upwind_transport(
        prior_state.astype(jnp.float32),
        west_east[..., :-2].astype(jnp.float32),
        west_east[..., 2:].astype(jnp.float32),
        south_north[..., :-2, :].astype(jnp.float32),
        south_north[..., 2:, :].astype(jnp.float32),
        courant[0][None, :, None],
        courant[1][None, :, None],
    )
    flattened_prediction = prediction.reshape(field_stack * level_list, member_list, count_of_cells)
    tile_self = lax.axis_index("lat") * lax.axis_size("lon") + lax.axis_index("lon")
    own_bits = tile_bits(loc_bits, tile_self[None])[:, 0]
    identity = jnp.eye(member_list, dtype=jnp.float32)
    current_state = flattened_prediction
    lower_pair = lax.broadcasted_iota(
        jnp.int32, (OBSERVED_BATCH, OBSERVED_BATCH), 0
    ) < lax.broadcasted_iota(jnp.int32, (OBSERVED_BATCH, OBSERVED_BATCH), 1)
    for order_index in range(BATCHES):
        batch_offset = batch_order[order_index] * OBSERVED_BATCH
        owner_tiles = lax.dynamic_slice_in_dim(obs_tile, batch_offset, OBSERVED_BATCH)
        sites = lax.dynamic_slice_in_dim(obs_site, batch_offset, OBSERVED_BATCH)
        obs_values = lax.dynamic_slice_in_dim(obs_value, batch_offset, OBSERVED_BATCH)
        obs_errors = lax.dynamic_slice_in_dim(obs_var, batch_offset, OBSERVED_BATCH)
        batch_bits = lax.dynamic_slice_in_dim(loc_bits, batch_offset, OBSERVED_BATCH, 0)
        mine_mask = lax.dynamic_slice_in_dim(own_bits, batch_offset, OBSERVED_BATCH)
        plane_index = sites // count_of_cells
        cell_index = sites % count_of_cells
        owned_here = owner_tiles == tile_self
        local_prior = current_state[plane_index, :, cell_index]
        same_owner = owner_tiles[:, None] == owner_tiles[None, :]
        slot_rank = jnp.sum((same_owner & lower_pair).astype(jnp.int32), axis=0)
        slot_ids = jnp.arange(CAP, dtype=jnp.int32)
        selector = (owned_here[None, :] & (slot_rank[None, :] == slot_ids[:, None])).astype(
            jnp.float32
        )
        outgoing = jnp.dot(selector, local_prior, precision=HIGHEST_PRECISE)
        collected = lax.all_gather(outgoing, ("lat", "lon"), axis=0, tiled=True)
        prior_values = collected[owner_tiles * CAP + slot_rank]
        cross_mask = tile_bits(batch_bits, owner_tiles)

        def advance(obs_index, loop_state):
            prior_values, transform_now = loop_state
            increment, weights = eakf_step(
                prior_values[obs_index], obs_values[obs_index], obs_errors[obs_index], member_list
            )
            projected = jnp.dot(prior_values, weights, precision=HIGHEST_PRECISE)
            prior_values = (
                prior_values
                + cross_mask[obs_index][:, None] * projected[:, None] * increment[None, :]
            )
            turned = jnp.dot(transform_now, weights, precision=HIGHEST_PRECISE)
            transform_now = (
                transform_now + mine_mask[obs_index] * turned[:, None] * increment[None, :]
            )
            return (prior_values, transform_now)

        prior_values, transform_now = lax.fori_loop(
            0, OBSERVED_BATCH, advance, (prior_values, identity)
        )
        current_state = jnp.einsum(
            "pec,eg->pgc", current_state, transform_now, precision=HIGHEST_PRECISE
        )
    return current_state.reshape(field_stack, level_list, member_list, rows_dev, cols_dev).astype(
        jnp.bfloat16
    )


def solution(mesh):
    placed = (
        P(None, None, None, "lat", "lon"),
        P(None, None, "lat", "lon"),
        P(),
        P(),
        P(),
        P(),
        P(),
        P(),
    )
    return jax.shard_map(
        per_device,
        mesh=mesh,
        in_specs=placed,
        out_specs=P(None, None, None, "lat", "lon"),
        check_vma=False,
    )
```

profile of v0, /device:TPU:0, one launch (start us, length us, event | category | flops | bytes accessed | tf_op | source)
XLA Modules:
  0.0 799.7 jit_solution(16305724905719371598)
XLA Ops:
  0.0 3.3 fusion.91
  3.4 2.3 copy.73
  6.9 4.1 collective-permute-start.1
  11.4 3.9 collective-permute-start.2
  15.4 1.3 collective-permute-start.3
  28.2 1.7 copy.46
  30.5 5.6 fusion.23
  36.1 4.9 copy.51
  41.0 1.3 gather_fusion
  42.4 41.6 %all-gather = f32[32,4,80]{2,1,0:T(4,128)S(1)} all-gather(f32[1,4,80]{2,1,0:T(4,128)S(1)} %convolution_bitcast_fusion.14), channel_id=1, replica_groups=mesh['lat'=4,'lon'=8] {'lat','lon'}, dimensions={0}, use_global_device_ids=true | all-gather | bytes 42240 | tf_op jit(solution)/shard_map/all_gather | solution.py:102
  84.5 139.3 %while.61 = (s32[]{:T(128)}, f32[16,80]{1,0:T(8,128)S(1)}, f32[80,80]{1,0:T(8,128)S(1)}, f32[16,16]{1,0:T(8,128)S(1)}, f32[16]{0:T(128)S(1)}, /*index=5*/f32[16]...) while((s32[]{:T(128)}, f32[16,80]{1,0:T(8,128)S(1)}, ...), condition=%wide.region_7.9_spmd, body=%wide.region_4.8_spmd.sunk | while | flops 108588 | bytes 96229 | solution.py:122
  92.1 0.8 fusion.146
  100.8 0.8 fusion.146
  109.6 0.8 fusion.146
  118.3 0.8 fusion.146
  127.0 0.8 fusion.146
  135.7 0.8 fusion.146
  144.4 0.8 fusion.146
  153.1 0.8 fusion.146
  161.8 0.8 fusion.146
  170.5 0.8 fusion.146
  179.2 0.8 fusion.146
  187.9 0.8 fusion.146
  196.6 0.8 fusion.146
  205.3 0.8 fusion.146
  214.0 0.8 fusion.146
  222.7 0.8 fusion.146
  223.9 6.7 convolution_bitcast_fusion.8
  230.6 3.3 copy.55
  233.9 1.3 gather_fusion.2
  235.3 36.9 %all-gather.1 = f32[32,4,80]{2,1,0:T(4,128)S(1)} all-gather(f32[1,4,80]{2,1,0:T(4,128)S(1)} %convolution_bitcast_fusion.13), channel_id=1, replica_groups=mesh['lat'=4,'lon'=8] {'lat','lon'}, dimensions={0}, use_global_device_ids=true | all-gather | bytes 42240 | tf_op jit(solution)/shard_map/all_gather | solution.py:102
  272.8 142.9 %while.62 = (s32[]{:T(128)}, f32[16,80]{1,0:T(8,128)S(1)}, f32[80,80]{1,0:T(8,128)S(1)}, f32[16,16]{1,0:T(8,128)S(1)}, f32[16]{0:T(128)S(1)}, /*index=5*/f32[16]...) while((s32[]{:T(128)}, f32[16,80]{1,0:T(8,128)S(1)}, ...), condition=%wide.region_11.13_spmd, body=%wide.region_8.12_spmd.sunk | while | flops 108588 | bytes 96229 | solution.py:122
  280.6 0.8 fusion.153
  289.5 0.8 fusion.153
  298.5 0.8 fusion.153
  307.4 0.8 fusion.153
  415.7 3.8 convolution_bitcast_fusion.10
  419.6 4.8 copy.58
  424.4 1.3 gather_fusion.4
  425.8 38.2 %all-gather.2 = f32[32,4,80]{2,1,0:T(4,128)S(1)} all-gather(f32[1,4,80]{2,1,0:T(4,128)S(1)} %convolution_bitcast_fusion.12), channel_id=1, replica_groups=mesh['lat'=4,'lon'=8] {'lat','lon'}, dimensions={0}, use_global_device_ids=true | all-gather | bytes 42240 | tf_op jit(solution)/shard_map/all_gather | solution.py:102
  464.7 141.5 %while.63 = (s32[]{:T(128)}, f32[16,80]{1,0:T(8,128)S(1)}, f32[80,80]{1,0:T(8,128)S(1)}, f32[16,16]{1,0:T(8,128)S(1)}, f32[16]{0:T(128)S(1)}, /*index=5*/f32[16]...) while((s32[]{:T(128)}, f32[16,80]{1,0:T(8,128)S(1)}, ...), condition=%wide.region_15.17_spmd, body=%wide.region_12.16_spmd.sunk | while | flops 108588 | bytes 96229 | solution.py:122
  606.2 3.8 convolution_bitcast_fusion.9
  610.0 4.8 copy.61
  614.9 1.3 gather_fusion.6
  616.3 37.1 %all-gather.3 = f32[32,4,80]{2,1,0:T(4,128)S(1)} all-gather(f32[1,4,80]{2,1,0:T(4,128)S(1)} %convolution_bitcast_fusion.11), channel_id=1, replica_groups=mesh['lat'=4,'lon'=8] {'lat','lon'}, dimensions={0}, use_global_device_ids=true | all-gather | bytes 42240 | tf_op jit(solution)/shard_map/all_gather | solution.py:102
  654.0 141.9 %while.64 = (s32[]{:T(128)}, f32[16,80]{1,0:T(8,128)S(1)}, f32[80,80]{1,0:T(8,128)S(1)}, f32[16,16]{1,0:T(8,128)S(1)}, f32[16]{0:T(128)S(1)}, /*index=5*/f32[16]...) while((s32[]{:T(128)}, f32[16,80]{1,0:T(8,128)S(1)}, ...), condition=%wide.region_19.21_spmd, body=%wide.region_16.20_spmd.sunk | while | flops 108588 | bytes 96229 | solution.py:122
  795.9 2.3 convolution_convert_fusion
  798.2 1.4 copy.77
  (758 shorter events, 260.8 us)
Async XLA Ops:
  3.3 7.7 copy-start.2
  3.3 13.4 %copy-start.13 = (s32[4]{0:T(128)S(1)}, s32[4]{0:T(128)}, u32[]{:S(2)}) copy-start(s32[4]{0:T(128)} %param.25) | copy-start | bytes 52
  3.3 16.6 %copy-start.9 = (s32[64]{0:T(128)S(1)}, s32[64]{0:T(128)}, u32[]{:S(2)}) copy-start(s32[64]{0:T(128)} %param.20) | copy-start | bytes 772
  3.3 19.4 %copy-start.10 = (s32[64]{0:T(128)S(1)}, s32[64]{0:T(128)}, u32[]{:S(2)}) copy-start(s32[64]{0:T(128)} %param.21) | copy-start | bytes 772
  3.3 19.6 %copy-start.7 = (f32[2,4,8,128]{3,2,1,0:T(8,128)S(1)}, f32[2,4,8,128]{3,2,1,0:T(8,128)}, u32[]{:S(2)}) copy-start(f32[2,4,8,128]{3,2,1,0:T(8,128)} %param.19) | copy-start | bytes 98308
  3.3 19.7 %copy-start.8 = (s32[64,2]{0,1:T(2,128)S(1)}, s32[64,2]{0,1:T(2,128)}, u32[]{:S(2)}) copy-start(s32[64,2]{0,1:T(2,128)} %param.24) | copy-start | bytes 1540
  3.3 20.4 %copy-start.11 = (f32[64]{0:T(128)S(1)}, f32[64]{0:T(128)}, u32[]{:S(2)}) copy-start(f32[64]{0:T(128)} %param.22) | copy-start | bytes 772
  3.4 20.4 %copy-start.12 = (f32[64]{0:T(128)S(1)}, f32[64]{0:T(128)}, u32[]{:S(2)}) copy-start(f32[64]{0:T(128)} %param.23) | copy-start | bytes 772
  5.6 21.9 %collective-permute-start = (bf16[2,4,80,8,1]{2,3,4,1,0:T(8,128)(2,1)S(1)}, bf16[2,4,80,8,1]{2,3,4,1,0:T(8,128)(2,1)S(1)}, u32[]{:S(2)}, u32[]{:S(2)}) collective-permute-start(bf16[2,4,80,8,1]{2,3,4,1,0:T(8,128)(2,1)S(1)} %copy.73), channel_id=1, source_target_pairs={{0,1},{1,2},{2,3},{3,4},{4,5},{5,6},{6,7},{7,0},{8,9},{9,10},{10,1... | collective-permute-start | bytes 30728 | tf_op jit(solution)/shard_map/ppermute | solution.py:23
  6.9 21.3 %collective-permute-start.1 = (bf16[2,4,80,8,1]{2,3,4,1,0:T(8,128)(2,1)S(1)}, bf16[2,4,80,8,1]{2,3,4,1,0:T(8,128)(2,1)S(1)}, u32[]{:S(2)}, u32[]{:S(2)}) collective-permute-start(bf16[2,4,80,8,1]{2,3,4,1,0:T(8,128)(2,1)S(1)} %copy.74), channel_id=1, source_target_pairs={{1,0},{2,1},{3,2},{4,3},{5,4},{6,5},{7,6},{0,7},{9,8},{10,9},{11,1... | collective-permute-start | bytes 30728 | tf_op jit(solution)/shard_map/ppermute | solution.py:25
  11.4 18.5 %collective-permute-start.2 = (bf16[2,4,80,1,128]{4,2,3,1,0:T(8,128)(2,1)S(1)}, bf16[2,4,80,1,128]{4,2,3,1,0:T(8,128)(2,1)S(1)}, u32[]{:S(2)}, u32[]{:S(2)}) collective-permute-start(bf16[2,4,80,1,128]{4,2,3,1,0:T(8,128)(2,1)S(1)} %copy.75), channel_id=1, source_target_pairs={{0,8},{8,16},{16,24},{1,9},{9,17},{17,25},{2,10},{10,18},{18,26},{... | collective-permute-start | bytes 491528 | tf_op jit(solution)/shard_map/ppermute | solution.py:23
  15.4 14.8 %collective-permute-start.3 = (bf16[2,4,80,1,128]{4,2,3,1,0:T(8,128)(2,1)S(1)}, bf16[2,4,80,1,128]{4,2,3,1,0:T(8,128)(2,1)S(1)}, u32[]{:S(2)}, u32[]{:S(2)}) collective-permute-start(bf16[2,4,80,1,128]{4,2,3,1,0:T(8,128)(2,1)S(1)} %copy.76), channel_id=1, source_target_pairs={{8,0},{16,8},{24,16},{9,1},{17,9},{25,17},{10,2},{18,10},{26,18},{... | collective-permute-start | bytes 491528 | tf_op jit(solution)/shard_map/ppermute | solution.py:25
  20.1 2.8 copy-start.20
  20.7 15.3 %copy-start.3 = (f32[80,80]{1,0:T(8,128)}, f32[80,80]{1,0:T(8,128)S(1)}, u32[]{:S(2)}) copy-start(f32[80,80]{1,0:T(8,128)S(1)} %fusion.31) | copy-start | bytes 76804
  21.4 1.7 copy-start.18
  22.1 4.3 copy-start.16
  22.7 3.6 copy-start.14
  36.1 6.2 copy-start.21
  36.1 6.2 copy-start.34
  36.1 48.5 %copy-start.35 = (f32[16]{0:T(128)S(1)}, f32[16]{0:T(128)}, u32[]{:S(2)}) copy-start(f32[16]{0:T(128)} %get-tuple-element.923) | copy-start | bytes 196
  36.1 48.5 %copy-start.36 = (f32[16]{0:T(128)S(1)}, f32[16]{0:T(128)}, u32[]{:S(2)}) copy-start(f32[16]{0:T(128)} %get-tuple-element.922) | copy-start | bytes 196
  36.1 48.5 %copy-start.37 = (f32[16]{0:T(128)S(1)}, f32[16]{0:T(128)}, u32[]{:S(2)}) copy-start(f32[16]{0:T(128)} %get-tuple-element.924) | copy-start | bytes 196
  230.5 4.6 copy-start.19
  230.5 4.6 copy-start.32
  230.5 42.2 %copy-start.5 = (f32[80,80]{1,0:T(8,128)S(1)}, f32[80,80]{1,0:T(8,128)}, u32[]{:S(2)}) copy-start(f32[80,80]{1,0:T(8,128)} %copy-done.3) | copy-start | bytes 76804
  230.6 42.2 %copy-start.30 = (f32[16]{0:T(128)S(1)}, f32[16]{0:T(128)}, u32[]{:S(2)}) copy-start(f32[16]{0:T(128)} %get-tuple-element.959) | copy-start | bytes 196
  230.6 42.2 %copy-start.31 = (f32[16]{0:T(128)S(1)}, f32[16]{0:T(128)}, u32[]{:S(2)}) copy-start(f32[16]{0:T(128)} %get-tuple-element.958) | copy-start | bytes 196
  230.6 42.2 %copy-start.33 = (f32[16]{0:T(128)S(1)}, f32[16]{0:T(128)}, u32[]{:S(2)}) copy-start(f32[16]{0:T(128)} %get-tuple-element.960) | copy-start | bytes 196
  419.5 6.2 copy-start.17
  419.5 6.2 copy-start.28
  419.5 45.1 %copy-start.6 = (f32[80,80]{1,0:T(8,128)S(1)}, f32[80,80]{1,0:T(8,128)}, u32[]{:S(2)}) copy-start(f32[80,80]{1,0:T(8,128)} %copy-done.3) | copy-start | bytes 76804
  419.5 45.1 %copy-start.26 = (f32[16]{0:T(128)S(1)}, f32[16]{0:T(128)}, u32[]{:S(2)}) copy-start(f32[16]{0:T(128)} %get-tuple-element.995) | copy-start | bytes 196
  419.5 45.1 %copy-start.27 = (f32[16]{0:T(128)S(1)}, f32[16]{0:T(128)}, u32[]{:S(2)}) copy-start(f32[16]{0:T(128)} %get-tuple-element.994) | copy-start | bytes 196
  419.5 45.1 %copy-start.29 = (f32[16]{0:T(128)S(1)}, f32[16]{0:T(128)}, u32[]{:S(2)}) copy-start(f32[16]{0:T(128)} %get-tuple-element.996) | copy-start | bytes 196
  419.6 186.6 %copy-start = (f32[8,80,1024]{2,1,0:T(8,128)S(1)}, f32[8,80,1024]{2,1,0:T(8,128)}, u32[]{:S(2)}) copy-start(f32[8,80,1024]{2,1,0:T(8,128)} %convolution_bitcast_fusion.10) | copy-start | bytes 7864324
  610.0 6.2 copy-start.15
  610.0 6.2 copy-start.24
  610.0 44.0 %copy-start.4 = (f32[80,80]{1,0:T(8,128)S(1)}, f32[80,80]{1,0:T(8,128)}, u32[]{:S(2)}) copy-start(f32[80,80]{1,0:T(8,128)} %copy-done.3) | copy-start | bytes 76804
  610.0 44.0 %copy-start.22 = (f32[16]{0:T(128)S(1)}, f32[16]{0:T(128)}, u32[]{:S(2)}) copy-start(f32[16]{0:T(128)} %get-tuple-element.1031) | copy-start | bytes 196
  610.0 44.0 %copy-start.23 = (f32[16]{0:T(128)S(1)}, f32[16]{0:T(128)}, u32[]{:S(2)}) copy-start(f32[16]{0:T(128)} %get-tuple-element.1030) | copy-start | bytes 196
  610.0 44.0 %copy-start.25 = (f32[16]{0:T(128)S(1)}, f32[16]{0:T(128)}, u32[]{:S(2)}) copy-start(f32[16]{0:T(128)} %get-tuple-element.1032) | copy-start | bytes 196
  610.0 185.9 %copy-start.1 = (f32[8,80,1024]{2,1,0:T(8,128)S(1)}, f32[8,80,1024]{2,1,0:T(8,128)}, u32[]{:S(2)}) copy-start(f32[8,80,1024]{2,1,0:T(8,128)} %convolution_bitcast_fusion.9) | copy-start | bytes 7864324
where the time goes:
time: 805 us; the launch traced here: 800 us
  loops' own time  303 us (38%)
  local copies, waits for them, and re-layouts  156 us (19%)
  blocking collectives  154 us (19%)
  other arithmetic  97.6 us (12%)
  matrix products  76.6 us (10%)
  starting transfers between devices  9.75 us (1%)
    another operation x4, loops' own time, per_device(): lax.fori_loop(0, OBSERVED_BATCH, advance, (prior_values, identity))  303 us
    all_gather x4, blocking collectives, per_device(): collected = lax.all_gather(outgoing, ('lat', 'lon'), axis=0, tiled=True)  154 us
    dot_general x64, matrix products, advance(): turned = jnp.dot(transform_now, weights, precision=HIGHEST_PRECISE)  50.7 us
    reduce_sum x64, other arithmetic, eakf_step(): mean_prior = jnp.mean(prior_row)  39.3 us
    dynamic_slice x64, local copies, waits for them, and re-layouts, advance(): obs_values[obs_index]  39.2 us
    reduce_sum x64, other arithmetic, eakf_step(): spread = jnp.sum(anomaly * anomaly) / (member_list - 1) + EPSILON  38.5 us
    dynamic_slice x64, local copies, waits for them, and re-layouts, advance(): obs_errors[obs_index]  37.7 us
    dynamic_slice x64, local copies, waits for them, and re-layouts, advance(): mine_mask[obs_index] * turned[:, None] * increment[None, :]  37.7 us
  transfers between devices with their start and end apart: 4, of which 0 were waited for; matrix products, arithmetic and copies ran while one was open for 1% of the time, Pallas kernels for 0%

commit v1 on v0

v1 whole, which is shorter than its diff:
```python
import functools

import jax
import jax.numpy as jnp
from jax import lax
from jax.experimental import pallas as pl
from jax.experimental.pallas import tpu as pltpu
from jax.sharding import PartitionSpec as P

EPSILON = 1e-05
HIGHEST = lax.Precision.HIGHEST
LANES = 128
SUBLANES = 8
F32 = jnp.float32
BF16 = jnp.bfloat16
VMEM = pl.BlockSpec(memory_space=pltpu.VMEM)
SMEM = pl.BlockSpec(memory_space=pltpu.SMEM)
HBM = pl.BlockSpec(memory_space=pl.ANY)
PARAMS = pltpu.CompilerParams(vmem_limit_bytes=48 * 1024 * 1024)


def iota(shape, dim):
    return lax.broadcasted_iota(jnp.int32, shape, dim)


def in_order(row, order_ref):
    nobs = row.shape[1]
    batches = order_ref.shape[0]
    batch = nobs // batches
    wide = jnp.concatenate([row, jnp.zeros((1, LANES - nobs), row.dtype)], axis=1)
    wide = jnp.broadcast_to(wide, (SUBLANES, LANES))
    lane = iota((SUBLANES, LANES), 1)
    result = jnp.zeros_like(wide)
    for i in range(batches):
        moved = pltpu.roll(wide, lax.rem(i * batch - order_ref[i] * batch + LANES, LANES), 1)
        result = jnp.where(lane // batch == i, moved, result)
    return result


def observe_kernel(n_lat, n_lon, levels, x_ref, courant_ref, tile_ref, site_ref, order_ref, pay_ref):
    planes, depth, cols = x_ref.shape
    rows = courant_ref.shape[0] // (2 * levels)
    members = depth // rows
    nobs = tile_ref.shape[1]
    cells = rows * cols
    my_lat, my_lon = lax.axis_index("lat"), lax.axis_index("lon")
    me = my_lat * n_lon + my_lon

    tile = in_order(tile_ref[...], order_ref)
    site = in_order(site_ref[...], order_ref)
    tile = tile + pltpu.roll(tile, nobs, 1)
    site = site + pltpu.roll(site, nobs, 1)
    shape = (SUBLANES, LANES)
    lane = iota(shape, 1)
    sub = iota(shape, 0)
    first = lane < nobs
    plane = site // cells
    row = (site // cols) % rows
    col = site % cols
    level = plane % levels
    lat, lon = tile // n_lon, tile % n_lon
    owner = tile == me
    from_west = (lat == my_lat) & ((lon + n_lon - 1) % n_lon == my_lon) & (col == 0)
    from_east = (lat == my_lat) & ((lon + 1) % n_lon == my_lon) & (col == cols - 1)
    from_south = (lat - 1 == my_lat) & (lon == my_lon) & (row == 0)
    from_north = (lat + 1 == my_lat) & (lon == my_lon) & (row == rows - 1)
    beside = from_west | from_east
    above = from_south | from_north
    far_col = jnp.where(from_west, cols - 1, jnp.where(from_east, 0, jnp.where(above, col, -1)))
    far_row = jnp.where(from_south, rows - 1, jnp.where(from_north, 0, row))

    down = iota((cols, LANES), 0)
    picked = jnp.dot(
        courant_ref[...], (down == col[:1]).astype(F32), precision=HIGHEST, preferred_element_type=F32
    )
    which = iota((2 * levels * rows, LANES), 0)
    at_cell = (level * rows + row)[:1]
    cu = jnp.sum(jnp.where(which == at_cell, picked, 0.0), axis=0, keepdims=True)
    cv = jnp.sum(jnp.where(which == at_cell + levels * rows, picked, 0.0), axis=0, keepdims=True)
    west, east = jnp.maximum(cu, 0.0), -jnp.minimum(cu, 0.0)
    south, north = jnp.maximum(cv, 0.0), -jnp.minimum(cv, 0.0)
    centre = 1.0 - west - east - south - north

    zero = jnp.zeros(shape, F32)
    own_rows = jnp.where(sub == row, centre, zero)
    own_rows = jnp.where(sub == row - 1, south, own_rows)
    own_rows = jnp.where(sub == row + 1, north, own_rows)
    half0 = jnp.where(first, own_rows, jnp.where(sub == row, west, zero))
    half0 = jnp.where(owner, half0, zero)
    half1 = jnp.where(first, jnp.where(owner & (sub == row), east, zero), ((beside | above) & (sub == far_row)).astype(F32))
    pick0 = (down == jnp.where(first, col, col - 1)[:1]).astype(F32)
    pick1 = (down == jnp.where(first, col + 1, far_col)[:1]).astype(F32)
    picks = jnp.concatenate([pick0, pick1], axis=1).astype(BF16)
    weights = [
        jnp.concatenate([jnp.where(plane == p, half0, zero), jnp.where(plane == p, half1, zero)], axis=1)
        for p in range(planes)
    ]
    parts = []
    group = SUBLANES * rows
    for g in range(members // SUBLANES):
        block = x_ref[:, g * group : (g + 1) * group, :].reshape(planes * group, cols)
        values = jnp.dot(block, picks, preferred_element_type=F32).reshape(planes, SUBLANES, rows, 2 * LANES)
        total = values[0] * weights[0][None]
        for p in range(1, planes):
            total = total + values[p] * weights[p][None]
        parts.append(jnp.sum(total, axis=1))
    both = jnp.concatenate(parts, axis=0)
    low, high = both[:, :LANES], both[:, LANES:]
    lane_m = iota((members, LANES), 1)
    own = low + pltpu.roll(low, nobs, 1) + high
    along_lon = jnp.where(beside[:1], high, 0.0)
    along_lat = jnp.where(above[:1] & (lane_m >= nobs), high, 0.0)
    pay_ref[0:members, :] = jnp.where(lane_m < nobs, own, along_lon)
    half = members // 2
    pay_ref[members : members + half, :] = pltpu.roll(along_lat[:half], nobs, 1) + along_lat[half:]
    factor_lon = jnp.where(col == 0, west, jnp.where(col == cols - 1, east, zero))
    factor_lat = jnp.where(row == 0, south, jnp.where(row == rows - 1, north, zero))
    pay_ref[members + half :, :] = jnp.where(owner, jnp.where(first, factor_lon, factor_lat), zero)


def edges_kernel(rows, x_ref, south_ref, north_ref, west_ref, east_ref, wide_ref):
    planes, depth, cols = x_ref.shape
    members = depth // rows
    lane = iota((rows, LANES), 1)

    @pl.loop(0, planes)
    def _(p):
        west = jnp.zeros((rows, LANES), F32)
        east = jnp.zeros((rows, LANES), F32)
        block = x_ref[p].astype(F32)
        wide_ref[...] = block
        for e in range(members):
            cell = block[e * rows : (e + 1) * rows]
            west = jnp.where(lane == e, pltpu.roll(cell, e, 1) if e else cell, west)
            east = jnp.where(lane == e, pltpu.roll(cell, (e + 1) % LANES, 1), east)
        west_ref[p] = west
        east_ref[p] = east
        south_ref[p] = wide_ref[pl.ds(0, members, stride=rows), :].astype(BF16)
        north_ref[p] = wide_ref[pl.ds(rows - 1, members, stride=rows), :].astype(BF16)


def forecast_kernel(levels, x_ref, courant_ref, south_ref, north_ref, west_ref, east_ref, hi_ref, lo_ref, wide_ref, rows_ref):
    planes, depth, cols = x_ref.shape
    rows = courant_ref.shape[0] // (2 * levels)
    members = depth // rows
    lane = iota((rows, cols), 1)
    sub = iota((rows, cols), 0)

    @pl.loop(0, planes)
    def _(p):
        level = lax.rem(p, levels)
        cu = courant_ref[pl.ds(pl.multiple_of(level * rows, rows), rows), :]
        cv = courant_ref[pl.ds(pl.multiple_of((levels + level) * rows, rows), rows), :]
        west, east = jnp.maximum(cu, 0.0), -jnp.minimum(cu, 0.0)
        south, north = jnp.maximum(cv, 0.0), -jnp.minimum(cv, 0.0)
        centre = 1.0 - west - east - south - north
        rows_ref[0] = south_ref[p].astype(F32)
        rows_ref[1] = north_ref[p].astype(F32)
        halo_west = west_ref[p]
        halo_east = east_ref[p]
        for e in range(members):
            x = x_ref[p, e * rows : (e + 1) * rows, :].astype(F32)
            xw = jnp.where(lane == 0, pltpu.roll(halo_west, (LANES - e) % LANES, 1) if e else halo_west, pltpu.roll(x, 1, 1))
            xe = jnp.where(lane == cols - 1, pltpu.roll(halo_east, (cols - 1 - e) % LANES, 1), pltpu.roll(x, cols - 1, 1))
            xs = jnp.where(sub == 0, rows_ref[0, e : e + 1, :], pltpu.roll(x, 1, 0))
            xn = jnp.where(sub == rows - 1, rows_ref[1, e : e + 1, :], pltpu.roll(x, rows - 1, 0))
            wide_ref[e * rows : (e + 1) * rows, :] = centre * x + west * xw + east * xe + south * xs + north * xn
        for r in range(rows):
            f = wide_ref[pl.ds(r, members, stride=rows), :]
            hi = f.astype(BF16)
            hi_ref[p, :, r * cols : (r + 1) * cols] = hi
            lo_ref[p, :, r * cols : (r + 1) * cols] = (f - hi.astype(F32)).astype(BF16)


def tile_mask(bits, tiles):
    words = bits.shape[1]
    word = tiles // 30
    place = tiles % 30
    chosen = jnp.zeros((bits.shape[0], LANES), jnp.int32)
    for w in range(words):
        chosen = jnp.where(word == w, bits[:, w : w + 1], chosen)
    return (jnp.right_shift(chosen, place) & 1).astype(F32)


def analysis_kernel(
    n_lon,
    rows,
    order_ref,
    value_ref,
    var_ref,
    pay_ref,
    tile_ref,
    bits_ref,
    hi_hbm,
    lo_hbm,
    out_hbm,
    hi_ref,
    lo_ref,
    out_ref,
    wide_ref,
    alpha_ref,
    anomaly_ref,
    in_sem,
    out_sem,
):
    planes, members, width = hi_ref.shape
    cols = width // rows
    nobs = tile_ref.shape[1]
    batches = order_ref.shape[0]
    batch = nobs // batches
    blocks = nobs // SUBLANES
    fetch_hi = pltpu.make_async_copy(hi_hbm, hi_ref, in_sem.at[0])
    fetch_lo = pltpu.make_async_copy(lo_hbm, lo_ref, in_sem.at[1])
    fetch_hi.start()
    fetch_lo.start()

    me = lax.axis_index("lat") * n_lon + lax.axis_index("lon")
    tile = in_order(tile_ref[...], order_ref)
    bits = jnp.concatenate(
        [bits_ref[pl.ds(pl.multiple_of(order_ref[i] * batch, batch), batch), :] for i in range(batches)], axis=0
    )
    mask = tile_mask(bits, tile[:1])
    mine = tile_mask(bits, jnp.full((1, LANES), me, jnp.int32))
    square = jnp.concatenate([mask, jnp.zeros((LANES - nobs, LANES), F32)], axis=0)
    turned = square.T

    half = members // 2
    own_lon = pay_ref[0:members, :]
    folded = pay_ref[members : members + half, :]
    factors = pay_ref[members + half : members + half + 1, :]
    first = iota((members, LANES), 1) < nobs
    along_lat = jnp.concatenate([folded, pltpu.roll(folded, nobs, 1)], axis=0)
    prior = own_lon + factors * pltpu.roll(own_lon, nobs, 1) + pltpu.roll(factors, nobs, 1) * along_lat
    prior = jnp.where(first, prior, 0.0)
    mean = jnp.sum(prior, axis=0, keepdims=True) * (1.0 / members)
    spread = prior - mean
    gram = lax.dot_general(spread, spread, (((0,), (0,)), ((), ())), precision=HIGHEST, preferred_element_type=F32)
    tall = jnp.concatenate([spread, jnp.zeros((LANES - members, LANES), F32)], axis=0).T

    def cut(array):
        return [array[b * SUBLANES : (b + 1) * SUBLANES] for b in range(blocks)]

    c_rows, b_rows, a_rows = cut(gram), cut(tall), cut(tall)
    masks, mines, turns = cut(mask), cut(mine), cut(turned)
    mean_own = jnp.zeros((1, LANES), F32)
    inv = 1.0 / (members - 1)
    for k in range(nobs):
        b, s = divmod(k, SUBLANES)
        at = order_ref[k // batch] * batch + k % batch
        r = jnp.full((1, 1), var_ref[at], F32)
        o = jnp.full((1, 1), value_ref[at], F32)
        g_c, g_b, g_a = (block[b][s : s + 1] for block in (c_rows, b_rows, a_rows))
        g_kk = g_c[:, k : k + 1]
        m_k = mean[:, k : k + 1]
        v = g_kk * inv + EPSILON
        u = lax.rsqrt(v + r)
        uu = u * u * inv
        c = -uu / (1.0 + jnp.sqrt(r) * u)
        gain = uu * (o - m_k)
        masked_c = masks[b][s : s + 1] * g_c
        masked_b = mines[b][s : s + 1] * g_b
        alpha_c = masked_c * c
        alpha_b = masked_b * c
        mean = mean + masked_c * gain
        mean_own = mean_own + masked_b * gain
        h_c = g_c + alpha_c * g_kk
        h_b = g_b + alpha_b * g_kk
        alpha_ref[k : k + 1, :] = alpha_b
        anomaly_ref[k : k + 1, :] = g_a
        for i in range((k + 1) // SUBLANES, blocks):
            g_i = c_rows[i][:, k : k + 1]
            alpha_i = (turns[i][:, k : k + 1] * g_i) * c
            c_rows[i] = c_rows[i] + alpha_i * h_c + g_i * alpha_c
            b_rows[i] = b_rows[i] + alpha_i * h_b + g_i * alpha_b
            a_rows[i] = a_rows[i] + alpha_i * g_a

    transform = lax.dot_general(
        anomaly_ref[...], alpha_ref[...], (((0,), (0,)), ((), ())), precision=HIGHEST, preferred_element_type=F32
    )
    transform = transform[:members] + mean_own + (iota((members, LANES), 0) == iota((members, LANES), 1)).astype(F32)
    hi = transform[:, :members].astype(BF16)
    lo = (transform[:, :members] - hi.astype(F32)).astype(BF16)

    fetch_hi.wait()
    fetch_lo.wait()
    for p in range(planes):
        result = jnp.dot(hi, hi_ref[p], preferred_element_type=F32)
        result = result + jnp.dot(lo, hi_ref[p], preferred_element_type=F32)
        result = result + jnp.dot(hi, lo_ref[p], preferred_element_type=F32)
        for q in range(rows):
            wide_ref[p % 2, pl.ds(q, members, stride=rows), :] = result[:, q * cols : (q + 1) * cols]
        out_ref[p] = wide_ref[p % 2].astype(BF16)
        pltpu.make_async_copy(out_ref.at[p], out_hbm.at[p], out_sem.at[p]).start()
    for p in range(planes):
        pltpu.make_async_copy(out_ref.at[p], out_hbm.at[p], out_sem.at[p]).wait()


def shifted(x, axis, by, closed):
    count = lax.axis_size(axis)
    pairs = [(i, (i + by) % count) for i in range(count) if closed or 0 <= i + by < count]
    return lax.ppermute(x, axis, pairs)


def summed(x, axis):
    count = lax.axis_size(axis)
    step = 1
    while step < count:
        x = x + lax.ppermute(x, axis, [(i, i ^ step) for i in range(count)])
        step *= 2
    return x


def per_device(prior_state, courant, obs_tile, obs_site, obs_value, obs_var, loc_bits, batch_order):
    fields, levels, members, rows, cols = prior_state.shape
    planes, depth = fields * levels, members * rows
    n_lat, n_lon = lax.axis_size("lat"), lax.axis_size("lon")
    nobs = obs_tile.shape[0]
    x = prior_state.reshape(planes, depth, cols)
    winds = courant.reshape(2 * levels * rows, cols)
    tile = obs_tile.reshape(1, nobs)
    site = obs_site.reshape(1, nobs)

    payload = pl.pallas_call(
        functools.partial(observe_kernel, n_lat, n_lon, levels),
        out_shape=jax.ShapeDtypeStruct((members + members // 2 + SUBLANES, LANES), F32),
        in_specs=[VMEM, VMEM, VMEM, VMEM, SMEM],
        out_specs=VMEM,
        compiler_params=PARAMS,
        name="observe",
    )(x, winds, tile, site, batch_order)

    row_type = jax.ShapeDtypeStruct((planes, members, cols), BF16)
    column_type = jax.ShapeDtypeStruct((planes, rows, LANES), F32)
    first_row, last_row, first_col, last_col = pl.pallas_call(
        functools.partial(edges_kernel, rows),
        out_shape=[row_type, row_type, column_type, column_type],
        in_specs=[VMEM],
        out_specs=[VMEM] * 4,
        scratch_shapes=[pltpu.VMEM((depth, cols), F32)],
        compiler_params=PARAMS,
        name="edges",
    )(x)
    south = shifted(last_row, "lat", 1, False)
    north = shifted(first_row, "lat", -1, False)
    west = shifted(last_col, "lon", 1, True)
    east = shifted(first_col, "lon", -1, True)

    payload = summed(payload, "lon")
    payload = summed(payload, "lat")

    split_type = jax.ShapeDtypeStruct((planes, members, rows * cols), BF16)
    hi, lo = pl.pallas_call(
        functools.partial(forecast_kernel, levels),
        out_shape=[split_type, split_type],
        in_specs=[VMEM] * 6,
        out_specs=[VMEM] * 2,
        scratch_shapes=[pltpu.VMEM((depth, cols), F32), pltpu.VMEM((2, members, cols), F32)],
        compiler_params=PARAMS,
        name="forecast",
    )(x, winds, south, north, west, east)

    out = pl.pallas_call(
        functools.partial(analysis_kernel, n_lon, rows),
        out_shape=jax.ShapeDtypeStruct((planes, depth, cols), BF16),
        in_specs=[SMEM, SMEM, SMEM, VMEM, VMEM, VMEM, HBM, HBM],
        out_specs=HBM,
        scratch_shapes=[
            pltpu.VMEM(split_type.shape, BF16),
            pltpu.VMEM(split_type.shape, BF16),
            pltpu.VMEM((planes, depth, cols), BF16),
            pltpu.VMEM((2, depth, cols), F32),
            pltpu.VMEM((nobs, LANES), F32),
            pltpu.VMEM((nobs, LANES), F32),
            pltpu.SemaphoreType.DMA((2,)),
            pltpu.SemaphoreType.DMA((planes,)),
        ],
        compiler_params=PARAMS,
        name="analysis",
    )(batch_order, obs_value, obs_var, payload, tile, loc_bits, hi, lo)
    return out.reshape(prior_state.shape)


def solution(mesh):
    placed = (P(None, None, None, "lat", "lon"), P(None, None, "lat", "lon")) + (P(),) * 6
    return jax.shard_map(
        per_device,
        mesh=mesh,
        in_specs=placed,
        out_specs=P(None, None, None, "lat", "lon"),
        check_vma=False,
    )
```

time: 805 us -> 49.5 us (0.06)
  loops' own time: 303 us -> 0 us
  blocking collectives: 154 us -> 0 us
  local copies, waits for them, and re-layouts: 156 us -> 4.17 us
  other arithmetic: 97.6 us -> 0.05 us
  matrix products: 76.6 us -> 0 us
  Pallas kernels: 0 us -> 16.4 us
  waiting for transfers between devices: 0.01 us -> 10.7 us
    another operation x4 -> x0, loops' own time: 303 us -> none  [per_device(): lax.fori_loop(0, OBSERVED_BATCH, advance, (prior_values, identity))]
    all_gather x4 -> x0, blocking collectives: 154 us -> none  [per_device(): collected = lax.all_gather(outgoing, ('lat', 'lon'), axis=0, tiled=True)]
    dynamic_slice x195 -> x0, local copies, waits for them, and re-layouts: 116 us -> none  [the longest x64 39.2 us: advance(): obs_values[obs_index]]
    reduce_sum x132 -> x0, other arithmetic: 78.2 us -> none  [the longest x64 39.3 us: eakf_step(): mean_prior = jnp.mean(prior_row)]
    dot_general x136 -> x0, matrix products: 76.6 us -> none  [the longest x64 50.7 us: advance(): turned = jnp.dot(transform_now, weights, precision=HIGHEST_PRECISE)]
    pallas_call x0 -> x4, Pallas kernels: none -> 16.4 us  [the longest x1 10.4 us: per_device(): pl.pallas_call(functools.partial(analysis_kernel, n_lon, rows), out_shape...]
    transpose x3 -> x0, local copies, waits for them, and re-layouts: 13 us -> none  [per_device(): jnp.einsum('pec,eg->pgc', current_state, transform_now, precision=HIGHEST...]
    ppermute x4 -> x9, waiting for transfers between devices: 0.01 us -> 10.7 us  [the longest x5 8.89 us: summed(): x = x + lax.ppermute(x, axis, [(i, i ^ step) for i in range(count)])]
  transfers between devices with their start and end apart: 4 -> 9, of which waited for: 0 -> 4; matrix products, arithmetic and copies ran while one was open for 1% -> 0% of each run, Pallas kernels for 0% -> 9%
where the time goes in v1:
time: 49.5 us; the launch traced here: 49.2 us
  starting transfers between devices  17.6 us (36%)
  Pallas kernels  16.4 us (33%)
  waiting for transfers between devices  10.7 us (22%)
  local copies, waits for them, and re-layouts  4.17 us (8%)
    pallas_call x1, Pallas kernels, per_device(): pl.pallas_call(functools.partial(analysis_kernel, n_lon, rows), out_shape...  10.4 us
    ppermute x5, starting transfers between devices, summed(): x = x + lax.ppermute(x, axis, [(i, i ^ step) for i in range(count)])  9.21 us
    ppermute x5, waiting for transfers between devices, summed(): x = x + lax.ppermute(x, axis, [(i, i ^ step) for i in range(count)])  8.89 us
    ppermute x4, starting transfers between devices, shifted(): return lax.ppermute(x, axis, pairs)  8.42 us
    unnamed x25, local copies, waits for them, and re-layouts  4.17 us
    pallas_call x1, Pallas kernels, per_device(): pl.pallas_call(functools.partial(forecast_kernel, levels), out_shape=[spl...  2.97 us
    ppermute x4, waiting for transfers between devices, shifted(): return lax.ppermute(x, axis, pairs)  1.8 us
    pallas_call x1, Pallas kernels, per_device(): pl.pallas_call(functools.partial(observe_kernel, n_lat, n_lon, levels), o...  1.7 us
  transfers between devices with their start and end apart: 9, of which 4 were waited for; matrix products, arithmetic and copies ran while one was open for 0% of the time, Pallas kernels for 9%

profile of v1, /device:TPU:0, one launch (start us, length us, event | category | flops | bytes accessed | tf_op | source)
XLA Modules:
  0.0 49.2 jit_solution(5943270096331202947)
XLA Ops:
  0.0 0.0 copy-start
  0.0 1.3 %copy-done = bf16[2,4,80,8,128]{4,3,2,1,0:T(8,128)(2,1)S(1)} copy-done((bf16[2,4,80,8,128]{4,3,2,1,0:T(8,128)(2,1)S(1)}, bf16[2,4,80,8,128]{4,3,2,1,0:T(8,128)(2,1)}, u32[]{:S(2)}) %copy-start) | copy-done | bytes 1310744
  1.3 0.0 copy-start.2
  1.3 0.8 %copy-done.2 = f32[2,4,8,128]{3,2,1,0:T(8,128)S(1)} copy-done((f32[2,4,8,128]{3,2,1,0:T(8,128)S(1)}, f32[2,4,8,128]{3,2,1,0:T(8,128)}, u32[]{:S(2)}) %copy-start.2) | copy-done | bytes 32792
  2.1 0.0 copy-start.4
  2.1 0.7 %copy-done.4 = s32[4]{0:T(128)S(1)} copy-done((s32[4]{0:T(128)S(1)}, s32[4]{0:T(128)}, u32[]{:S(2)}) %copy-start.4) | copy-done | bytes 40
  2.7 0.0 copy-start.6
  2.7 0.7 %copy-done.6 = s32[64]{0:T(128)S(1)} copy-done((s32[64]{0:T(128)S(1)}, s32[64]{0:T(128)}, u32[]{:S(2)}) %copy-start.6) | copy-done | bytes 280
  3.4 0.0 copy-start.8
  3.4 0.7 %copy-done.8 = s32[64]{0:T(128)S(1)} copy-done((s32[64]{0:T(128)S(1)}, s32[64]{0:T(128)}, u32[]{:S(2)}) %copy-start.8) | copy-done | bytes 280
  4.0 1.7 %observe.1 = f32[128,128]{1,0:T(8,128)S(1)} custom-call(bf16[8,640,128]{2,1,0:T(8,128)(2,1)S(1)} %bitcast.5, f32[64,128]{1,0:T(8,128)S(1)} %bitcast.8, s32[1,64]{1,0:T(1,128)S(1)} %bitcast.10, s32[1,64]{1,0:T(1,128)S(1)} %bitcast.12, s32[4]{0:T(128)S(1)} %copy-done.4), custom_call_target="tpu_custom_call" | custom-call | tf_op jit(solution)/shard_map/observe/pallas_call | solution.py:323
  5.7 0.0 copy-start.11
  5.7 0.0 copy-start.1
  5.8 0.0 copy-start.3
  5.8 0.5 %collective-permute-start = (f32[128,128]{1,0:T(8,128)S(1)}, f32[128,128]{1,0:T(8,128)S(1)}, u32[]{:S(2)}, u32[]{:S(2)}) collective-permute-start(f32[128,128]{1,0:T(8,128)S(1)} %observe.1), channel_id=1, source_target_pairs={{0,1},{1,0},{2,3},{3,2},{4,5},{5,4},{6,7},{7,6},{8,9},{9,8},{10,11... | collective-permute-start | bytes 196616 | tf_op jit(solution)/shard_map/ppermute | solution.py:308
  6.3 0.9 %collective-permute-done = f32[128,128]{1,0:T(8,128)S(1)} collective-permute-done((f32[128,128]{1,0:T(8,128)S(1)}, f32[128,128]{1,0:T(8,128)S(1)}, u32[]{:S(2)}, u32[]{:S(2)}) %collective-permute-start) | collective-permute-done | bytes 65568 | tf_op jit(solution)/shard_map/ppermute | solution.py:308
  7.2 3.0 %collective-permute-start.1 = (f32[128,128]{1,0:T(8,128)S(1)}, f32[128,128]{1,0:T(8,128)S(1)}, u32[]{:S(2)}, u32[]{:S(2)}) collective-permute-start(f32[128,128]{1,0:T(8,128)S(1)} %add.15), channel_id=1, source_target_pairs={{0,2},{1,3},{2,0},{3,1},{4,6},{5,7},{6,4},{7,5},{8,10},{9,11},{10,... | collective-permute-start | bytes 196616 | tf_op jit(solution)/shard_map/ppermute | solution.py:308
  10.2 2.4 %collective-permute-done.1 = f32[128,128]{1,0:T(8,128)S(1)} collective-permute-done((f32[128,128]{1,0:T(8,128)S(1)}, f32[128,128]{1,0:T(8,128)S(1)}, u32[]{:S(2)}, u32[]{:S(2)}) %collective-permute-start.1) | collective-permute-done | bytes 65568 | tf_op jit(solution)/shard_map/ppermute | solution.py:308
  12.6 2.9 %collective-permute-start.2 = (f32[128,128]{1,0:T(8,128)S(1)}, f32[128,128]{1,0:T(8,128)S(1)}, u32[]{:S(2)}, u32[]{:S(2)}) collective-permute-start(f32[128,128]{1,0:T(8,128)S(1)} %add.16), channel_id=1, source_target_pairs={{0,4},{1,5},{2,6},{3,7},{4,0},{5,1},{6,2},{7,3},{8,12},{9,13},{10,... | collective-permute-start | bytes 196616 | tf_op jit(solution)/shard_map/ppermute | solution.py:308
  15.5 1.4 %edges.1 = (bf16[8,80,128]{2,1,0:T(8,128)(2,1)S(1)}, bf16[8,80,128]{2,1,0:T(8,128)(2,1)S(1)}, f32[8,8,128]{2,1,0:T(8,128)S(1)}, f32[8,8,128]{2,1,0:T(8,128)S(1)}) custom-call(bf16[8,640,128]{2,1,0:T(8,128)(2,1)S(1)} %bitcast.6), custom_call_target="tpu_custom_call" | custom-call | tf_op jit(solution)/shard_map/edges/pallas_call | solution.py:334
  16.9 0.0 copy-start.5
  16.9 0.0 copy-start.7
  16.9 0.0 copy-start.9
  16.9 0.0 copy-start.10
  17.0 3.5 %collective-permute-start.5 = (bf16[8,80,128]{2,1,0:T(8,128)(2,1)S(1)}, bf16[8,80,128]{2,1,0:T(8,128)(2,1)S(1)}, u32[]{:S(2)}, u32[]{:S(2)}) collective-permute-start(bf16[8,80,128]{2,1,0:T(8,128)(2,1)S(1)} %get-tuple-element.11), channel_id=1, source_target_pairs={{0,8},{8,16},{16,24},{1,9},{9,17},{17,25},{2,10},{10,18},{18,26},{... | collective-permute-start | bytes 491528 | tf_op jit(solution)/shard_map/ppermute | solution.py:301
  20.5 1.3 %collective-permute-start.6 = (bf16[8,80,128]{2,1,0:T(8,128)(2,1)S(1)}, bf16[8,80,128]{2,1,0:T(8,128)(2,1)S(1)}, u32[]{:S(2)}, u32[]{:S(2)}) collective-permute-start(bf16[8,80,128]{2,1,0:T(8,128)(2,1)S(1)} %get-tuple-element.12), channel_id=1, source_target_pairs={{8,0},{16,8},{24,16},{9,1},{17,9},{25,17},{10,2},{18,10},{26,18},{... | collective-permute-start | bytes 491528 | tf_op jit(solution)/shard_map/ppermute | solution.py:301
  21.8 0.0 collective-permute-done.2
  21.8 2.7 %collective-permute-start.3 = (f32[128,128]{1,0:T(8,128)S(1)}, f32[128,128]{1,0:T(8,128)S(1)}, u32[]{:S(2)}, u32[]{:S(2)}) collective-permute-start(f32[128,128]{1,0:T(8,128)S(1)} %add.17), channel_id=1, source_target_pairs={{0,8},{8,0},{16,24},{24,16},{1,9},{9,1},{17,25},{25,17},{2,10},{10... | collective-permute-start | bytes 196616 | tf_op jit(solution)/shard_map/ppermute | solution.py:308
  24.5 5.6 %collective-permute-done.3 = f32[128,128]{1,0:T(8,128)S(1)} collective-permute-done((f32[128,128]{1,0:T(8,128)S(1)}, f32[128,128]{1,0:T(8,128)S(1)}, u32[]{:S(2)}, u32[]{:S(2)}) %collective-permute-start.3) | collective-permute-done | bytes 65568 | tf_op jit(solution)/shard_map/ppermute | solution.py:308
  30.1 0.1 collective-permute-start.4
  30.2 0.1 collective-permute-start.7
  30.3 3.5 %collective-permute-start.8 = (f32[8,8,128]{2,1,0:T(8,128)S(1)}, f32[8,8,128]{2,1,0:T(8,128)S(1)}, u32[]{:S(2)}, u32[]{:S(2)}) collective-permute-start(f32[8,8,128]{2,1,0:T(8,128)S(1)} %get-tuple-element.14), channel_id=1, source_target_pairs={{0,7},{1,0},{2,1},{3,2},{4,3},{5,4},{6,5},{7,6},{8,15},{9,8},{10,9... | collective-permute-start | bytes 98312 | tf_op jit(solution)/shard_map/ppermute | solution.py:301
  33.8 0.0 copy-done.11
  33.8 0.1 copy.9.bits_ref
  33.9 1.8 %collective-permute-done.7.west_ref = f32[8,8,128]{2,1,0:T(8,128)S(1)} collective-permute-done((f32[8,8,128]{2,1,0:T(8,128)S(1)}, f32[8,8,128]{2,1,0:T(8,128)S(1)}, u32[]{:S(2)}, u32[]{:S(2)}) %collective-permute-start.7) | collective-permute-done | bytes 32800 | tf_op jit(solution)/shard_map/ppermute | solution.py:301
  35.7 0.0 collective-permute-done.8.east_ref
  35.7 0.0 collective-permute-done.5.south_ref
  35.7 0.0 collective-permute-done.6.north_ref
  35.7 0.0 copy-done.1
  35.7 0.0 copy-done.3
  35.7 3.0 %forecast.1 = (bf16[8,80,1024]{2,1,0:T(8,128)(2,1)S(1)}, bf16[8,80,1024]{2,1,0:T(8,128)(2,1)S(1)}) custom-call(bf16[8,640,128]{2,1,0:T(8,128)(2,1)S(1)} %bitcast.7, f32[64,128]{1,0:T(8,128)S(1)} %bitcast.9, bf16[8,80,128]{2,1,0:T(8,128)(2,1)S(1)} %collective-permute-done.5.south_ref, bf16[8,80,128]{2,1,0:T(8,128)(2,1)S(1)} %collective-permute-done.6.north_ref, ...), custom_call_target="tpu_custom_call" | custom-call | tf_op jit(solution)/shard_map/forecast/pallas_call | solution.py:352
  38.7 0.0 collective-permute-done.4
  38.7 0.0 copy-done.5
  38.7 0.0 copy-done.7
  38.7 0.0 copy-done.9
  38.8 0.0 copy-done.10
  38.8 10.4 %analysis.1 = bf16[8,640,128]{2,1,0:T(8,128)(2,1)} custom-call(s32[4]{0:T(128)S(1)} %copy-done.5, f32[64]{0:T(128)S(1)} %copy-done.9, f32[64]{0:T(128)S(1)} %copy-done.10, f32[128,128]{1,0:T(8,128)S(1)} %add.19.pay_ref, s32[1,64]{1,0:T(1,128)S(1)} %bitcast.11, s32[64,2]{1,0:T(8,128)S(1)} %copy.9.bits_ref, bf16[8,80,1024]{2,1,0:T(8,128)(2,1)S(1)} %get-tuple-element.15.hi_hbm, ...), custom_call_target="tpu_custom_call" | custom-call | tf_op jit(solution)/shard_map/analysis/pallas_call | solution.py:362
  (5 shorter events, 0.0 us)
Async XLA Ops:
  0.0 1.3 %copy-start = (bf16[2,4,80,8,128]{4,3,2,1,0:T(8,128)(2,1)S(1)}, bf16[2,4,80,8,128]{4,3,2,1,0:T(8,128)(2,1)}, u32[]{:S(2)}) copy-start(bf16[2,4,80,8,128]{4,3,2,1,0:T(8,128)(2,1)} %param.8) | copy-start | bytes 3932164
  1.3 0.8 %copy-start.2 = (f32[2,4,8,128]{3,2,1,0:T(8,128)S(1)}, f32[2,4,8,128]{3,2,1,0:T(8,128)}, u32[]{:S(2)}) copy-start(f32[2,4,8,128]{3,2,1,0:T(8,128)} %param.9) | copy-start | bytes 98308
  2.1 0.7 %copy-start.4 = (s32[4]{0:T(128)S(1)}, s32[4]{0:T(128)}, u32[]{:S(2)}) copy-start(s32[4]{0:T(128)} %order_ref.3) | copy-start | bytes 52
  2.7 0.7 %copy-start.6 = (s32[64]{0:T(128)S(1)}, s32[64]{0:T(128)}, u32[]{:S(2)}) copy-start(s32[64]{0:T(128)} %param.10) | copy-start | bytes 772
  3.4 0.7 %copy-start.8 = (s32[64]{0:T(128)S(1)}, s32[64]{0:T(128)}, u32[]{:S(2)}) copy-start(s32[64]{0:T(128)} %param.11) | copy-start | bytes 772
  5.7 28.1 %copy-start.11 = (s32[64,2]{0,1:T(2,128)S(1)}, s32[64,2]{0,1:T(2,128)}, u32[]{:S(2)}) copy-start(s32[64,2]{0,1:T(2,128)} %param.14) | copy-start | bytes 1540
  5.7 30.0 %copy-start.1 = (bf16[2,4,80,8,128]{4,3,2,1,0:T(8,128)(2,1)S(1)}, bf16[2,4,80,8,128]{4,3,2,1,0:T(8,128)(2,1)}, u32[]{:S(2)}) copy-start(bf16[2,4,80,8,128]{4,3,2,1,0:T(8,128)(2,1)} %param.8) | copy-start | bytes 3932164
  5.8 30.0 %copy-start.3 = (f32[2,4,8,128]{3,2,1,0:T(8,128)S(1)}, f32[2,4,8,128]{3,2,1,0:T(8,128)}, u32[]{:S(2)}) copy-start(f32[2,4,8,128]{3,2,1,0:T(8,128)} %param.9) | copy-start | bytes 98308
  5.8 1.4 %collective-permute-start = (f32[128,128]{1,0:T(8,128)S(1)}, f32[128,128]{1,0:T(8,128)S(1)}, u32[]{:S(2)}, u32[]{:S(2)}) collective-permute-start(f32[128,128]{1,0:T(8,128)S(1)} %observe.1), channel_id=1, source_target_pairs={{0,1},{1,0},{2,3},{3,2},{4,5},{5,4},{6,7},{7,6},{8,9},{9,8},{10,11... | collective-permute-start | bytes 196616 | tf_op jit(solution)/shard_map/ppermute | solution.py:308
  7.2 5.4 %collective-permute-start.1 = (f32[128,128]{1,0:T(8,128)S(1)}, f32[128,128]{1,0:T(8,128)S(1)}, u32[]{:S(2)}, u32[]{:S(2)}) collective-permute-start(f32[128,128]{1,0:T(8,128)S(1)} %add.15), channel_id=1, source_target_pairs={{0,2},{1,3},{2,0},{3,1},{4,6},{5,7},{6,4},{7,5},{8,10},{9,11},{10,... | collective-permute-start | bytes 196616 | tf_op jit(solution)/shard_map/ppermute | solution.py:308
  12.6 9.2 %collective-permute-start.2 = (f32[128,128]{1,0:T(8,128)S(1)}, f32[128,128]{1,0:T(8,128)S(1)}, u32[]{:S(2)}, u32[]{:S(2)}) collective-permute-start(f32[128,128]{1,0:T(8,128)S(1)} %add.16), channel_id=1, source_target_pairs={{0,4},{1,5},{2,6},{3,7},{4,0},{5,1},{6,2},{7,3},{8,12},{9,13},{10,... | collective-permute-start | bytes 196616 | tf_op jit(solution)/shard_map/ppermute | solution.py:308
  16.9 21.8 %copy-start.5 = (s32[4]{0:T(128)S(1)}, s32[4]{0:T(128)}, u32[]{:S(2)}) copy-start(s32[4]{0:T(128)} %order_ref.3) | copy-start | bytes 52
  16.9 21.8 %copy-start.7 = (s32[64]{0:T(128)S(1)}, s32[64]{0:T(128)}, u32[]{:S(2)}) copy-start(s32[64]{0:T(128)} %param.10) | copy-start | bytes 772
  16.9 21.8 %copy-start.9 = (f32[64]{0:T(128)S(1)}, f32[64]{0:T(128)}, u32[]{:S(2)}) copy-start(f32[64]{0:T(128)} %value_ref.1) | copy-start | bytes 772
  16.9 21.8 %copy-start.10 = (f32[64]{0:T(128)S(1)}, f32[64]{0:T(128)}, u32[]{:S(2)}) copy-start(f32[64]{0:T(128)} %var_ref.1) | copy-start | bytes 772
  17.0 18.7 %collective-permute-start.5 = (bf16[8,80,128]{2,1,0:T(8,128)(2,1)S(1)}, bf16[8,80,128]{2,1,0:T(8,128)(2,1)S(1)}, u32[]{:S(2)}, u32[]{:S(2)}) collective-permute-start(bf16[8,80,128]{2,1,0:T(8,128)(2,1)S(1)} %get-tuple-element.11), channel_id=1, source_target_pairs={{0,8},{8,16},{16,24},{1,9},{9,17},{17,25},{2,10},{10,18},{18,26},{... | collective-permute-start | bytes 491528 | tf_op jit(solution)/shard_map/ppermute | solution.py:301
  20.5 15.2 %collective-permute-start.6 = (bf16[8,80,128]{2,1,0:T(8,128)(2,1)S(1)}, bf16[8,80,128]{2,1,0:T(8,128)(2,1)S(1)}, u32[]{:S(2)}, u32[]{:S(2)}) collective-permute-start(bf16[8,80,128]{2,1,0:T(8,128)(2,1)S(1)} %get-tuple-element.12), channel_id=1, source_target_pairs={{8,0},{16,8},{24,16},{9,1},{17,9},{25,17},{10,2},{18,10},{26,18},{... | collective-permute-start | bytes 491528 | tf_op jit(solution)/shard_map/ppermute | solution.py:301
  21.8 8.3 %collective-permute-start.3 = (f32[128,128]{1,0:T(8,128)S(1)}, f32[128,128]{1,0:T(8,128)S(1)}, u32[]{:S(2)}, u32[]{:S(2)}) collective-permute-start(f32[128,128]{1,0:T(8,128)S(1)} %add.17), channel_id=1, source_target_pairs={{0,8},{8,0},{16,24},{24,16},{1,9},{9,1},{17,25},{25,17},{2,10},{10... | collective-permute-start | bytes 196616 | tf_op jit(solution)/shard_map/ppermute | solution.py:308
  30.1 8.6 %collective-permute-start.4 = (f32[128,128]{1,0:T(8,128)S(1)}, f32[128,128]{1,0:T(8,128)S(1)}, u32[]{:S(2)}, u32[]{:S(2)}) collective-permute-start(f32[128,128]{1,0:T(8,128)S(1)} %add.18), channel_id=1, source_target_pairs={{0,16},{8,24},{16,0},{24,8},{1,17},{9,25},{17,1},{25,9},{2,18},{10... | collective-permute-start | bytes 196616 | tf_op jit(solution)/shard_map/ppermute | solution.py:308
  30.2 5.5 %collective-permute-start.7 = (f32[8,8,128]{2,1,0:T(8,128)S(1)}, f32[8,8,128]{2,1,0:T(8,128)S(1)}, u32[]{:S(2)}, u32[]{:S(2)}) collective-permute-start(f32[8,8,128]{2,1,0:T(8,128)S(1)} %get-tuple-element.13), channel_id=1, source_target_pairs={{0,1},{1,2},{2,3},{3,4},{4,5},{5,6},{6,7},{7,0},{8,9},{9,10},{10,1... | collective-permute-start | bytes 98312 | tf_op jit(solution)/shard_map/ppermute | solution.py:301
  30.3 5.4 %collective-permute-start.8 = (f32[8,8,128]{2,1,0:T(8,128)S(1)}, f32[8,8,128]{2,1,0:T(8,128)S(1)}, u32[]{:S(2)}, u32[]{:S(2)}) collective-permute-start(f32[8,8,128]{2,1,0:T(8,128)S(1)} %get-tuple-element.14), channel_id=1, source_target_pairs={{0,7},{1,0},{2,1},{3,2},{4,3},{5,4},{6,5},{7,6},{8,15},{9,8},{10,9... | collective-permute-start | bytes 98312 | tf_op jit(solution)/shard_map/ppermute | solution.py:301

commit v2 on v1

v2 whole, which is shorter than its diff:
```python
import functools

import jax
import jax.numpy as jnp
from jax import lax
from jax.experimental import pallas as pl
from jax.experimental.pallas import tpu as pltpu
from jax.sharding import PartitionSpec as P

EPSILON = 1e-05
HIGHEST = lax.Precision.HIGHEST
LANES = 128
PLAN = {"columns": 0, "pair": 2, "odd": 2, "inner": {1: [(0, 5)], 2: [(5, 8)]}, "settle": {0: ["column"], 2: ["pair_rows", "odd_rows"], 4:["pair"]}}
SUBLANES = 8
F32 = jnp.float32
BF16 = jnp.bfloat16
VMEM = pl.BlockSpec(memory_space=pltpu.VMEM)
SMEM = pl.BlockSpec(memory_space=pltpu.SMEM)
HBM = pl.BlockSpec(memory_space=pltpu.HBM)
SMALL = pl.CostEstimate(flops=0, bytes_accessed=0, transcendentals=0)
PARAMS = pltpu.CompilerParams(vmem_limit_bytes=16 * 1024 * 1024)


def iota(shape, dim):
    return lax.broadcasted_iota(jnp.int32, shape, dim)


def in_order(row, order_ref):
    nobs = row.shape[1]
    batches = order_ref.shape[0]
    batch = nobs // batches
    wide = jnp.concatenate([row, jnp.zeros((1, LANES - nobs), row.dtype)], axis=1)
    wide = jnp.broadcast_to(wide, (SUBLANES, LANES))
    lane = iota((SUBLANES, LANES), 1)
    result = jnp.zeros_like(wide)
    for i in range(batches):
        moved = pltpu.roll(wide, lax.rem(i * batch - order_ref[i] * batch + LANES, LANES), 1)
        result = jnp.where(lane // batch == i, moved, result)
    return result


def observe_kernel(
    n_lon, levels, x_hbm, courant_hbm, tile_hbm, site_hbm, order_hbm, pay_ref, x_ref, courant_ref, tile_ref, site_ref, order_ref, x_sem, sem
):
    planes, depth, cols = x_ref.shape
    small = [
        pltpu.make_async_copy(source, target, sem.at[i])
        for i, (source, target) in enumerate(
            ((order_hbm, order_ref), (tile_hbm, tile_ref), (site_hbm, site_ref), (courant_hbm, courant_ref))
        )
    ]
    for copy in small:
        copy.start()
    pieces = x_sem.shape[0]
    piece = depth // pieces
    large = [
        pltpu.make_async_copy(
            x_hbm.at[:, i * piece : (i + 1) * piece, :], x_ref.at[:, i * piece : (i + 1) * piece, :], x_sem.at[i]
        )
        for i in range(pieces)
    ]
    for copy in large:
        copy.start()
    for copy in small:
        copy.wait()
    rows = courant_ref.shape[0] // (2 * levels)
    members = depth // rows
    nobs = tile_ref.shape[1]
    cells = rows * cols
    my_lat, my_lon = lax.axis_index("lat"), lax.axis_index("lon")
    me = my_lat * n_lon + my_lon

    tile = in_order(tile_ref[...], order_ref)
    site = in_order(site_ref[...], order_ref)
    tile = tile + pltpu.roll(tile, nobs, 1)
    site = site + pltpu.roll(site, nobs, 1)
    shape = (SUBLANES, LANES)
    lane = iota(shape, 1)
    sub = iota(shape, 0)
    first = lane < nobs
    plane = site // cells
    row = (site // cols) % rows
    col = site % cols
    level = plane % levels
    lat, lon = tile // n_lon, tile % n_lon
    owner = tile == me
    from_west = (lat == my_lat) & ((lon + n_lon - 1) % n_lon == my_lon) & (col == 0)
    from_east = (lat == my_lat) & ((lon + 1) % n_lon == my_lon) & (col == cols - 1)
    from_south = (lat - 1 == my_lat) & (lon == my_lon) & (row == 0)
    from_north = (lat + 1 == my_lat) & (lon == my_lon) & (row == rows - 1)
    beside = from_west | from_east
    above = from_south | from_north
    far_col = jnp.where(from_west, cols - 1, jnp.where(from_east, 0, jnp.where(above, col, -1)))
    far_row = jnp.where(from_south, rows - 1, jnp.where(from_north, 0, row))

    down = iota((cols, LANES), 0)
    picked = jnp.dot(
        courant_ref[...], (down == col[:1]).astype(F32), precision=HIGHEST, preferred_element_type=F32
    )
    which = iota((2 * levels * rows, LANES), 0)
    at_cell = (level * rows + row)[:1]
    cu = jnp.sum(jnp.where(which == at_cell, picked, 0.0), axis=0, keepdims=True)
    cv = jnp.sum(jnp.where(which == at_cell + levels * rows, picked, 0.0), axis=0, keepdims=True)
    west, east = jnp.maximum(cu, 0.0), -jnp.minimum(cu, 0.0)
    south, north = jnp.maximum(cv, 0.0), -jnp.minimum(cv, 0.0)
    centre = 1.0 - west - east - south - north

    zero = jnp.zeros(shape, F32)
    own_rows = jnp.where(sub == row, centre, zero)
    own_rows = jnp.where(sub == row - 1, south, own_rows)
    own_rows = jnp.where(sub == row + 1, north, own_rows)
    half0 = jnp.where(first, own_rows, jnp.where(sub == row, west, zero))
    half0 = jnp.where(owner, half0, zero)
    half1 = jnp.where(first, jnp.where(owner & (sub == row), east, zero), ((beside | above) & (sub == far_row)).astype(F32))
    col0 = jnp.where(first, col, jnp.where(col > 0, col - 1, -1))
    col1 = jnp.where(first, jnp.where(col < cols - 1, col + 1, -1), far_col)
    at = jnp.concatenate([jnp.where(c < 0, -1, plane * cols + c)[:1] for c in (col0, col1)], axis=1)
    picks = (iota((planes * cols, 2 * LANES), 0) == at).astype(F32).astype(BF16)
    weights = jnp.concatenate([half0, half1], axis=1)
    for copy in large:
        copy.wait()
    block = jnp.concatenate([x_ref[p] for p in range(planes)], axis=1)
    values = jnp.dot(block, picks, preferred_element_type=F32).reshape(members, rows, 2 * LANES)
    both = jnp.sum(values * weights[None], axis=1)
    low, high = both[:, :LANES], both[:, LANES:]
    lane_m = iota((members, LANES), 1)
    own = jnp.where(lane_m < nobs, low + pltpu.roll(low, nobs, 1) + high, 0.0)
    far = jnp.where(lane_m < nobs, 0.0, high)
    put_split(pay_ref, 0, own, nobs)
    along_lon = pltpu.roll(jnp.where(beside[:1], far, 0.0), nobs, 1)
    pay_ref[members : 2 * members, :] = (along_lon + jnp.where(above[:1], far, 0.0)).astype(BF16)
    factor_lon = jnp.where(col == 0, west, jnp.where(col == cols - 1, east, zero))
    factor_lat = jnp.where(row == 0, south, jnp.where(row == rows - 1, north, zero))
    factors = jnp.where(owner, jnp.where(first, factor_lon, factor_lat), zero)
    coarse = factors.astype(BF16)
    fine = (factors - coarse.astype(F32)).astype(BF16)
    pay_ref[2 * members :, :] = jnp.concatenate([coarse, fine], axis=0)


def put_split(ref, start, values, nobs):
    coarse = values.astype(BF16)
    fine = (values - coarse.astype(F32)).astype(BF16)
    both = coarse.astype(F32) + pltpu.roll(fine.astype(F32), nobs, 1)
    ref[start : start + values.shape[0], :] = both.astype(BF16)


def edge_rows_kernel(rows, facing, x_ref, row_ref, wide_ref):
    planes, depth, cols = x_ref.shape
    members = depth // rows
    upper = lax.rem(lax.axis_index("lat"), 2) == (0 if facing else 1)
    row = jnp.where(upper, rows - 1, 0)
    for p in range(planes):
        wide_ref[p] = x_ref[p].astype(F32)
        row_ref[p] = wide_ref[p, pl.ds(row, members, stride=rows), :].astype(BF16)


def edge_columns_kernel(rows, x_ref, column_ref, wide_ref):
    planes, depth, cols = x_ref.shape
    members = depth // rows
    lane = iota((members, LANES), 1)
    total = jnp.zeros((members, LANES), F32)
    for p in range(planes):
        wide_ref[p] = x_ref[p].astype(F32)
        for r in range(rows):
            n = p * rows + r
            cell = wide_ref[p, pl.ds(r, members, stride=rows), :]
            total = jnp.where(lane // 2 == n, pltpu.roll(cell, 2 * n + 1, 1) if 2 * n + 1 < LANES else cell, total)
    total = jnp.where(lane % 2 == 0, pltpu.roll(total, LANES - 1, 1), pltpu.roll(total, 1, 1))
    column_ref[...] = total.astype(BF16)


def winds_of(courant_ref, levels, p):
    rows = courant_ref.shape[0] // (2 * levels)
    level = p % levels
    cu = courant_ref[level * rows : (level + 1) * rows, :]
    cv = courant_ref[(levels + level) * rows : (levels + level + 1) * rows, :]
    return jnp.maximum(cu, 0.0), -jnp.minimum(cu, 0.0), jnp.maximum(cv, 0.0), -jnp.minimum(cv, 0.0)


def inner_kernel(levels, start, x_ref, courant_ref, inner_ref, wide_ref, factor_ref):
    planes, rows, members, cols = inner_ref.shape
    lane = iota((rows, cols), 1)
    for i in range(planes):
        p = start + i
        wide_ref[i] = x_ref[p].astype(F32)
        west, east, south, north = winds_of(courant_ref, levels, p)
        factor_ref[i, 0] = 1.0 - west - east - south - north
        factor_ref[i, 1] = jnp.where(lane == 0, 0.0, west)
        factor_ref[i, 2] = jnp.where(lane == cols - 1, 0.0, east)
        factor_ref[i, 3] = south
        factor_ref[i, 4] = north
        for m in range(0, members, SUBLANES):
            cells = [wide_ref[i, pl.ds(m * rows + r, SUBLANES, stride=rows), :] for r in range(rows)]
            for r in range(rows):
                x = cells[r]
                value = factor_ref[i, 0, r : r + 1, :] * x
                value = value + factor_ref[i, 1, r : r + 1, :] * pltpu.roll(x, 1, 1)
                value = value + factor_ref[i, 2, r : r + 1, :] * pltpu.roll(x, cols - 1, 1)
                if r > 0:
                    value = value + factor_ref[i, 3, r : r + 1, :] * cells[r - 1]
                if r < rows - 1:
                    value = value + factor_ref[i, 4, r : r + 1, :] * cells[r + 1]
                inner_ref[i, r, m : m + SUBLANES, :] = value


def tile_mask(bits, tiles):
    words = bits.shape[1]
    word = tiles // 30
    place = tiles % 30
    chosen = jnp.zeros((bits.shape[0], LANES), jnp.int32)
    for w in range(words):
        chosen = jnp.where(word == w, bits[:, w : w + 1], chosen)
    return (jnp.right_shift(chosen, place) & 1).astype(F32)


def half_kernel(full_ref, other_ref, half_ref):
    size = half_ref.shape[0]
    upper = lax.rem(lax.axis_index("lon"), 2) == 1
    total = full_ref[...].astype(F32) + other_ref[...].astype(F32)
    half_ref[...] = jnp.where(upper, total[total.shape[0] - size :], total[:size]).astype(BF16)


def join_kernel(n_lon, stages, *refs):
    own_ref, other_ref, column_ref = refs[:3]
    column_refs, out_ref = refs[3 : 3 + stages], refs[-1]
    size, block = own_ref.shape[0], column_ref.shape[0]
    other_lon = lax.bitwise_xor(lax.axis_index("lon"), 1)
    odd = jnp.where(lax.rem(other_lon, 2) == 0, lax.rem(other_lon + n_lon - 1, n_lon), other_lon)
    far = column_refs[0][...].astype(F32)
    for i in range(1, stages):
        low = (2 << i) - 1
        far = jnp.where(jnp.bitwise_and(odd, low) == low, column_refs[i][...].astype(F32), far)
    out_ref[:size, :] = (own_ref[...].astype(F32) + other_ref[:size, :].astype(F32)).astype(BF16)
    out_ref[size : size + block, :] = column_ref[...]
    out_ref[size + block :, :] = far.astype(BF16)


def split_store(f, hi_ref, lo_ref, p, start):
    cols = f.shape[1]
    hi = f.astype(BF16)
    hi_ref[p, :, start : start + cols] = hi
    lo_ref[p, :, start : start + cols] = (f - hi.astype(F32)).astype(BF16)


def edge_factor(courant_ref, levels, p, r):
    rows, cols = courant_ref.shape[0] // (2 * levels), courant_ref.shape[1]
    west, east, _, _ = winds_of(courant_ref, levels, p)
    lane = iota((rows, cols), 1)
    return jnp.where(lane == 0, west, jnp.where(lane == cols - 1, east, 0.0))[r : r + 1]


def filter_kernel(n_lon, levels, parts, *refs):
    order_ref, value_ref, var_ref, mine_half_ref, join_ref, tile_ref, bits_ref, courant_ref = refs[:8]
    inner_refs, refs = refs[8 : 8 + len(parts)], refs[8 + len(parts) :]
    transform_ref, halo_ref, hi_ref, lo_ref, alpha_ref, anomaly_ref, mask_ref, mine_ref, row_ref = refs
    planes, members, width = hi_ref.shape
    rows = courant_ref.shape[0] // (2 * levels)
    cols = width // (rows - 2)
    nobs = tile_ref.shape[1]
    batches = order_ref.shape[0]
    batch = nobs // batches
    blocks = nobs // SUBLANES
    size = mine_half_ref.shape[0]

    my_lat, my_lon = lax.axis_index("lat"), lax.axis_index("lon")
    lon_even = lax.rem(my_lon, 2) == 0
    near = join_ref[size : size + members, :].astype(F32)
    far = join_ref[size + members :, :].astype(F32)
    halo_ref[...] = jnp.where((iota((members, LANES), 1) % 2 == 0) == lon_even, near, far)

    def complete(p, r):
        first, inner = next((a, ref) for (a, z), ref in zip(parts, inner_refs, strict=True) if a <= p < z)
        n = p * rows + r
        f = inner[p - first, r] + edge_factor(courant_ref, levels, p, r) * pltpu.roll(halo_ref[...], LANES - 1 - 2 * n, 1)
        split_store(f, hi_ref, lo_ref, p, (r - 1) * cols)

    todo = [(p, r) for p in range(planes) for r in range(1, rows - 1)]
    each = -(-len(todo) // nobs)

    me = my_lat * n_lon + my_lon
    tile = in_order(tile_ref[...], order_ref)
    bits = jnp.concatenate(
        [bits_ref[pl.ds(pl.multiple_of(order_ref[i] * batch, batch), batch), :] for i in range(batches)], axis=0
    )
    mask = tile_mask(bits, tile[:1])
    mine = tile_mask(bits, jnp.full((1, LANES), me, jnp.int32))
    mask_ref[...] = mask
    mine_ref[...] = mine
    square = jnp.concatenate([mask, jnp.zeros((LANES - nobs, LANES), F32)], axis=0)
    turned = square.T

    mine_half, other_half = mine_half_ref[...].astype(F32), join_ref[:size, :].astype(F32)
    lower = jnp.where(lon_even, mine_half, other_half)
    upper = jnp.where(lon_even, other_half, mine_half)
    payload = jnp.concatenate([lower, upper[2 * size - 2 * members - 2 * SUBLANES :]], axis=0)
    own = payload[:members]
    far = payload[members : 2 * members]
    factors = payload[2 * members :]
    both = own + far * (factors[:1] + factors[SUBLANES : SUBLANES + 1])
    prior = jnp.where(iota((members, LANES), 1) < nobs, both + pltpu.roll(both, nobs, 1), 0.0)
    mean = jnp.sum(prior, axis=0, keepdims=True) * (1.0 / members)
    spread = prior - mean
    gram = lax.dot_general(spread, spread, (((0,), (0,)), ((), ())), precision=HIGHEST, preferred_element_type=F32)
    tall = jnp.concatenate([spread, jnp.zeros((LANES - members, LANES), F32)], axis=0).T

    def cut(array):
        return [array[b * SUBLANES : (b + 1) * SUBLANES] for b in range(blocks)]

    c_rows, b_rows, a_rows = cut(gram), cut(tall), cut(tall)
    turns = cut(turned)
    mean = jnp.broadcast_to(mean, (SUBLANES, LANES))
    mean_own = jnp.zeros((1, LANES), F32)
    inv = 1.0 / (members - 1)

    def whole(array, s):
        return jnp.broadcast_to(array[s : s + 1], (SUBLANES, LANES))

    def lanes(array, k):
        return jnp.broadcast_to(array[:, k : k + 1], (SUBLANES, LANES))

    for b in range(blocks):
        base = b * SUBLANES
        at = order_ref[base // batch] * batch + base % batch
        columns = [lanes(c_rows[b], base + j) for j in range(SUBLANES)]
        allowed = [lanes(turns[b], base + j) for j in range(SUBLANES)]
        entry = {(i, j): whole(columns[j], i) for j in range(SUBLANES) for i in range(j, SUBLANES)}
        allow = {(j, q): whole(allowed[q], j) for q in range(SUBLANES) for j in range(q + 1, SUBLANES)}
        means = [lanes(mean, base + j) for j in range(SUBLANES)]
        scale, alphas, afters = [], {}, {}
        for q in range(SUBLANES):
            k = base + q
            for _ in range(each):
                if todo:
                    complete(*todo.pop(0))
            r = jnp.full((SUBLANES, LANES), var_ref[at + q], F32)
            o = jnp.full((SUBLANES, LANES), value_ref[at + q], F32)
            g = entry[q, q]
            u = lax.rsqrt(g * inv + EPSILON + r)
            uu = u * u * inv
            c = -uu / (1.0 + jnp.sqrt(r) * u)
            gain = uu * (o - means[q])
            scale.append(c)
            for j in range(q + 1, SUBLANES):
                masked = allow[j, q] * entry[j, q]
                alphas[j, q] = masked * c
                afters[j, q] = entry[j, q] + alphas[j, q] * g
                means[j] = means[j] + masked * gain
            for j in range(q + 1, SUBLANES):
                for i in range(j, SUBLANES):
                    entry[i, j] = entry[i, j] + alphas[i, q] * afters[j, q] + entry[i, q] * alphas[j, q]
            g_c, g_b, g_a = whole(c_rows[b], q), whole(b_rows[b], q), whole(a_rows[b], q)
            masked_c = jnp.broadcast_to(mask_ref[k : k + 1, :], (SUBLANES, LANES)) * g_c
            masked_b = jnp.broadcast_to(mine_ref[k : k + 1, :], (SUBLANES, LANES)) * g_b
            alpha_c, alpha_b = masked_c * c, masked_b * c
            h_c, h_b = g_c + alpha_c * g, g_b + alpha_b * g
            mean = mean + masked_c * gain
            mean_own = mean_own + (masked_b * gain)[:1]
            alpha_ref[k : k + 1, :] = alpha_b[:1]
            anomaly_ref[k : k + 1, :] = g_a[:1]
            row_ref[0, k : k + 1, :] = alpha_c[:1]
            row_ref[1, k : k + 1, :] = h_c[:1]
            row_ref[2, k : k + 1, :] = h_b[:1]
            if q < SUBLANES - 1:
                g_i = columns[q]
                alpha_i = allowed[q] * g_i * c
                c_rows[b] = c_rows[b] + alpha_i * h_c + g_i * alpha_c
                b_rows[b] = b_rows[b] + alpha_i * h_b + g_i * alpha_b
                a_rows[b] = a_rows[b] + alpha_i * g_a
                for j in range(q + 1, SUBLANES):
                    columns[j] = columns[j] + alpha_i * afters[j, q] + g_i * alphas[j, q]
        for i in range(b + 1, blocks):
            columns = [lanes(c_rows[i], base + j) for j in range(SUBLANES)]
            allowed = [lanes(turns[i], base + j) for j in range(SUBLANES)]
            for q in range(SUBLANES):
                k = base + q
                g_i = columns[q]
                alpha_i = allowed[q] * g_i * scale[q]
                c_rows[i] = c_rows[i] + alpha_i * row_ref[1, k : k + 1, :] + g_i * row_ref[0, k : k + 1, :]
                b_rows[i] = b_rows[i] + alpha_i * row_ref[2, k : k + 1, :] + g_i * alpha_ref[k : k + 1, :]
                a_rows[i] = a_rows[i] + alpha_i * anomaly_ref[k : k + 1, :]
                for j in range(q + 1, SUBLANES):
                    columns[j] = columns[j] + alpha_i * afters[j, q] + g_i * alphas[j, q]

    transform = lax.dot_general(
        anomaly_ref[...], alpha_ref[...], (((0,), (0,)), ((), ())), precision=HIGHEST, preferred_element_type=F32
    )
    transform = transform[:members] + mean_own + (iota((members, LANES), 0) == iota((members, LANES), 1)).astype(F32)
    for item in todo:
        complete(*item)
    transform_ref[...] = transform


def analysis_kernel(n_lat, levels, parts, *refs):
    transform_ref, halo_ref, hi_ref, lo_ref, courant_ref, pair_ref, odd_ref = refs[:7]
    inner_refs, refs = refs[7 : 7 + len(parts)], refs[7 + len(parts) :]
    out_hbm, edge_hi_ref, edge_lo_ref, out_ref, wide_ref, out_sem = refs
    planes, members, width = hi_ref.shape
    rows = courant_ref.shape[0] // (2 * levels)
    cols = width // (rows - 2)
    my_lat = lax.axis_index("lat")
    lat_even = lax.rem(my_lat, 2) == 0
    has_south, has_north = (my_lat > 0).astype(F32), (my_lat < n_lat - 1).astype(F32)

    transform = transform_ref[:, :members]
    hi = transform.astype(BF16)
    lo = (transform - hi.astype(F32)).astype(BF16)
    for p in range(planes):
        first, inner = next((a, ref) for (a, z), ref in zip(parts, inner_refs, strict=True) if a <= p < z)
        _, _, south, north = winds_of(courant_ref, levels, p)
        near, far = pair_ref[p].astype(F32), odd_ref[p].astype(F32)
        for r in (0, rows - 1):
            n = p * rows + r
            f = inner[p - first, r] + edge_factor(courant_ref, levels, p, r) * pltpu.roll(halo_ref[...], LANES - 1 - 2 * n, 1)
            if r == 0:
                f = f + (south[:1] * has_south) * jnp.where(lat_even, far, near)
            else:
                f = f + (north[r:] * has_north) * jnp.where(lat_even, near, far)
            split_store(f, edge_hi_ref, edge_lo_ref, p, 0 if r == 0 else cols)
    for p in range(planes):
        for h_ref, l_ref, which in ((hi_ref, lo_ref, range(1, rows - 1)), (edge_hi_ref, edge_lo_ref, (0, rows - 1))):
            result = jnp.dot(hi, h_ref[p], preferred_element_type=F32)
            result = result + jnp.dot(lo, h_ref[p], preferred_element_type=F32)
            result = result + jnp.dot(hi, l_ref[p], preferred_element_type=F32)
            for i, r in enumerate(which):
                wide_ref[p % 2, pl.ds(r, members, stride=rows), :] = result[:, i * cols : (i + 1) * cols]
        out_ref[p] = wide_ref[p % 2].astype(BF16)
        pltpu.make_async_copy(out_ref.at[p], out_hbm.at[p], out_sem.at[p]).start()
    for p in range(planes):
        pltpu.make_async_copy(out_ref.at[p], out_hbm.at[p], out_sem.at[p]).wait()


def exchanged(x, axis, step):
    return lax.ppermute(x, axis, [(i, i ^ step) for i in range(lax.axis_size(axis))])


def exchanged_odd(x, axis):
    count = lax.axis_size(axis)
    return lax.ppermute(x, axis, [pair for i in range(1, count - 1, 2) for pair in ((i, i + 1), (i + 1, i))])


def per_device(prior_state, courant, obs_tile, obs_site, obs_value, obs_var, loc_bits, batch_order):
    fields, levels, members, rows, cols = prior_state.shape
    planes, depth = fields * levels, members * rows
    n_lat, n_lon = lax.axis_size("lat"), lax.axis_size("lon")
    nobs = obs_tile.shape[0]
    x = prior_state.reshape(planes, depth, cols)
    winds = courant.reshape(2 * levels * rows, cols)
    tile = obs_tile.reshape(1, nobs)
    site = obs_site.reshape(1, nobs)

    arguments = [pltpu.with_memory_space_constraint(array, pltpu.HBM) for array in (x, winds, tile, site, batch_order)]
    payload = pl.pallas_call(
        functools.partial(observe_kernel, n_lon, levels),
        out_shape=jax.ShapeDtypeStruct((2 * members + 2 * SUBLANES, LANES), BF16),
        in_specs=[HBM] * 5,
        out_specs=VMEM,
        scratch_shapes=[
            pltpu.VMEM(x.shape, BF16),
            pltpu.VMEM(winds.shape, F32),
            pltpu.VMEM(tile.shape, jnp.int32),
            pltpu.VMEM(site.shape, jnp.int32),
            pltpu.SMEM(batch_order.shape, jnp.int32),
            pltpu.SemaphoreType.DMA((5,)),
            pltpu.SemaphoreType.DMA((4,)),
        ],
        compiler_params=PARAMS,
        name="observe",
    )(*arguments)
    payload, x = lax.optimization_barrier((payload, x))

    def local(kernel, name, out, scratch, *operands):
        return pl.pallas_call(
            kernel,
            out_shape=out,
            in_specs=[VMEM] * len(operands),
            out_specs=jax.tree.map(lambda _: VMEM, out),
            scratch_shapes=scratch,
            compiler_params=PARAMS,
            cost_estimate=SMALL,
            name=name,
        )(*operands)

    def edge_rows(x, facing):
        return local(
            functools.partial(edge_rows_kernel, rows, facing),
            "edge_rows",
            jax.ShapeDtypeStruct((planes, members, cols), BF16),
            [pltpu.VMEM((planes, depth, cols), F32)],
            x,
        )

    def inner(x, start, stop):
        return local(
            functools.partial(inner_kernel, levels, start),
            "inner",
            jax.ShapeDtypeStruct((stop - start, rows, members, cols), F32),
            [pltpu.VMEM((stop - start, depth, cols), F32), pltpu.VMEM((stop - start, 5, rows, cols), F32)],
            x,
            winds,
        )

    lat_steps = [1 << i for i in range(n_lat.bit_length() - 1)]
    lon_steps = [2 << i for i in range(n_lon.bit_length() - 2)]
    size = (payload.shape[0] // 2 + 15) // 16 * 16
    half_type = jax.ShapeDtypeStruct((size, LANES), BF16)
    done = {}
    parts, inners = [], []

    def beside(stage, x):
        if stage == PLAN["columns"]:
            done["column"] = local(
                functools.partial(edge_columns_kernel, rows),
                "edge_columns",
                jax.ShapeDtypeStruct((members, LANES), BF16),
                [pltpu.VMEM((planes, depth, cols), F32)],
                x,
            )
        if stage == PLAN["pair"]:
            done["pair_rows"] = edge_rows(x, True)
            done["pair"] = exchanged(done["pair_rows"], "lat", 1)
        if stage == PLAN["odd"]:
            done["odd_rows"] = edge_rows(x, False)
            done["odd"] = exchanged_odd(done["odd_rows"], "lat")
        for start, stop in PLAN["inner"].get(stage, ()):
            parts.append((start, stop))
            inners.append(inner(x, start, stop))

    def settle(stage, *arrays):
        held = [done.pop(name) for name in PLAN["settle"].get(stage, ())]
        names = PLAN["settle"].get(stage, ())
        arrays, new, held = lax.optimization_barrier((arrays, list(inners), held))
        inners[:] = new
        done.update(zip(names, held, strict=True))
        return arrays

    other = exchanged(payload, "lon", 1)
    beside(0, x)
    half = local(half_kernel, "half", half_type, [], payload, other)
    half, x = settle(0, half, x)
    stage = 1
    for step in lat_steps:
        other = exchanged(half, "lat", step)
        beside(stage, x)
        half = half + other
        half, x = settle(stage, half, x)
        stage += 1
    block, blocks = done["column"], []
    for step in lon_steps:
        other = exchanged(jnp.concatenate([half, block], axis=0), "lon", step)
        beside(stage, x)
        block = other[size:]
        blocks.append(block)
        if step != lon_steps[-1]:
            half = half + other[:size]
            half, block, x = settle(stage, half, block, x)
            stage += 1
    join_type = jax.ShapeDtypeStruct((size + 2 * members, LANES), BF16)
    join = local(
        functools.partial(join_kernel, n_lon, len(blocks)), "join", join_type, [], half, other, done["column"], *blocks
    )
    join, x = settle(stage, join, x)
    received = exchanged(join, "lon", 1)
    beside(stage + 1, x)

    middle_type = jax.ShapeDtypeStruct((planes, members, (rows - 2) * cols), BF16)
    square_type = jax.ShapeDtypeStruct((members, LANES), F32)
    transform, halo, hi, lo = pl.pallas_call(
        functools.partial(filter_kernel, n_lon, levels, parts),
        out_shape=[square_type, square_type, middle_type, middle_type],
        in_specs=[SMEM] * 3 + [VMEM] * (5 + len(parts)),
        out_specs=[VMEM] * 4,
        scratch_shapes=[pltpu.VMEM((nobs, LANES), F32)] * 4 + [pltpu.VMEM((3, nobs, LANES), F32)],
        compiler_params=PARAMS,
        cost_estimate=SMALL,
        name="filter",
    )(batch_order, obs_value, obs_var, join[:size], received, tile, loc_bits, winds, *inners)

    edge_type = pltpu.VMEM((planes, members, 2 * cols), BF16)
    out = pl.pallas_call(
        functools.partial(analysis_kernel, n_lat, levels, parts),
        out_shape=jax.ShapeDtypeStruct((planes, depth, cols), BF16),
        in_specs=[VMEM] * (7 + len(parts)),
        out_specs=HBM,
        scratch_shapes=[
            edge_type,
            edge_type,
            pltpu.VMEM((planes, depth, cols), BF16),
            pltpu.VMEM((2, depth, cols), F32),
            pltpu.SemaphoreType.DMA((planes,)),
        ],
        compiler_params=PARAMS,
        name="analysis",
    )(transform, halo, hi, lo, winds, done["pair"], done["odd"], *inners)
    return out.reshape(prior_state.shape)


def solution(mesh):
    placed = (P(None, None, None, "lat", "lon"), P(None, None, "lat", "lon")) + (P(),) * 6
    return jax.shard_map(
        per_device,
        mesh=mesh,
        in_specs=placed,
        out_specs=P(None, None, None, "lat", "lon"),
        check_vma=False,
    )
```

time: 49.5 us -> 32.3 us (0.65)
  the two profiles are of different devices: /device:TPU:0 before, /device:TPU:3 now
where the time goes in v2:
time: 32.3 us; the launch traced here: 32.2 us
  starting transfers between devices  14.9 us (46%)
  Pallas kernels  12.2 us (38%)
  waiting for transfers between devices  4.71 us (15%)
    ppermute x7, starting transfers between devices, exchanged(): lax.ppermute(x, axis, [(i, i ^ step) for i in range(lax.axis_size(axis))])  10.8 us
    pallas_call x1, Pallas kernels, per_device(): pl.pallas_call(functools.partial(filter_kernel, n_lon, levels, parts), ou...  4.73 us
    ppermute x7, waiting for transfers between devices, exchanged(): lax.ppermute(x, axis, [(i, i ^ step) for i in range(lax.axis_size(axis))])  4.71 us
    ppermute x1, starting transfers between devices, exchanged_odd(): lax.ppermute(x, axis, [pair for i in range(1, count - 1, 2) for pair in (...  4.06 us
    pallas_call x7, Pallas kernels, local(): pl.pallas_call(kernel, out_shape=out, in_specs=[VMEM] * len(operands), ou...  2.86 us
    pallas_call x1, Pallas kernels, per_device(): pl.pallas_call(functools.partial(observe_kernel, n_lon, levels), out_shap...  2.54 us
    pallas_call x1, Pallas kernels, per_device(): pl.pallas_call(functools.partial(analysis_kernel, n_lat, levels, parts),...  2.09 us
  transfers between devices with their start and end apart: 8, of which 5 were waited for; matrix products, arithmetic and copies ran while one was open for 0% of the time, Pallas kernels for 24%

profile of v2, /device:TPU:3, one launch (start us, length us, event | category | flops | bytes accessed | tf_op | source)
XLA Modules:
  0.0 32.2 jit_solution(669577790332553445)
XLA Ops:
  0.0 0.0 copy-start
  0.0 0.0 copy-start.1
  0.0 2.5 %observe.1.full_ref = bf16[176,128]{1,0:T(8,128)(2,1)S(1)} custom-call(bf16[8,640,128]{2,1,0:T(8,128)(2,1)} %bitcast.5, f32[64,128]{1,0:T(8,128)} %bitcast.11, s32[1,64]{1,0:T(1,128)} %bitcast.16, s32[1,64]{1,0:T(1,128)} %bitcast.18, s32[4]{0:T(128)} %refs_0_.1), custom_call_target="tpu_custom_call" | custom-call | tf_op jit(solution)/shard_map/observe/pallas_call | solution.py:452
  2.5 0.7 %collective-permute-start = (bf16[176,128]{1,0:T(8,128)(2,1)S(1)}, bf16[176,128]{1,0:T(8,128)(2,1)S(1)}, u32[]{:S(2)}, u32[]{:S(2)}) collective-permute-start(bf16[176,128]{1,0:T(8,128)(2,1)S(1)} %observe.1.full_ref), channel_id=1, source_target_pairs={{0,1},{1,0},{2,3},{3,2},{4,5},{5,4},{6,7},{7,6},{8,9},{9,8},{10,11... | collective-permute-start | bytes 135176 | tf_op jit(solution)/shard_map/ppermute | solution.py:433
  3.3 0.0 copy-done
  3.3 0.7 %edge_columns.1.refs_2_ = bf16[80,128]{1,0:T(8,128)(2,1)S(1)} custom-call(bf16[8,640,128]{2,1,0:T(8,128)(2,1)S(1)} %bitcast.6), custom_call_target="tpu_custom_call" | custom-call | tf_op jit(solution)/shard_map/edge_columns/pallas_call | solution.py:472
  4.0 0.2 collective-permute-done.other_ref
  4.2 0.1 collective-permute-start.1
  4.3 0.0 copy-done.1
  4.3 0.9 %inner.2.refs_8_.refs_7_ = f32[5,8,80,128]{3,2,1,0:T(8,128)S(1)} custom-call(bf16[8,640,128]{2,1,0:T(8,128)(2,1)S(1)} %bitcast.7, f32[64,128]{1,0:T(8,128)S(1)} %bitcast.12), custom_call_target="tpu_custom_call" | custom-call | tf_op jit(solution)/shard_map/inner/pallas_call | solution.py:472
  5.2 1.7 %collective-permute-done.1 = bf16[96,128]{1,0:T(8,128)(2,1)S(1)} collective-permute-done((bf16[96,128]{1,0:T(8,128)(2,1)S(1)}, bf16[96,128]{1,0:T(8,128)(2,1)S(1)}, u32[]{:S(2)}, u32[]{:S(2)}) %collective-permute-start.1) | collective-permute-done | bytes 24608 | tf_op jit(solution)/shard_map/ppermute | solution.py:433
  6.9 1.3 %collective-permute-start.2 = (bf16[96,128]{1,0:T(8,128)(2,1)S(1)}, bf16[96,128]{1,0:T(8,128)(2,1)S(1)}, u32[]{:S(2)}, u32[]{:S(2)}) collective-permute-start(bf16[96,128]{1,0:T(8,128)(2,1)S(1)} %add.9), channel_id=1, source_target_pairs={{0,16},{8,24},{16,0},{24,8},{1,17},{9,25},{17,1},{25,9},{2,18},{10... | collective-permute-start | bytes 73736 | tf_op jit(solution)/shard_map/ppermute | solution.py:433
  8.2 0.3 %edge_rows.3 = bf16[8,80,128]{2,1,0:T(8,128)(2,1)S(1)} custom-call(bf16[8,640,128]{2,1,0:T(8,128)(2,1)S(1)} %bitcast.8), custom_call_target="tpu_custom_call" | custom-call | tf_op jit(solution)/shard_map/edge_rows/pallas_call | solution.py:472
  8.6 0.3 %edge_rows.2 = bf16[8,80,128]{2,1,0:T(8,128)(2,1)S(1)} custom-call(bf16[8,640,128]{2,1,0:T(8,128)(2,1)S(1)} %bitcast.9), custom_call_target="tpu_custom_call" | custom-call | tf_op jit(solution)/shard_map/edge_rows/pallas_call | solution.py:472
  8.9 0.0 copy-start.6
  8.9 0.0 copy-start.2
  8.9 0.0 copy-start.3
  8.9 0.0 copy-start.4
  8.9 0.0 copy-start.5
  9.0 0.6 %inner.3.refs_9_.refs_8_ = f32[3,8,80,128]{3,2,1,0:T(8,128)S(1)} custom-call(bf16[8,640,128]{2,1,0:T(8,128)(2,1)S(1)} %bitcast.10, f32[64,128]{1,0:T(8,128)S(1)} %bitcast.13), custom_call_target="tpu_custom_call" | custom-call | tf_op jit(solution)/shard_map/inner/pallas_call | solution.py:472
  9.5 0.1 collective-permute-done.2
  9.7 1.4 %collective-permute-start.3 = (bf16[176,128]{1,0:T(8,128)(2,1)S(1)}, bf16[176,128]{1,0:T(8,128)(2,1)S(1)}, u32[]{:S(2)}, u32[]{:S(2)}) collective-permute-start(bf16[176,128]{1,0:T(8,128)(2,1)S(1)} %pad_maximum_fusion), channel_id=1, source_target_pairs={{0,2},{1,3},{2,0},{3,1},{4,6},{5,7},{6,4},{7,5},{8,10},{9,11},{10,... | collective-permute-start | bytes 135176 | tf_op jit(solution)/shard_map/ppermute | solution.py:433
  11.1 0.3 collective-permute-start.5
  11.3 4.1 %collective-permute-start.7 = (bf16[8,80,128]{2,1,0:T(8,128)(2,1)S(1)}, bf16[8,80,128]{2,1,0:T(8,128)(2,1)S(1)}, u32[]{:S(2)}, u32[]{:S(2)}) collective-permute-start(bf16[8,80,128]{2,1,0:T(8,128)(2,1)S(1)} %edge_rows.3), channel_id=1, source_target_pairs={{8,16},{16,8},{9,17},{17,9},{10,18},{18,10},{11,19},{19,11},{12,20... | collective-permute-start | bytes 491528 | tf_op jit(solution)/shard_map/ppermute | solution.py:438
  15.4 0.0 collective-permute-done.3
  15.4 2.4 %collective-permute-start.4 = (bf16[176,128]{1,0:T(8,128)(2,1)S(1)}, bf16[176,128]{1,0:T(8,128)(2,1)S(1)}, u32[]{:S(2)}, u32[]{:S(2)}) collective-permute-start(bf16[176,128]{1,0:T(8,128)(2,1)S(1)} %pad_maximum_fusion.1), channel_id=1, source_target_pairs={{0,4},{1,5},{2,6},{3,7},{4,0},{5,1},{6,2},{7,3},{8,12},{9,13},{10,... | collective-permute-start | bytes 135176 | tf_op jit(solution)/shard_map/ppermute | solution.py:433
  17.8 1.8 %collective-permute-done.4.refs_1_ = bf16[176,128]{1,0:T(8,128)(2,1)S(1)} collective-permute-done((bf16[176,128]{1,0:T(8,128)(2,1)S(1)}, bf16[176,128]{1,0:T(8,128)(2,1)S(1)}, u32[]{:S(2)}, u32[]{:S(2)}) %collective-permute-start.4) | collective-permute-done | bytes 45088 | tf_op jit(solution)/shard_map/ppermute | solution.py:433
  19.7 0.0 collective-permute-done.5.refs_5_
  19.7 4.7 %collective-permute-start.6 = (bf16[256,128]{1,0:T(8,128)(2,1)S(1)}, bf16[256,128]{1,0:T(8,128)(2,1)S(1)}, u32[]{:S(2)}, u32[]{:S(2)}) collective-permute-start(bf16[256,128]{1,0:T(8,128)(2,1)S(1)} %join.1), channel_id=1, source_target_pairs={{0,1},{1,0},{2,3},{3,2},{4,5},{5,4},{6,7},{7,6},{8,9},{9,8},{10,11... | collective-permute-start | bytes 196616 | tf_op jit(solution)/shard_map/ppermute | solution.py:433
  24.4 0.0 copy-done.6
  24.4 0.1 copy.9.refs_6_
  24.5 0.8 %collective-permute-done.6.refs_4_ = bf16[256,128]{1,0:T(8,128)(2,1)S(1)} collective-permute-done((bf16[256,128]{1,0:T(8,128)(2,1)S(1)}, bf16[256,128]{1,0:T(8,128)(2,1)S(1)}, u32[]{:S(2)}, u32[]{:S(2)}) %collective-permute-start.6) | collective-permute-done | bytes 65568 | tf_op jit(solution)/shard_map/ppermute | solution.py:433
  25.3 0.0 copy-done.2
  25.3 0.0 copy-done.3
  25.3 0.0 copy-done.4
  25.3 0.0 copy-done.5
  25.3 4.7 %filter.1 = (f32[80,128]{1,0:T(8,128)S(1)}, f32[80,128]{1,0:T(8,128)S(1)}, bf16[8,80,768]{2,1,0:T(8,128)(2,1)S(1)}, bf16[8,80,768]{2,1,0:T(8,128)(2,1)S(1)}) custom-call(s32[4]{0:T(128)S(1)} %copy-done.2, f32[64]{0:T(128)S(1)} %copy-done.4, f32[64]{0:T(128)S(1)} %copy-done.5, bf16[96,128]{1,0:T(8,128)(2,1)S(1)} %slice.15.refs_3_, ...), custom_call_target="tpu_custom_call" | custom-call | tf_op jit(solution)/shard_map/filter/pallas_call | solution.py:567
  30.1 0.0 collective-permute-done.7.refs_6_
  30.1 2.1 %analysis.1 = bf16[8,640,128]{2,1,0:T(8,128)(2,1)} custom-call(f32[80,128]{1,0:T(8,128)S(1)} %get-tuple-element.46.refs_0_, f32[80,128]{1,0:T(8,128)S(1)} %get-tuple-element.47.refs_1_, bf16[8,80,768]{2,1,0:T(8,128)(2,1)S(1)} %get-tuple-element.48.refs_2_, bf16[8,80,768]{2,1,0:T(8,128)(2,1)S(1)} %get-tuple-element.49.refs_3_, f32[64,128]{1,0:T(8,128)S(1)} %bitcast.15, ...), custom_call_target="tpu_custom_call" | custom-call | tf_op jit(solution)/shard_map/analysis/pallas_call | solution.py:579
  (10 shorter events, 0.1 us)
Async XLA Ops:
  0.0 3.3 %copy-start = (bf16[2,4,80,8,128]{4,3,2,1,0:T(8,128)(2,1)S(1)}, bf16[2,4,80,8,128]{4,3,2,1,0:T(8,128)(2,1)}, u32[]{:S(2)}) copy-start(bf16[2,4,80,8,128]{4,3,2,1,0:T(8,128)(2,1)} %param.8) | copy-start | bytes 3932164
  0.0 4.3 %copy-start.1 = (f32[2,4,8,128]{3,2,1,0:T(8,128)S(1)}, f32[2,4,8,128]{3,2,1,0:T(8,128)}, u32[]{:S(2)}) copy-start(f32[2,4,8,128]{3,2,1,0:T(8,128)} %param.9) | copy-start | bytes 98308
  2.5 1.6 %collective-permute-start = (bf16[176,128]{1,0:T(8,128)(2,1)S(1)}, bf16[176,128]{1,0:T(8,128)(2,1)S(1)}, u32[]{:S(2)}, u32[]{:S(2)}) collective-permute-start(bf16[176,128]{1,0:T(8,128)(2,1)S(1)} %observe.1.full_ref), channel_id=1, source_target_pairs={{0,1},{1,0},{2,3},{3,2},{4,5},{5,4},{6,7},{7,6},{8,9},{9,8},{10,11... | collective-permute-start | bytes 135176 | tf_op jit(solution)/shard_map/ppermute | solution.py:433
  4.2 2.7 %collective-permute-start.1 = (bf16[96,128]{1,0:T(8,128)(2,1)S(1)}, bf16[96,128]{1,0:T(8,128)(2,1)S(1)}, u32[]{:S(2)}, u32[]{:S(2)}) collective-permute-start(bf16[96,128]{1,0:T(8,128)(2,1)S(1)} %half.1), channel_id=1, source_target_pairs={{0,8},{8,0},{16,24},{24,16},{1,9},{9,1},{17,25},{25,17},{2,10},{10... | collective-permute-start | bytes 73736 | tf_op jit(solution)/shard_map/ppermute | solution.py:433
  6.9 2.7 %collective-permute-start.2 = (bf16[96,128]{1,0:T(8,128)(2,1)S(1)}, bf16[96,128]{1,0:T(8,128)(2,1)S(1)}, u32[]{:S(2)}, u32[]{:S(2)}) collective-permute-start(bf16[96,128]{1,0:T(8,128)(2,1)S(1)} %add.9), channel_id=1, source_target_pairs={{0,16},{8,24},{16,0},{24,8},{1,17},{9,25},{17,1},{25,9},{2,18},{10... | collective-permute-start | bytes 73736 | tf_op jit(solution)/shard_map/ppermute | solution.py:433
  8.9 15.5 %copy-start.6 = (s32[64,2]{0,1:T(2,128)S(1)}, s32[64,2]{0,1:T(2,128)}, u32[]{:S(2)}) copy-start(s32[64,2]{0,1:T(2,128)} %param.14) | copy-start | bytes 1540
  8.9 16.4 %copy-start.2 = (s32[4]{0:T(128)S(1)}, s32[4]{0:T(128)}, u32[]{:S(2)}) copy-start(s32[4]{0:T(128)} %refs_0_.1) | copy-start | bytes 52
  8.9 16.4 %copy-start.3 = (s32[64]{0:T(128)S(1)}, s32[64]{0:T(128)}, u32[]{:S(2)}) copy-start(s32[64]{0:T(128)} %param.10) | copy-start | bytes 772
  8.9 16.4 %copy-start.4 = (f32[64]{0:T(128)S(1)}, f32[64]{0:T(128)}, u32[]{:S(2)}) copy-start(f32[64]{0:T(128)} %refs_1_.1) | copy-start | bytes 772
  8.9 16.4 %copy-start.5 = (f32[64]{0:T(128)S(1)}, f32[64]{0:T(128)}, u32[]{:S(2)}) copy-start(f32[64]{0:T(128)} %refs_2_.1) | copy-start | bytes 772
  9.7 5.7 %collective-permute-start.3 = (bf16[176,128]{1,0:T(8,128)(2,1)S(1)}, bf16[176,128]{1,0:T(8,128)(2,1)S(1)}, u32[]{:S(2)}, u32[]{:S(2)}) collective-permute-start(bf16[176,128]{1,0:T(8,128)(2,1)S(1)} %pad_maximum_fusion), channel_id=1, source_target_pairs={{0,2},{1,3},{2,0},{3,1},{4,6},{5,7},{6,4},{7,5},{8,10},{9,11},{10,... | collective-permute-start | bytes 135176 | tf_op jit(solution)/shard_map/ppermute | solution.py:433
  11.1 8.6 %collective-permute-start.5 = (bf16[8,80,128]{2,1,0:T(8,128)(2,1)S(1)}, bf16[8,80,128]{2,1,0:T(8,128)(2,1)S(1)}, u32[]{:S(2)}, u32[]{:S(2)}) collective-permute-start(bf16[8,80,128]{2,1,0:T(8,128)(2,1)S(1)} %edge_rows.2), channel_id=1, source_target_pairs={{0,8},{8,0},{16,24},{24,16},{1,9},{9,1},{17,25},{25,17},{2,10},{10... | collective-permute-start | bytes 491528 | tf_op jit(solution)/shard_map/ppermute | solution.py:433
  11.3 18.7 %collective-permute-start.7 = (bf16[8,80,128]{2,1,0:T(8,128)(2,1)S(1)}, bf16[8,80,128]{2,1,0:T(8,128)(2,1)S(1)}, u32[]{:S(2)}, u32[]{:S(2)}) collective-permute-start(bf16[8,80,128]{2,1,0:T(8,128)(2,1)S(1)} %edge_rows.3), channel_id=1, source_target_pairs={{8,16},{16,8},{9,17},{17,9},{10,18},{18,10},{11,19},{19,11},{12,20... | collective-permute-start | bytes 491528 | tf_op jit(solution)/shard_map/ppermute | solution.py:438
  15.4 4.2 %collective-permute-start.4 = (bf16[176,128]{1,0:T(8,128)(2,1)S(1)}, bf16[176,128]{1,0:T(8,128)(2,1)S(1)}, u32[]{:S(2)}, u32[]{:S(2)}) collective-permute-start(bf16[176,128]{1,0:T(8,128)(2,1)S(1)} %pad_maximum_fusion.1), channel_id=1, source_target_pairs={{0,4},{1,5},{2,6},{3,7},{4,0},{5,1},{6,2},{7,3},{8,12},{9,13},{10,... | collective-permute-start | bytes 135176 | tf_op jit(solution)/shard_map/ppermute | solution.py:433
  19.7 5.6 %collective-permute-start.6 = (bf16[256,128]{1,0:T(8,128)(2,1)S(1)}, bf16[256,128]{1,0:T(8,128)(2,1)S(1)}, u32[]{:S(2)}, u32[]{:S(2)}) collective-permute-start(bf16[256,128]{1,0:T(8,128)(2,1)S(1)} %join.1), channel_id=1, source_target_pairs={{0,1},{1,0},{2,3},{3,2},{4,5},{5,4},{6,7},{7,6},{8,9},{9,8},{10,11... | collective-permute-start | bytes 196616 | tf_op jit(solution)/shard_map/ppermute | solution.py:433

commit v3 on v2

--- a/solution.py
+++ b/solution.py
@@ -10,7 +10,7 @@
 EPSILON = 1e-05
 HIGHEST = lax.Precision.HIGHEST
 LANES = 128
-PLAN = {"columns": 0, "pair": 2, "odd": 2, "inner": {1: [(0, 5)], 2: [(5, 8)]}, "settle": {0: ["column"], 2: ["pair_rows", "odd_rows"], 4:["pair"]}}
+PLAN = {"filter": 0, "columns": 0, "pair": 2, "odd": 2, "inner": {1: [(0, 5)], 2: [(5, 8)]}, "settle": {0: ["column"], 2: ["pair_rows", "odd_rows"]}}
 SUBLANES = 8
 F32 = jnp.float32
 BF16 = jnp.bfloat16
@@ -252,7 +252,7 @@
 def filter_kernel(n_lon, levels, parts, *refs):
     order_ref, value_ref, var_ref, mine_half_ref, join_ref, tile_ref, bits_ref, courant_ref = refs[:8]
     inner_refs, refs = refs[8 : 8 + len(parts)], refs[8 + len(parts) :]
-    transform_ref, halo_ref, hi_ref, lo_ref, alpha_ref, anomaly_ref, mask_ref, mine_ref, row_ref = refs
+    transform_ref, halo_ref, hi_ref, lo_ref, alpha_ref, anomaly_ref, mask_ref, mine_ref, row_ref, move_ref = refs
     planes, members, width = hi_ref.shape
     rows = courant_ref.shape[0] // (2 * levels)
     cols = width // (rows - 2)
@@ -300,17 +300,17 @@
     prior = jnp.where(iota((members, LANES), 1) < nobs, both + pltpu.roll(both, nobs, 1), 0.0)
     mean = jnp.sum(prior, axis=0, keepdims=True) * (1.0 / members)
     spread = prior - mean
-    gram = lax.dot_general(spread, spread, (((0,), (0,)), ((), ())), precision=HIGHEST, preferred_element_type=F32)
+    inv = 1.0 / (members - 1)
+    gram = inv * lax.dot_general(spread, spread, (((0,), (0,)), ((), ())), precision=HIGHEST, preferred_element_type=F32)
     tall = jnp.concatenate([spread, jnp.zeros((LANES - members, LANES), F32)], axis=0).T
 
     def cut(array):
         return [array[b * SUBLANES : (b + 1) * SUBLANES] for b in range(blocks)]
 
-    c_rows, b_rows, a_rows = cut(gram), cut(tall), cut(tall)
+    c_rows, b_rows, a_rows = cut(gram), cut(tall * inv), cut(tall)
     turns = cut(turned)
     mean = jnp.broadcast_to(mean, (SUBLANES, LANES))
     mean_own = jnp.zeros((1, LANES), F32)
-    inv = 1.0 / (members - 1)
 
     def whole(array, s):
         return jnp.broadcast_to(array[s : s + 1], (SUBLANES, LANES))
@@ -321,12 +321,21 @@
     for b in range(blocks):
         base = b * SUBLANES
         at = order_ref[base // batch] * batch + base % batch
-        columns = [lanes(c_rows[b], base + j) for j in range(SUBLANES)]
-        allowed = [lanes(turns[b], base + j) for j in range(SUBLANES)]
-        entry = {(i, j): whole(columns[j], i) for j in range(SUBLANES) for i in range(j, SUBLANES)}
-        allow = {(j, q): whole(allowed[q], j) for q in range(SUBLANES) for j in range(q + 1, SUBLANES)}
+        ahead = range(b, min(b + 3, blocks))
+        columns = {i: [lanes(c_rows[i], base + j) for j in range(SUBLANES)] for i in ahead}
+        allowed = {i: [lanes(turns[i], base + j) for j in range(SUBLANES)] for i in ahead}
+        place = move_ref.at[b % 2]
+        for j in range(SUBLANES):
+            place[4 + j] = columns[b][j]
+            place[12 + j] = allowed[b][j]
+
+        def taken(i, s):
+            return jnp.broadcast_to(move_ref[b % 2, i, s : s + 1, :], (SUBLANES, LANES))
+
+        entry = {(i, j): taken(4 + j, i) for j in range(SUBLANES) for i in range(j, SUBLANES)}
+        allow = {(j, q): taken(12 + q, j) for q in range(SUBLANES) for j in range(q + 1, SUBLANES)}
         means = [lanes(mean, base + j) for j in range(SUBLANES)]
-        scale, alphas, afters = [], {}, {}
+        alphas, afters = {}, {}
         for q in range(SUBLANES):
             k = base + q
             for _ in range(each):
@@ -335,11 +344,14 @@
             r = jnp.full((SUBLANES, LANES), var_ref[at + q], F32)
             o = jnp.full((SUBLANES, LANES), value_ref[at + q], F32)
             g = entry[q, q]
-            u = lax.rsqrt(g * inv + EPSILON + r)
-            uu = u * u * inv
-            c = -uu / (1.0 + jnp.sqrt(r) * u)
+            u = lax.rsqrt(total if q else g + (r + EPSILON))
+            uu = u * u
+            c = -uu * pl.reciprocal(1.0 + jnp.sqrt(r) * u, approx=True)
             gain = uu * (o - means[q])
-            scale.append(c)
+            if q + 1 < SUBLANES:
+                g_j, masked = entry[q + 1, q], allow[q + 1, q] * entry[q + 1, q]
+                next_r = jnp.full((SUBLANES, LANES), var_ref[at + q + 1], F32) + EPSILON
+                total = (entry[q + 1, q + 1] + next_r) + c * (2.0 * masked * g_j + c * (masked * masked * g))
             for j in range(q + 1, SUBLANES):
                 masked = allow[j, q] * entry[j, q]
                 alphas[j, q] = masked * c
@@ -360,26 +372,30 @@
             row_ref[0, k : k + 1, :] = alpha_c[:1]
             row_ref[1, k : k + 1, :] = h_c[:1]
             row_ref[2, k : k + 1, :] = h_b[:1]
-            if q < SUBLANES - 1:
-                g_i = columns[q]
-                alpha_i = allowed[q] * g_i * c
-                c_rows[b] = c_rows[b] + alpha_i * h_c + g_i * alpha_c
-                b_rows[b] = b_rows[b] + alpha_i * h_b + g_i * alpha_b
-                a_rows[b] = a_rows[b] + alpha_i * g_a
+            row_ref[3, k : k + 1, :] = g_c[:1]
+            for i in ahead:
+                if i == b and q == SUBLANES - 1:
+                    continue
+                g_i = columns[i][q]
+                alpha_i = allowed[i][q] * g_i * c
+                c_rows[i] = c_rows[i] + alpha_i * h_c + g_i * alpha_c
+                b_rows[i] = b_rows[i] + alpha_i * h_b + g_i * alpha_b
+                a_rows[i] = a_rows[i] + alpha_i * g_a
                 for j in range(q + 1, SUBLANES):
-                    columns[j] = columns[j] + alpha_i * afters[j, q] + g_i * alphas[j, q]
-        for i in range(b + 1, blocks):
-            columns = [lanes(c_rows[i], base + j) for j in range(SUBLANES)]
-            allowed = [lanes(turns[i], base + j) for j in range(SUBLANES)]
-            for q in range(SUBLANES):
-                k = base + q
-                g_i = columns[q]
-                alpha_i = allowed[q] * g_i * scale[q]
-                c_rows[i] = c_rows[i] + alpha_i * row_ref[1, k : k + 1, :] + g_i * row_ref[0, k : k + 1, :]
-                b_rows[i] = b_rows[i] + alpha_i * row_ref[2, k : k + 1, :] + g_i * alpha_ref[k : k + 1, :]
-                a_rows[i] = a_rows[i] + alpha_i * anomaly_ref[k : k + 1, :]
-                for j in range(q + 1, SUBLANES):
-                    columns[j] = columns[j] + alpha_i * afters[j, q] + g_i * alphas[j, q]
+                    columns[i][j] = columns[i][j] + alpha_i * afters[j, q] + g_i * alphas[j, q]
+        if b + 3 < blocks:
+            own = slice(base, base + SUBLANES)
+            alpha_c, h_c, h_b, g_c = (row_ref[i, own, :] for i in range(4))
+            left = jnp.concatenate([alpha_c, g_c], axis=0)[:, :nobs]
+            zero = jnp.zeros((SUBLANES, LANES), F32)
+            upper = jnp.concatenate([h_c, h_b, anomaly_ref[own, :]], axis=1)
+            right = jnp.concatenate([upper, jnp.concatenate([alpha_c, alpha_ref[own, :], zero], axis=1)], axis=0)
+            change = lax.dot_general(left, right, (((0,), (0,)), ((), ())), precision=HIGHEST, preferred_element_type=F32)
+            for i in range(b + 3, blocks):
+                part = change[i * SUBLANES : (i + 1) * SUBLANES]
+                c_rows[i] = c_rows[i] + part[:, :LANES]
+                b_rows[i] = b_rows[i] + part[:, LANES : 2 * LANES]
+                a_rows[i] = a_rows[i] + part[:, 2 * LANES :]
 
     transform = lax.dot_general(
         anomaly_ref[...], alpha_ref[...], (((0,), (0,)), ((), ())), precision=HIGHEST, preferred_element_type=F32
@@ -435,7 +451,7 @@
 
 def exchanged_odd(x, axis):
     count = lax.axis_size(axis)
-    return lax.ppermute(x, axis, [pair for i in range(1, count - 1, 2) for pair in ((i, i + 1), (i + 1, i))])
+    return lax.ppermute(x, axis, [pair for i in range(1, count, 2) for pair in ((i, (i + 1) % count), ((i + 1) % count, i))])
 
 
 def per_device(prior_state, courant, obs_tile, obs_site, obs_value, obs_var, loc_bits, batch_order):
@@ -569,9 +585,9 @@
         out_shape=[square_type, square_type, middle_type, middle_type],
         in_specs=[SMEM] * 3 + [VMEM] * (5 + len(parts)),
         out_specs=[VMEM] * 4,
-        scratch_shapes=[pltpu.VMEM((nobs, LANES), F32)] * 4 + [pltpu.VMEM((3, nobs, LANES), F32)],
+        scratch_shapes=[pltpu.VMEM((nobs, LANES), F32)] * 4 + [pltpu.VMEM((4, nobs, LANES), F32), pltpu.VMEM((2, 32, SUBLANES, LANES), F32)],
         compiler_params=PARAMS,
-        cost_estimate=SMALL,
+        cost_estimate=pl.CostEstimate(flops=0, bytes_accessed=PLAN["filter"], transcendentals=0),
         name="filter",
     )(batch_order, obs_value, obs_var, join[:size], received, tile, loc_bits, winds, *inners)
 

time: 32.3 us -> 30.4 us (0.941)
  the two profiles are of different devices: /device:TPU:3 before, /device:TPU:0 now
where the time goes in v3:
time: 30.4 us; the launch traced here: 30.3 us
  starting transfers between devices  13.4 us (44%)
  Pallas kernels  11.5 us (38%)
  waiting for transfers between devices  5.07 us (17%)
    ppermute x7, starting transfers between devices, exchanged(): lax.ppermute(x, axis, [(i, i ^ step) for i in range(lax.axis_size(axis))])  11.9 us
    ppermute x7, waiting for transfers between devices, exchanged(): lax.ppermute(x, axis, [(i, i ^ step) for i in range(lax.axis_size(axis))])  5.07 us
    pallas_call x1, Pallas kernels, per_device(): pl.pallas_call(functools.partial(filter_kernel, n_lon, levels, parts), ou...  3.99 us
    pallas_call x7, Pallas kernels, local(): pl.pallas_call(kernel, out_shape=out, in_specs=[VMEM] * len(operands), ou...  2.86 us
    pallas_call x1, Pallas kernels, per_device(): pl.pallas_call(functools.partial(observe_kernel, n_lon, levels), out_shap...  2.54 us
    pallas_call x1, Pallas kernels, per_device(): pl.pallas_call(functools.partial(analysis_kernel, n_lat, levels, parts),...  2.09 us
    ppermute x1, starting transfers between devices, exchanged_odd(): lax.ppermute(x, axis, [pair for i in range(1, count, 2) for pair in ((i,...  1.49 us
  transfers between devices with their start and end apart: 8, of which 5 were waited for; matrix products, arithmetic and copies ran while one was open for 0% of the time, Pallas kernels for 23%

profile of v3, /device:TPU:0, one launch (start us, length us, event | category | flops | bytes accessed | tf_op | source)
XLA Modules:
  0.0 30.3 jit_solution(16875357517726003907)
XLA Ops:
  0.0 0.0 copy-start
  0.0 0.0 copy-start.1
  0.0 2.5 %observe.1.full_ref = bf16[176,128]{1,0:T(8,128)(2,1)S(1)} custom-call(bf16[8,640,128]{2,1,0:T(8,128)(2,1)} %bitcast.5, f32[64,128]{1,0:T(8,128)} %bitcast.11, s32[1,64]{1,0:T(1,128)} %bitcast.16, s32[1,64]{1,0:T(1,128)} %bitcast.18, s32[4]{0:T(128)} %refs_0_.1), custom_call_target="tpu_custom_call" | custom-call | tf_op jit(solution)/shard_map/observe/pallas_call | solution.py:468
  2.5 0.5 %collective-permute-start = (bf16[176,128]{1,0:T(8,128)(2,1)S(1)}, bf16[176,128]{1,0:T(8,128)(2,1)S(1)}, u32[]{:S(2)}, u32[]{:S(2)}) collective-permute-start(bf16[176,128]{1,0:T(8,128)(2,1)S(1)} %observe.1.full_ref), channel_id=1, source_target_pairs={{0,1},{1,0},{2,3},{3,2},{4,5},{5,4},{6,7},{7,6},{8,9},{9,8},{10,11... | collective-permute-start | bytes 135176 | tf_op jit(solution)/shard_map/ppermute | solution.py:449
  3.1 0.0 copy-done
  3.1 0.7 %edge_columns.1.refs_2_ = bf16[80,128]{1,0:T(8,128)(2,1)S(1)} custom-call(bf16[8,640,128]{2,1,0:T(8,128)(2,1)S(1)} %bitcast.6), custom_call_target="tpu_custom_call" | custom-call | tf_op jit(solution)/shard_map/edge_columns/pallas_call | solution.py:488
  3.7 0.2 collective-permute-done.other_ref
  4.0 2.9 %collective-permute-start.1 = (bf16[96,128]{1,0:T(8,128)(2,1)S(1)}, bf16[96,128]{1,0:T(8,128)(2,1)S(1)}, u32[]{:S(2)}, u32[]{:S(2)}) collective-permute-start(bf16[96,128]{1,0:T(8,128)(2,1)S(1)} %half.1), channel_id=1, source_target_pairs={{0,8},{8,0},{16,24},{24,16},{1,9},{9,1},{17,25},{25,17},{2,10},{10... | collective-permute-start | bytes 73736 | tf_op jit(solution)/shard_map/ppermute | solution.py:449
  6.9 0.0 copy-done.1
  6.9 0.9 %inner.2.refs_8_.refs_7_ = f32[5,8,80,128]{3,2,1,0:T(8,128)S(1)} custom-call(bf16[8,640,128]{2,1,0:T(8,128)(2,1)S(1)} %bitcast.7, f32[64,128]{1,0:T(8,128)S(1)} %bitcast.12), custom_call_target="tpu_custom_call" | custom-call | tf_op jit(solution)/shard_map/inner/pallas_call | solution.py:488
  7.8 0.9 %collective-permute-done.1 = bf16[96,128]{1,0:T(8,128)(2,1)S(1)} collective-permute-done((bf16[96,128]{1,0:T(8,128)(2,1)S(1)}, bf16[96,128]{1,0:T(8,128)(2,1)S(1)}, u32[]{:S(2)}, u32[]{:S(2)}) %collective-permute-start.1) | collective-permute-done | bytes 24608 | tf_op jit(solution)/shard_map/ppermute | solution.py:449
  8.7 2.1 %collective-permute-start.2 = (bf16[96,128]{1,0:T(8,128)(2,1)S(1)}, bf16[96,128]{1,0:T(8,128)(2,1)S(1)}, u32[]{:S(2)}, u32[]{:S(2)}) collective-permute-start(bf16[96,128]{1,0:T(8,128)(2,1)S(1)} %add.9), channel_id=1, source_target_pairs={{0,16},{8,24},{16,0},{24,8},{1,17},{9,25},{17,1},{25,9},{2,18},{10... | collective-permute-start | bytes 73736 | tf_op jit(solution)/shard_map/ppermute | solution.py:449
  10.8 0.3 %edge_rows.3 = bf16[8,80,128]{2,1,0:T(8,128)(2,1)S(1)} custom-call(bf16[8,640,128]{2,1,0:T(8,128)(2,1)S(1)} %bitcast.8), custom_call_target="tpu_custom_call" | custom-call | tf_op jit(solution)/shard_map/edge_rows/pallas_call | solution.py:488
  11.1 0.3 %edge_rows.2 = bf16[8,80,128]{2,1,0:T(8,128)(2,1)S(1)} custom-call(bf16[8,640,128]{2,1,0:T(8,128)(2,1)S(1)} %bitcast.9), custom_call_target="tpu_custom_call" | custom-call | tf_op jit(solution)/shard_map/edge_rows/pallas_call | solution.py:488
  11.4 0.0 copy-start.6
  11.5 0.0 copy-start.2
  11.5 0.0 copy-start.3
  11.5 0.0 copy-start.4
  11.5 0.0 copy-start.5
  11.5 0.6 %inner.3.refs_9_.refs_8_ = f32[3,8,80,128]{3,2,1,0:T(8,128)S(1)} custom-call(bf16[8,640,128]{2,1,0:T(8,128)(2,1)S(1)} %bitcast.10, f32[64,128]{1,0:T(8,128)S(1)} %bitcast.13), custom_call_target="tpu_custom_call" | custom-call | tf_op jit(solution)/shard_map/inner/pallas_call | solution.py:488
  12.1 0.5 %collective-permute-done.2 = bf16[96,128]{1,0:T(8,128)(2,1)S(1)} collective-permute-done((bf16[96,128]{1,0:T(8,128)(2,1)S(1)}, bf16[96,128]{1,0:T(8,128)(2,1)S(1)}, u32[]{:S(2)}, u32[]{:S(2)}) %collective-permute-start.2) | collective-permute-done | bytes 24608 | tf_op jit(solution)/shard_map/ppermute | solution.py:449
  12.6 2.1 %collective-permute-start.3 = (bf16[176,128]{1,0:T(8,128)(2,1)S(1)}, bf16[176,128]{1,0:T(8,128)(2,1)S(1)}, u32[]{:S(2)}, u32[]{:S(2)}) collective-permute-start(bf16[176,128]{1,0:T(8,128)(2,1)S(1)} %pad_maximum_fusion), channel_id=1, source_target_pairs={{0,2},{1,3},{2,0},{3,1},{4,6},{5,7},{6,4},{7,5},{8,10},{9,11},{10,... | collective-permute-start | bytes 135176 | tf_op jit(solution)/shard_map/ppermute | solution.py:449
  14.8 1.5 %collective-permute-start.6 = (bf16[8,80,128]{2,1,0:T(8,128)(2,1)S(1)}, bf16[8,80,128]{2,1,0:T(8,128)(2,1)S(1)}, u32[]{:S(2)}, u32[]{:S(2)}) collective-permute-start(bf16[8,80,128]{2,1,0:T(8,128)(2,1)S(1)} %edge_rows.2), channel_id=1, source_target_pairs={{0,8},{8,0},{16,24},{24,16},{1,9},{9,1},{17,25},{25,17},{2,10},{10... | collective-permute-start | bytes 491528 | tf_op jit(solution)/shard_map/ppermute | solution.py:449
  16.3 1.5 %collective-permute-start.7 = (bf16[8,80,128]{2,1,0:T(8,128)(2,1)S(1)}, bf16[8,80,128]{2,1,0:T(8,128)(2,1)S(1)}, u32[]{:S(2)}, u32[]{:S(2)}) collective-permute-start(bf16[8,80,128]{2,1,0:T(8,128)(2,1)S(1)} %edge_rows.3), channel_id=1, source_target_pairs={{8,16},{16,8},{24,0},{0,24},{9,17},{17,9},{25,1},{1,25},{10,18},{1... | collective-permute-start | bytes 491528 | tf_op jit(solution)/shard_map/ppermute | solution.py:454
  17.8 0.0 collective-permute-done.3
  17.8 2.6 %collective-permute-start.4 = (bf16[176,128]{1,0:T(8,128)(2,1)S(1)}, bf16[176,128]{1,0:T(8,128)(2,1)S(1)}, u32[]{:S(2)}, u32[]{:S(2)}) collective-permute-start(bf16[176,128]{1,0:T(8,128)(2,1)S(1)} %pad_maximum_fusion.1), channel_id=1, source_target_pairs={{0,4},{1,5},{2,6},{3,7},{4,0},{5,1},{6,2},{7,3},{8,12},{9,13},{10,... | collective-permute-start | bytes 135176 | tf_op jit(solution)/shard_map/ppermute | solution.py:449
  20.4 2.4 %collective-permute-done.4.refs_1_ = bf16[176,128]{1,0:T(8,128)(2,1)S(1)} collective-permute-done((bf16[176,128]{1,0:T(8,128)(2,1)S(1)}, bf16[176,128]{1,0:T(8,128)(2,1)S(1)}, u32[]{:S(2)}, u32[]{:S(2)}) %collective-permute-start.4) | collective-permute-done | bytes 45088 | tf_op jit(solution)/shard_map/ppermute | solution.py:449
  22.8 0.1 collective-permute-start.5
  22.9 0.0 copy-done.6
  22.9 0.1 copy.9.refs_6_
  23.0 1.1 %collective-permute-done.5.refs_4_ = bf16[256,128]{1,0:T(8,128)(2,1)S(1)} collective-permute-done((bf16[256,128]{1,0:T(8,128)(2,1)S(1)}, bf16[256,128]{1,0:T(8,128)(2,1)S(1)}, u32[]{:S(2)}, u32[]{:S(2)}) %collective-permute-start.5) | collective-permute-done | bytes 65568 | tf_op jit(solution)/shard_map/ppermute | solution.py:449
  24.2 0.0 copy-done.2
  24.2 0.0 copy-done.3
  24.2 0.0 copy-done.4
  24.2 0.0 copy-done.5
  24.2 4.0 %filter.1 = (f32[80,128]{1,0:T(8,128)S(1)}, f32[80,128]{1,0:T(8,128)S(1)}, bf16[8,80,768]{2,1,0:T(8,128)(2,1)S(1)}, bf16[8,80,768]{2,1,0:T(8,128)(2,1)S(1)}) custom-call(s32[4]{0:T(128)S(1)} %copy-done.2, f32[64]{0:T(128)S(1)} %copy-done.4, f32[64]{0:T(128)S(1)} %copy-done.5, bf16[96,128]{1,0:T(8,128)(2,1)S(1)} %slice.15.refs_3_, ...), custom_call_target="tpu_custom_call" | custom-call | tf_op jit(solution)/shard_map/filter/pallas_call | solution.py:583
  28.2 0.0 collective-permute-done.6.refs_5_
  28.2 0.0 collective-permute-done.7.refs_6_
  28.2 2.1 %analysis.1 = bf16[8,640,128]{2,1,0:T(8,128)(2,1)} custom-call(f32[80,128]{1,0:T(8,128)S(1)} %get-tuple-element.45.refs_0_, f32[80,128]{1,0:T(8,128)S(1)} %get-tuple-element.46.refs_1_, bf16[8,80,768]{2,1,0:T(8,128)(2,1)S(1)} %get-tuple-element.47.refs_2_, bf16[8,80,768]{2,1,0:T(8,128)(2,1)S(1)} %get-tuple-element.48.refs_3_, f32[64,128]{1,0:T(8,128)S(1)} %bitcast.15, ...), custom_call_target="tpu_custom_call" | custom-call | tf_op jit(solution)/shard_map/analysis/pallas_call | solution.py:595
  (10 shorter events, 0.1 us)
Async XLA Ops:
  0.0 3.1 %copy-start = (bf16[2,4,80,8,128]{4,3,2,1,0:T(8,128)(2,1)S(1)}, bf16[2,4,80,8,128]{4,3,2,1,0:T(8,128)(2,1)}, u32[]{:S(2)}) copy-start(bf16[2,4,80,8,128]{4,3,2,1,0:T(8,128)(2,1)} %param.8) | copy-start | bytes 3932164
  0.0 6.9 %copy-start.1 = (f32[2,4,8,128]{3,2,1,0:T(8,128)S(1)}, f32[2,4,8,128]{3,2,1,0:T(8,128)}, u32[]{:S(2)}) copy-start(f32[2,4,8,128]{3,2,1,0:T(8,128)} %param.9) | copy-start | bytes 98308
  2.5 1.4 %collective-permute-start = (bf16[176,128]{1,0:T(8,128)(2,1)S(1)}, bf16[176,128]{1,0:T(8,128)(2,1)S(1)}, u32[]{:S(2)}, u32[]{:S(2)}) collective-permute-start(bf16[176,128]{1,0:T(8,128)(2,1)S(1)} %observe.1.full_ref), channel_id=1, source_target_pairs={{0,1},{1,0},{2,3},{3,2},{4,5},{5,4},{6,7},{7,6},{8,9},{9,8},{10,11... | collective-permute-start | bytes 135176 | tf_op jit(solution)/shard_map/ppermute | solution.py:449
  4.0 4.7 %collective-permute-start.1 = (bf16[96,128]{1,0:T(8,128)(2,1)S(1)}, bf16[96,128]{1,0:T(8,128)(2,1)S(1)}, u32[]{:S(2)}, u32[]{:S(2)}) collective-permute-start(bf16[96,128]{1,0:T(8,128)(2,1)S(1)} %half.1), channel_id=1, source_target_pairs={{0,8},{8,0},{16,24},{24,16},{1,9},{9,1},{17,25},{25,17},{2,10},{10... | collective-permute-start | bytes 73736 | tf_op jit(solution)/shard_map/ppermute | solution.py:449
  8.7 3.9 %collective-permute-start.2 = (bf16[96,128]{1,0:T(8,128)(2,1)S(1)}, bf16[96,128]{1,0:T(8,128)(2,1)S(1)}, u32[]{:S(2)}, u32[]{:S(2)}) collective-permute-start(bf16[96,128]{1,0:T(8,128)(2,1)S(1)} %add.9), channel_id=1, source_target_pairs={{0,16},{8,24},{16,0},{24,8},{1,17},{9,25},{17,1},{25,9},{2,18},{10... | collective-permute-start | bytes 73736 | tf_op jit(solution)/shard_map/ppermute | solution.py:449
  11.4 11.5 %copy-start.6 = (s32[64,2]{0,1:T(2,128)S(1)}, s32[64,2]{0,1:T(2,128)}, u32[]{:S(2)}) copy-start(s32[64,2]{0,1:T(2,128)} %param.14) | copy-start | bytes 1540
  11.5 12.7 %copy-start.2 = (s32[4]{0:T(128)S(1)}, s32[4]{0:T(128)}, u32[]{:S(2)}) copy-start(s32[4]{0:T(128)} %refs_0_.1) | copy-start | bytes 52
  11.5 12.7 %copy-start.3 = (s32[64]{0:T(128)S(1)}, s32[64]{0:T(128)}, u32[]{:S(2)}) copy-start(s32[64]{0:T(128)} %param.10) | copy-start | bytes 772
  11.5 12.7 %copy-start.4 = (f32[64]{0:T(128)S(1)}, f32[64]{0:T(128)}, u32[]{:S(2)}) copy-start(f32[64]{0:T(128)} %refs_1_.1) | copy-start | bytes 772
  11.5 12.7 %copy-start.5 = (f32[64]{0:T(128)S(1)}, f32[64]{0:T(128)}, u32[]{:S(2)}) copy-start(f32[64]{0:T(128)} %refs_2_.1) | copy-start | bytes 772
  12.6 5.1 %collective-permute-start.3 = (bf16[176,128]{1,0:T(8,128)(2,1)S(1)}, bf16[176,128]{1,0:T(8,128)(2,1)S(1)}, u32[]{:S(2)}, u32[]{:S(2)}) collective-permute-start(bf16[176,128]{1,0:T(8,128)(2,1)S(1)} %pad_maximum_fusion), channel_id=1, source_target_pairs={{0,2},{1,3},{2,0},{3,1},{4,6},{5,7},{6,4},{7,5},{8,10},{9,11},{10,... | collective-permute-start | bytes 135176 | tf_op jit(solution)/shard_map/ppermute | solution.py:449
  14.8 13.4 %collective-permute-start.6 = (bf16[8,80,128]{2,1,0:T(8,128)(2,1)S(1)}, bf16[8,80,128]{2,1,0:T(8,128)(2,1)S(1)}, u32[]{:S(2)}, u32[]{:S(2)}) collective-permute-start(bf16[8,80,128]{2,1,0:T(8,128)(2,1)S(1)} %edge_rows.2), channel_id=1, source_target_pairs={{0,8},{8,0},{16,24},{24,16},{1,9},{9,1},{17,25},{25,17},{2,10},{10... | collective-permute-start | bytes 491528 | tf_op jit(solution)/shard_map/ppermute | solution.py:449
  16.3 11.9 %collective-permute-start.7 = (bf16[8,80,128]{2,1,0:T(8,128)(2,1)S(1)}, bf16[8,80,128]{2,1,0:T(8,128)(2,1)S(1)}, u32[]{:S(2)}, u32[]{:S(2)}) collective-permute-start(bf16[8,80,128]{2,1,0:T(8,128)(2,1)S(1)} %edge_rows.3), channel_id=1, source_target_pairs={{8,16},{16,8},{24,0},{0,24},{9,17},{17,9},{25,1},{1,25},{10,18},{1... | collective-permute-start | bytes 491528 | tf_op jit(solution)/shard_map/ppermute | solution.py:454
  17.8 5.0 %collective-permute-start.4 = (bf16[176,128]{1,0:T(8,128)(2,1)S(1)}, bf16[176,128]{1,0:T(8,128)(2,1)S(1)}, u32[]{:S(2)}, u32[]{:S(2)}) collective-permute-start(bf16[176,128]{1,0:T(8,128)(2,1)S(1)} %pad_maximum_fusion.1), channel_id=1, source_target_pairs={{0,4},{1,5},{2,6},{3,7},{4,0},{5,1},{6,2},{7,3},{8,12},{9,13},{10,... | collective-permute-start | bytes 135176 | tf_op jit(solution)/shard_map/ppermute | solution.py:449
  22.8 1.3 %collective-permute-start.5 = (bf16[256,128]{1,0:T(8,128)(2,1)S(1)}, bf16[256,128]{1,0:T(8,128)(2,1)S(1)}, u32[]{:S(2)}, u32[]{:S(2)}) collective-permute-start(bf16[256,128]{1,0:T(8,128)(2,1)S(1)} %join.1), channel_id=1, source_target_pairs={{0,1},{1,0},{2,3},{3,2},{4,5},{5,4},{6,7},{7,6},{8,9},{9,8},{10,11... | collective-permute-start | bytes 196616 | tf_op jit(solution)/shard_map/ppermute | solution.py:449

commit v4 on v3

--- a/solution.py
+++ b/solution.py
@@ -52,11 +52,9 @@
     for copy in small:
         copy.start()
     pieces = x_sem.shape[0]
-    piece = depth // pieces
+    share = planes // pieces
     large = [
-        pltpu.make_async_copy(
-            x_hbm.at[:, i * piece : (i + 1) * piece, :], x_ref.at[:, i * piece : (i + 1) * piece, :], x_sem.at[i]
-        )
+        pltpu.make_async_copy(x_hbm.at[i * share : (i + 1) * share], x_ref.at[i * share : (i + 1) * share], x_sem.at[i])
         for i in range(pieces)
     ]
     for copy in large:
@@ -117,10 +115,13 @@
     at = jnp.concatenate([jnp.where(c < 0, -1, plane * cols + c)[:1] for c in (col0, col1)], axis=1)
     picks = (iota((planes * cols, 2 * LANES), 0) == at).astype(F32).astype(BF16)
     weights = jnp.concatenate([half0, half1], axis=1)
-    for copy in large:
-        copy.wait()
-    block = jnp.concatenate([x_ref[p] for p in range(planes)], axis=1)
-    values = jnp.dot(block, picks, preferred_element_type=F32).reshape(members, rows, 2 * LANES)
+    values = None
+    for i in range(pieces):
+        large[i].wait()
+        block = jnp.concatenate([x_ref[p] for p in range(i * share, (i + 1) * share)], axis=1)
+        part = jnp.dot(block, picks[i * share * cols : (i + 1) * share * cols], preferred_element_type=F32)
+        values = part if values is None else values + part
+    values = values.reshape(members, rows, 2 * LANES)
     both = jnp.sum(values * weights[None], axis=1)
     low, high = both[:, :LANES], both[:, LANES:]
     lane_m = iota((members, LANES), 1)
@@ -417,9 +418,14 @@
     lat_even = lax.rem(my_lat, 2) == 0
     has_south, has_north = (my_lat > 0).astype(F32), (my_lat < n_lat - 1).astype(F32)
 
-    transform = transform_ref[:, :members]
-    hi = transform.astype(BF16)
-    lo = (transform - hi.astype(F32)).astype(BF16)
+    transform = transform_ref[...]
+    hi = transform.astype(BF16).astype(F32)
+    lo = transform - hi
+    lane = iota((members, LANES), 1)
+    spill = 2 * members - LANES
+    left = jnp.where(lane < members, hi, pltpu.roll(lo, members, 1))
+    right = jnp.where(lane < spill, pltpu.roll(lo, members, 1), pltpu.roll(hi, spill, 1))
+    terms = jnp.concatenate([left, right], axis=1).astype(BF16)[:, : 3 * members]
     for p in range(planes):
         first, inner = next((a, ref) for (a, z), ref in zip(parts, inner_refs, strict=True) if a <= p < z)
         _, _, south, north = winds_of(courant_ref, levels, p)
@@ -434,9 +440,8 @@
             split_store(f, edge_hi_ref, edge_lo_ref, p, 0 if r == 0 else cols)
     for p in range(planes):
         for h_ref, l_ref, which in ((hi_ref, lo_ref, range(1, rows - 1)), (edge_hi_ref, edge_lo_ref, (0, rows - 1))):
-            result = jnp.dot(hi, h_ref[p], preferred_element_type=F32)
-            result = result + jnp.dot(lo, h_ref[p], preferred_element_type=F32)
-            result = result + jnp.dot(hi, l_ref[p], preferred_element_type=F32)
+            stacked = jnp.concatenate([h_ref[p], h_ref[p], l_ref[p]], axis=0)
+            result = jnp.dot(terms, stacked, preferred_element_type=F32)
             for i, r in enumerate(which):
                 wide_ref[p % 2, pl.ds(r, members, stride=rows), :] = result[:, i * cols : (i + 1) * cols]
         out_ref[p] = wide_ref[p % 2].astype(BF16)
@@ -476,7 +481,7 @@
             pltpu.VMEM(tile.shape, jnp.int32),
             pltpu.VMEM(site.shape, jnp.int32),
             pltpu.SMEM(batch_order.shape, jnp.int32),
-            pltpu.SemaphoreType.DMA((5,)),
+            pltpu.SemaphoreType.DMA((1,)),
             pltpu.SemaphoreType.DMA((4,)),
         ],
         compiler_params=PARAMS,

time: 30.4 us -> 29.8 us (0.980)
  Pallas kernels: 11.5 us -> 10.9 us
    pallas_call x1, Pallas kernels: 2.54 us -> 2.22 us  [per_device(): pl.pallas_call(functools.partial(observe_kernel, n_lon, levels), out_shap...]
where the time goes in v4:
time: 29.8 us; the launch traced here: 29.7 us
  starting transfers between devices  13.4 us (45%)
  Pallas kernels  10.9 us (37%)
  waiting for transfers between devices  5.06 us (17%)
    ppermute x7, starting transfers between devices, exchanged(): lax.ppermute(x, axis, [(i, i ^ step) for i in range(lax.axis_size(axis))])  11.9 us
    ppermute x7, waiting for transfers between devices, exchanged(): lax.ppermute(x, axis, [(i, i ^ step) for i in range(lax.axis_size(axis))])  5.06 us
    pallas_call x1, Pallas kernels, per_device(): pl.pallas_call(functools.partial(filter_kernel, n_lon, levels, parts), ou...  3.99 us
    pallas_call x7, Pallas kernels, local(): pl.pallas_call(kernel, out_shape=out, in_specs=[VMEM] * len(operands), ou...  2.86 us
    pallas_call x1, Pallas kernels, per_device(): pl.pallas_call(functools.partial(observe_kernel, n_lon, levels), out_shap...  2.22 us
    pallas_call x1, Pallas kernels, per_device(): pl.pallas_call(functools.partial(analysis_kernel, n_lat, levels, parts),...  1.82 us
    ppermute x1, starting transfers between devices, exchanged_odd(): lax.ppermute(x, axis, [pair for i in range(1, count, 2) for pair in ((i,...  1.49 us
  transfers between devices with their start and end apart: 8, of which 5 were waited for; matrix products, arithmetic and copies ran while one was open for 0% of the time, Pallas kernels for 23%

profile of v4, /device:TPU:0, one launch (start us, length us, event | category | flops | bytes accessed | tf_op | source)
XLA Modules:
  0.0 29.7 jit_solution(5346851997084377249)
XLA Ops:
  0.0 0.0 copy-start
  0.0 0.0 copy-start.1
  0.0 2.2 %observe.1.full_ref = bf16[176,128]{1,0:T(8,128)(2,1)S(1)} custom-call(bf16[8,640,128]{2,1,0:T(8,128)(2,1)} %bitcast.5, f32[64,128]{1,0:T(8,128)} %bitcast.11, s32[1,64]{1,0:T(1,128)} %bitcast.16, s32[1,64]{1,0:T(1,128)} %bitcast.18, s32[4]{0:T(128)} %refs_0_.1), custom_call_target="tpu_custom_call" | custom-call | tf_op jit(solution)/shard_map/observe/pallas_call | solution.py:473
  2.2 0.5 %collective-permute-start = (bf16[176,128]{1,0:T(8,128)(2,1)S(1)}, bf16[176,128]{1,0:T(8,128)(2,1)S(1)}, u32[]{:S(2)}, u32[]{:S(2)}) collective-permute-start(bf16[176,128]{1,0:T(8,128)(2,1)S(1)} %observe.1.full_ref), channel_id=1, source_target_pairs={{0,1},{1,0},{2,3},{3,2},{4,5},{5,4},{6,7},{7,6},{8,9},{9,8},{10,11... | collective-permute-start | bytes 135176 | tf_op jit(solution)/shard_map/ppermute | solution.py:454
  2.8 0.0 copy-done
  2.8 0.7 %edge_columns.1.refs_2_ = bf16[80,128]{1,0:T(8,128)(2,1)S(1)} custom-call(bf16[8,640,128]{2,1,0:T(8,128)(2,1)S(1)} %bitcast.6), custom_call_target="tpu_custom_call" | custom-call | tf_op jit(solution)/shard_map/edge_columns/pallas_call | solution.py:493
  3.4 0.2 collective-permute-done.other_ref
  3.7 2.9 %collective-permute-start.1 = (bf16[96,128]{1,0:T(8,128)(2,1)S(1)}, bf16[96,128]{1,0:T(8,128)(2,1)S(1)}, u32[]{:S(2)}, u32[]{:S(2)}) collective-permute-start(bf16[96,128]{1,0:T(8,128)(2,1)S(1)} %half.1), channel_id=1, source_target_pairs={{0,8},{8,0},{16,24},{24,16},{1,9},{9,1},{17,25},{25,17},{2,10},{10... | collective-permute-start | bytes 73736 | tf_op jit(solution)/shard_map/ppermute | solution.py:454
  6.6 0.0 copy-done.1
  6.6 0.9 %inner.2.refs_8_.refs_7_ = f32[5,8,80,128]{3,2,1,0:T(8,128)S(1)} custom-call(bf16[8,640,128]{2,1,0:T(8,128)(2,1)S(1)} %bitcast.7, f32[64,128]{1,0:T(8,128)S(1)} %bitcast.12), custom_call_target="tpu_custom_call" | custom-call | tf_op jit(solution)/shard_map/inner/pallas_call | solution.py:493
  7.5 0.9 %collective-permute-done.1 = bf16[96,128]{1,0:T(8,128)(2,1)S(1)} collective-permute-done((bf16[96,128]{1,0:T(8,128)(2,1)S(1)}, bf16[96,128]{1,0:T(8,128)(2,1)S(1)}, u32[]{:S(2)}, u32[]{:S(2)}) %collective-permute-start.1) | collective-permute-done | bytes 24608 | tf_op jit(solution)/shard_map/ppermute | solution.py:454
  8.4 2.1 %collective-permute-start.2 = (bf16[96,128]{1,0:T(8,128)(2,1)S(1)}, bf16[96,128]{1,0:T(8,128)(2,1)S(1)}, u32[]{:S(2)}, u32[]{:S(2)}) collective-permute-start(bf16[96,128]{1,0:T(8,128)(2,1)S(1)} %add.9), channel_id=1, source_target_pairs={{0,16},{8,24},{16,0},{24,8},{1,17},{9,25},{17,1},{25,9},{2,18},{10... | collective-permute-start | bytes 73736 | tf_op jit(solution)/shard_map/ppermute | solution.py:454
  10.5 0.3 %edge_rows.3 = bf16[8,80,128]{2,1,0:T(8,128)(2,1)S(1)} custom-call(bf16[8,640,128]{2,1,0:T(8,128)(2,1)S(1)} %bitcast.8), custom_call_target="tpu_custom_call" | custom-call | tf_op jit(solution)/shard_map/edge_rows/pallas_call | solution.py:493
  10.8 0.3 %edge_rows.2 = bf16[8,80,128]{2,1,0:T(8,128)(2,1)S(1)} custom-call(bf16[8,640,128]{2,1,0:T(8,128)(2,1)S(1)} %bitcast.9), custom_call_target="tpu_custom_call" | custom-call | tf_op jit(solution)/shard_map/edge_rows/pallas_call | solution.py:493
  11.1 0.0 copy-start.6
  11.1 0.0 copy-start.2
  11.2 0.0 copy-start.3
  11.2 0.0 copy-start.4
  11.2 0.0 copy-start.5
  11.2 0.6 %inner.3.refs_9_.refs_8_ = f32[3,8,80,128]{3,2,1,0:T(8,128)S(1)} custom-call(bf16[8,640,128]{2,1,0:T(8,128)(2,1)S(1)} %bitcast.10, f32[64,128]{1,0:T(8,128)S(1)} %bitcast.13), custom_call_target="tpu_custom_call" | custom-call | tf_op jit(solution)/shard_map/inner/pallas_call | solution.py:493
  11.8 0.5 %collective-permute-done.2 = bf16[96,128]{1,0:T(8,128)(2,1)S(1)} collective-permute-done((bf16[96,128]{1,0:T(8,128)(2,1)S(1)}, bf16[96,128]{1,0:T(8,128)(2,1)S(1)}, u32[]{:S(2)}, u32[]{:S(2)}) %collective-permute-start.2) | collective-permute-done | bytes 24608 | tf_op jit(solution)/shard_map/ppermute | solution.py:454
  12.3 2.1 %collective-permute-start.3 = (bf16[176,128]{1,0:T(8,128)(2,1)S(1)}, bf16[176,128]{1,0:T(8,128)(2,1)S(1)}, u32[]{:S(2)}, u32[]{:S(2)}) collective-permute-start(bf16[176,128]{1,0:T(8,128)(2,1)S(1)} %pad_maximum_fusion), channel_id=1, source_target_pairs={{0,2},{1,3},{2,0},{3,1},{4,6},{5,7},{6,4},{7,5},{8,10},{9,11},{10,... | collective-permute-start | bytes 135176 | tf_op jit(solution)/shard_map/ppermute | solution.py:454
  14.5 1.5 %collective-permute-start.6 = (bf16[8,80,128]{2,1,0:T(8,128)(2,1)S(1)}, bf16[8,80,128]{2,1,0:T(8,128)(2,1)S(1)}, u32[]{:S(2)}, u32[]{:S(2)}) collective-permute-start(bf16[8,80,128]{2,1,0:T(8,128)(2,1)S(1)} %edge_rows.2), channel_id=1, source_target_pairs={{0,8},{8,0},{16,24},{24,16},{1,9},{9,1},{17,25},{25,17},{2,10},{10... | collective-permute-start | bytes 491528 | tf_op jit(solution)/shard_map/ppermute | solution.py:454
  16.0 1.5 %collective-permute-start.7 = (bf16[8,80,128]{2,1,0:T(8,128)(2,1)S(1)}, bf16[8,80,128]{2,1,0:T(8,128)(2,1)S(1)}, u32[]{:S(2)}, u32[]{:S(2)}) collective-permute-start(bf16[8,80,128]{2,1,0:T(8,128)(2,1)S(1)} %edge_rows.3), channel_id=1, source_target_pairs={{8,16},{16,8},{24,0},{0,24},{9,17},{17,9},{25,1},{1,25},{10,18},{1... | collective-permute-start | bytes 491528 | tf_op jit(solution)/shard_map/ppermute | solution.py:459
  17.4 0.0 collective-permute-done.3
  17.5 2.7 %collective-permute-start.4 = (bf16[176,128]{1,0:T(8,128)(2,1)S(1)}, bf16[176,128]{1,0:T(8,128)(2,1)S(1)}, u32[]{:S(2)}, u32[]{:S(2)}) collective-permute-start(bf16[176,128]{1,0:T(8,128)(2,1)S(1)} %pad_maximum_fusion.1), channel_id=1, source_target_pairs={{0,4},{1,5},{2,6},{3,7},{4,0},{5,1},{6,2},{7,3},{8,12},{9,13},{10,... | collective-permute-start | bytes 135176 | tf_op jit(solution)/shard_map/ppermute | solution.py:454
  20.1 2.4 %collective-permute-done.4.refs_1_ = bf16[176,128]{1,0:T(8,128)(2,1)S(1)} collective-permute-done((bf16[176,128]{1,0:T(8,128)(2,1)S(1)}, bf16[176,128]{1,0:T(8,128)(2,1)S(1)}, u32[]{:S(2)}, u32[]{:S(2)}) %collective-permute-start.4) | collective-permute-done | bytes 45088 | tf_op jit(solution)/shard_map/ppermute | solution.py:454
  22.5 0.1 collective-permute-start.5
  22.6 0.0 copy-done.6
  22.6 0.1 copy.9.refs_6_
  22.7 1.1 %collective-permute-done.5.refs_4_ = bf16[256,128]{1,0:T(8,128)(2,1)S(1)} collective-permute-done((bf16[256,128]{1,0:T(8,128)(2,1)S(1)}, bf16[256,128]{1,0:T(8,128)(2,1)S(1)}, u32[]{:S(2)}, u32[]{:S(2)}) %collective-permute-start.5) | collective-permute-done | bytes 65568 | tf_op jit(solution)/shard_map/ppermute | solution.py:454
  23.8 0.0 copy-done.2
  23.8 0.0 copy-done.3
  23.8 0.0 copy-done.4
  23.8 0.0 copy-done.5
  23.9 4.0 %filter.1 = (f32[80,128]{1,0:T(8,128)S(1)}, f32[80,128]{1,0:T(8,128)S(1)}, bf16[8,80,768]{2,1,0:T(8,128)(2,1)S(1)}, bf16[8,80,768]{2,1,0:T(8,128)(2,1)S(1)}) custom-call(s32[4]{0:T(128)S(1)} %copy-done.2, f32[64]{0:T(128)S(1)} %copy-done.4, f32[64]{0:T(128)S(1)} %copy-done.5, bf16[96,128]{1,0:T(8,128)(2,1)S(1)} %slice.15.refs_3_, ...), custom_call_target="tpu_custom_call" | custom-call | tf_op jit(solution)/shard_map/filter/pallas_call | solution.py:588
  27.9 0.0 collective-permute-done.6.refs_5_
  27.9 0.0 collective-permute-done.7.refs_6_
  27.9 1.8 %analysis.1 = bf16[8,640,128]{2,1,0:T(8,128)(2,1)} custom-call(f32[80,128]{1,0:T(8,128)S(1)} %get-tuple-element.45.refs_0_, f32[80,128]{1,0:T(8,128)S(1)} %get-tuple-element.46.refs_1_, bf16[8,80,768]{2,1,0:T(8,128)(2,1)S(1)} %get-tuple-element.47.refs_2_, bf16[8,80,768]{2,1,0:T(8,128)(2,1)S(1)} %get-tuple-element.48.refs_3_, f32[64,128]{1,0:T(8,128)S(1)} %bitcast.15, ...), custom_call_target="tpu_custom_call" | custom-call | tf_op jit(solution)/shard_map/analysis/pallas_call | solution.py:600
  (10 shorter events, 0.1 us)
Async XLA Ops:
  0.0 2.8 %copy-start = (bf16[2,4,80,8,128]{4,3,2,1,0:T(8,128)(2,1)S(1)}, bf16[2,4,80,8,128]{4,3,2,1,0:T(8,128)(2,1)}, u32[]{:S(2)}) copy-start(bf16[2,4,80,8,128]{4,3,2,1,0:T(8,128)(2,1)} %param.8) | copy-start | bytes 3932164
  0.0 6.6 %copy-start.1 = (f32[2,4,8,128]{3,2,1,0:T(8,128)S(1)}, f32[2,4,8,128]{3,2,1,0:T(8,128)}, u32[]{:S(2)}) copy-start(f32[2,4,8,128]{3,2,1,0:T(8,128)} %param.9) | copy-start | bytes 98308
  2.2 1.4 %collective-permute-start = (bf16[176,128]{1,0:T(8,128)(2,1)S(1)}, bf16[176,128]{1,0:T(8,128)(2,1)S(1)}, u32[]{:S(2)}, u32[]{:S(2)}) collective-permute-start(bf16[176,128]{1,0:T(8,128)(2,1)S(1)} %observe.1.full_ref), channel_id=1, source_target_pairs={{0,1},{1,0},{2,3},{3,2},{4,5},{5,4},{6,7},{7,6},{8,9},{9,8},{10,11... | collective-permute-start | bytes 135176 | tf_op jit(solution)/shard_map/ppermute | solution.py:454
  3.7 4.7 %collective-permute-start.1 = (bf16[96,128]{1,0:T(8,128)(2,1)S(1)}, bf16[96,128]{1,0:T(8,128)(2,1)S(1)}, u32[]{:S(2)}, u32[]{:S(2)}) collective-permute-start(bf16[96,128]{1,0:T(8,128)(2,1)S(1)} %half.1), channel_id=1, source_target_pairs={{0,8},{8,0},{16,24},{24,16},{1,9},{9,1},{17,25},{25,17},{2,10},{10... | collective-permute-start | bytes 73736 | tf_op jit(solution)/shard_map/ppermute | solution.py:454
  8.4 3.9 %collective-permute-start.2 = (bf16[96,128]{1,0:T(8,128)(2,1)S(1)}, bf16[96,128]{1,0:T(8,128)(2,1)S(1)}, u32[]{:S(2)}, u32[]{:S(2)}) collective-permute-start(bf16[96,128]{1,0:T(8,128)(2,1)S(1)} %add.9), channel_id=1, source_target_pairs={{0,16},{8,24},{16,0},{24,8},{1,17},{9,25},{17,1},{25,9},{2,18},{10... | collective-permute-start | bytes 73736 | tf_op jit(solution)/shard_map/ppermute | solution.py:454
  11.1 11.5 %copy-start.6 = (s32[64,2]{0,1:T(2,128)S(1)}, s32[64,2]{0,1:T(2,128)}, u32[]{:S(2)}) copy-start(s32[64,2]{0,1:T(2,128)} %param.14) | copy-start | bytes 1540
  11.1 12.7 %copy-start.2 = (s32[4]{0:T(128)S(1)}, s32[4]{0:T(128)}, u32[]{:S(2)}) copy-start(s32[4]{0:T(128)} %refs_0_.1) | copy-start | bytes 52
  11.2 12.7 %copy-start.3 = (s32[64]{0:T(128)S(1)}, s32[64]{0:T(128)}, u32[]{:S(2)}) copy-start(s32[64]{0:T(128)} %param.10) | copy-start | bytes 772
  11.2 12.7 %copy-start.4 = (f32[64]{0:T(128)S(1)}, f32[64]{0:T(128)}, u32[]{:S(2)}) copy-start(f32[64]{0:T(128)} %refs_1_.1) | copy-start | bytes 772
  11.2 12.7 %copy-start.5 = (f32[64]{0:T(128)S(1)}, f32[64]{0:T(128)}, u32[]{:S(2)}) copy-start(f32[64]{0:T(128)} %refs_2_.1) | copy-start | bytes 772
  12.3 5.1 %collective-permute-start.3 = (bf16[176,128]{1,0:T(8,128)(2,1)S(1)}, bf16[176,128]{1,0:T(8,128)(2,1)S(1)}, u32[]{:S(2)}, u32[]{:S(2)}) collective-permute-start(bf16[176,128]{1,0:T(8,128)(2,1)S(1)} %pad_maximum_fusion), channel_id=1, source_target_pairs={{0,2},{1,3},{2,0},{3,1},{4,6},{5,7},{6,4},{7,5},{8,10},{9,11},{10,... | collective-permute-start | bytes 135176 | tf_op jit(solution)/shard_map/ppermute | solution.py:454
  14.5 13.4 %collective-permute-start.6 = (bf16[8,80,128]{2,1,0:T(8,128)(2,1)S(1)}, bf16[8,80,128]{2,1,0:T(8,128)(2,1)S(1)}, u32[]{:S(2)}, u32[]{:S(2)}) collective-permute-start(bf16[8,80,128]{2,1,0:T(8,128)(2,1)S(1)} %edge_rows.2), channel_id=1, source_target_pairs={{0,8},{8,0},{16,24},{24,16},{1,9},{9,1},{17,25},{25,17},{2,10},{10... | collective-permute-start | bytes 491528 | tf_op jit(solution)/shard_map/ppermute | solution.py:454
  16.0 11.9 %collective-permute-start.7 = (bf16[8,80,128]{2,1,0:T(8,128)(2,1)S(1)}, bf16[8,80,128]{2,1,0:T(8,128)(2,1)S(1)}, u32[]{:S(2)}, u32[]{:S(2)}) collective-permute-start(bf16[8,80,128]{2,1,0:T(8,128)(2,1)S(1)} %edge_rows.3), channel_id=1, source_target_pairs={{8,16},{16,8},{24,0},{0,24},{9,17},{17,9},{25,1},{1,25},{10,18},{1... | collective-permute-start | bytes 491528 | tf_op jit(solution)/shard_map/ppermute | solution.py:459
  17.5 5.0 %collective-permute-start.4 = (bf16[176,128]{1,0:T(8,128)(2,1)S(1)}, bf16[176,128]{1,0:T(8,128)(2,1)S(1)}, u32[]{:S(2)}, u32[]{:S(2)}) collective-permute-start(bf16[176,128]{1,0:T(8,128)(2,1)S(1)} %pad_maximum_fusion.1), channel_id=1, source_target_pairs={{0,4},{1,5},{2,6},{3,7},{4,0},{5,1},{6,2},{7,3},{8,12},{9,13},{10,... | collective-permute-start | bytes 135176 | tf_op jit(solution)/shard_map/ppermute | solution.py:454
  22.5 1.3 %collective-permute-start.5 = (bf16[256,128]{1,0:T(8,128)(2,1)S(1)}, bf16[256,128]{1,0:T(8,128)(2,1)S(1)}, u32[]{:S(2)}, u32[]{:S(2)}) collective-permute-start(bf16[256,128]{1,0:T(8,128)(2,1)S(1)} %join.1), channel_id=1, source_target_pairs={{0,1},{1,0},{2,3},{3,2},{4,5},{5,4},{6,7},{7,6},{8,9},{9,8},{10,11... | collective-permute-start | bytes 196616 | tf_op jit(solution)/shard_map/ppermute | solution.py:454

commit v5 on v4

--- a/solution.py
+++ b/solution.py
@@ -10,7 +10,7 @@
 EPSILON = 1e-05
 HIGHEST = lax.Precision.HIGHEST
 LANES = 128
-PLAN = {"filter": 0, "columns": 0, "pair": 2, "odd": 2, "inner": {1: [(0, 5)], 2: [(5, 8)]}, "settle": {0: ["column"], 2: ["pair_rows", "odd_rows"]}}
+PLAN = {"filter": 1000000000, "columns": 0, "pieces": (1, 1), "pair": 2, "pair_send": 2, "odd": 2, "odd_send": 4, "inner": {1: [(0, 5)], 2: [(5, 8)]}, "settle": {0: ["column"], 2: ["pair_rows", "odd_rows"], 3: ["odd_rows"], 4: ["pair"]}}
 SUBLANES = 8
 F32 = jnp.float32
 BF16 = jnp.bfloat16
@@ -145,17 +145,30 @@
     ref[start : start + values.shape[0], :] = both.astype(BF16)
 
 
-def edge_rows_kernel(rows, facing, x_ref, row_ref, wide_ref):
+def edge_rows_kernel(rows, facing, x_ref, *refs):
     planes, depth, cols = x_ref.shape
     members = depth // rows
     upper = lax.rem(lax.axis_index("lat"), 2) == (0 if facing else 1)
     row = jnp.where(upper, rows - 1, 0)
+    *row_refs, wide_ref = refs
+    share = planes // len(row_refs)
     for p in range(planes):
         wide_ref[p] = x_ref[p].astype(F32)
-        row_ref[p] = wide_ref[p, pl.ds(row, members, stride=rows), :].astype(BF16)
-
-
-def edge_columns_kernel(rows, x_ref, column_ref, wide_ref):
+        row_refs[p // share][p % share] = wide_ref[p, pl.ds(row, members, stride=rows), :].astype(BF16)
+
+
+def folded(values, size):
+    half = values.shape[0] // 2
+    odd = iota((half, LANES), 1) % 2 == 1
+    both = jnp.where(odd, values[:half], pltpu.roll(values[half:], LANES - 1, 1))
+    return jnp.concatenate([both, jnp.zeros((size - half, LANES), F32)], axis=0)
+
+
+def unfolded(values):
+    return jnp.concatenate([values, pltpu.roll(values, 1, 1)], axis=0)
+
+
+def edge_columns_kernel(rows, x_ref, near_ref, far_ref, wide_ref):
     planes, depth, cols = x_ref.shape
     members = depth // rows
     lane = iota((members, LANES), 1)
@@ -166,8 +179,11 @@
             n = p * rows + r
             cell = wide_ref[p, pl.ds(r, members, stride=rows), :]
             total = jnp.where(lane // 2 == n, pltpu.roll(cell, 2 * n + 1, 1) if 2 * n + 1 < LANES else cell, total)
-    total = jnp.where(lane % 2 == 0, pltpu.roll(total, LANES - 1, 1), pltpu.roll(total, 1, 1))
-    column_ref[...] = total.astype(BF16)
+    last = pltpu.roll(total, 1, 1)
+    even = lax.rem(lax.axis_index("lon"), 2) == 0
+    size = near_ref.shape[0]
+    near_ref[...] = folded(jnp.where(even, last, total), size).astype(BF16)
+    far_ref[...] = folded(jnp.where(even, total, last), size).astype(BF16)
 
 
 def winds_of(courant_ref, levels, p):
@@ -265,9 +281,12 @@
 
     my_lat, my_lon = lax.axis_index("lat"), lax.axis_index("lon")
     lon_even = lax.rem(my_lon, 2) == 0
-    near = join_ref[size : size + members, :].astype(F32)
-    far = join_ref[size + members :, :].astype(F32)
-    halo_ref[...] = jnp.where((iota((members, LANES), 1) % 2 == 0) == lon_even, near, far)
+    block = (join_ref.shape[0] - size) // 2
+    near, far = (
+        unfolded(join_ref[start : start + block, :].astype(F32)[: members // 2]) for start in (size, size + block)
+    )
+    west, east = jnp.where(lon_even, far, near), jnp.where(lon_even, near, far)
+    halo_ref[...] = jnp.where(iota((members, LANES), 1) % 2 == 1, west, pltpu.roll(east, LANES - 1, 1))
 
     def complete(p, r):
         first, inner = next((a, ref) for (a, z), ref in zip(parts, inner_refs, strict=True) if a <= p < z)
@@ -408,8 +427,11 @@
 
 
 def analysis_kernel(n_lat, levels, parts, *refs):
-    transform_ref, halo_ref, hi_ref, lo_ref, courant_ref, pair_ref, odd_ref = refs[:7]
-    inner_refs, refs = refs[7 : 7 + len(parts)], refs[7 + len(parts) :]
+    transform_ref, halo_ref, hi_ref, lo_ref, courant_ref = refs[:5]
+    odd_pieces, pair_pieces = PLAN["pieces"]
+    pair_refs, refs = refs[5 : 5 + pair_pieces], refs[5 + pair_pieces :]
+    odd_refs, refs = refs[:odd_pieces], refs[odd_pieces:]
+    inner_refs, refs = refs[: len(parts)], refs[len(parts) :]
     out_hbm, edge_hi_ref, edge_lo_ref, out_ref, wide_ref, out_sem = refs
     planes, members, width = hi_ref.shape
     rows = courant_ref.shape[0] // (2 * levels)
@@ -429,7 +451,9 @@
     for p in range(planes):
         first, inner = next((a, ref) for (a, z), ref in zip(parts, inner_refs, strict=True) if a <= p < z)
         _, _, south, north = winds_of(courant_ref, levels, p)
-        near, far = pair_ref[p].astype(F32), odd_ref[p].astype(F32)
+        near, far = (
+            one[p // (planes // len(one))][p % (planes // len(one))].astype(F32) for one in (pair_refs, odd_refs)
+        )
         for r in (0, rows - 1):
             n = p * rows + r
             f = inner[p - first, r] + edge_factor(courant_ref, levels, p, r) * pltpu.roll(halo_ref[...], LANES - 1 - 2 * n, 1)
@@ -502,10 +526,11 @@
         )(*operands)
 
     def edge_rows(x, facing):
+        pieces = PLAN["pieces"][facing]
         return local(
             functools.partial(edge_rows_kernel, rows, facing),
             "edge_rows",
-            jax.ShapeDtypeStruct((planes, members, cols), BF16),
+            [jax.ShapeDtypeStruct((planes // pieces, members, cols), BF16)] * pieces,
             [pltpu.VMEM((planes, depth, cols), F32)],
             x,
         )
@@ -529,19 +554,21 @@
 
     def beside(stage, x):
         if stage == PLAN["columns"]:
-            done["column"] = local(
+            done["near"], done["column"] = local(
                 functools.partial(edge_columns_kernel, rows),
                 "edge_columns",
-                jax.ShapeDtypeStruct((members, LANES), BF16),
+                [jax.ShapeDtypeStruct(((members // 2 + 15) // 16 * 16, LANES), BF16)] * 2,
                 [pltpu.VMEM((planes, depth, cols), F32)],
                 x,
             )
-        if stage == PLAN["pair"]:
-            done["pair_rows"] = edge_rows(x, True)
-            done["pair"] = exchanged(done["pair_rows"], "lat", 1)
-        if stage == PLAN["odd"]:
-            done["odd_rows"] = edge_rows(x, False)
-            done["odd"] = exchanged_odd(done["odd_rows"], "lat")
+        for name, facing, send in (
+            ("pair", True, lambda part: exchanged(part, "lat", 1)),
+            ("odd", False, lambda part: exchanged_odd(part, "lat")),
+        ):
+            if stage == PLAN[name]:
+                done[name + "_rows"] = edge_rows(x, facing)
+            if stage == PLAN[name + "_send"]:
+                done[name] = [send(part) for part in done[name + "_rows"]]
         for start, stop in PLAN["inner"].get(stage, ()):
             parts.append((start, stop))
             inners.append(inner(x, start, stop))
@@ -566,6 +593,7 @@
         half, x = settle(stage, half, x)
         stage += 1
     block, blocks = done["column"], []
+    column_rows = block.shape[0]
     for step in lon_steps:
         other = exchanged(jnp.concatenate([half, block], axis=0), "lon", step)
         beside(stage, x)
@@ -575,9 +603,9 @@
             half = half + other[:size]
             half, block, x = settle(stage, half, block, x)
             stage += 1
-    join_type = jax.ShapeDtypeStruct((size + 2 * members, LANES), BF16)
+    join_type = jax.ShapeDtypeStruct((size + 2 * column_rows, LANES), BF16)
     join = local(
-        functools.partial(join_kernel, n_lon, len(blocks)), "join", join_type, [], half, other, done["column"], *blocks
+        functools.partial(join_kernel, n_lon, len(blocks)), "join", join_type, [], half, other, done["near"], *blocks
     )
     join, x = settle(stage, join, x)
     received = exchanged(join, "lon", 1)
@@ -592,7 +620,7 @@
         out_specs=[VMEM] * 4,
         scratch_shapes=[pltpu.VMEM((nobs, LANES), F32)] * 4 + [pltpu.VMEM((4, nobs, LANES), F32), pltpu.VMEM((2, 32, SUBLANES, LANES), F32)],
         compiler_params=PARAMS,
-        cost_estimate=pl.CostEstimate(flops=0, bytes_accessed=PLAN["filter"], transcendentals=0),
+        cost_estimate=pl.CostEstimate(flops=PLAN["filter"], bytes_accessed=0, transcendentals=0),
         name="filter",
     )(batch_order, obs_value, obs_var, join[:size], received, tile, loc_bits, winds, *inners)
 
@@ -600,7 +628,7 @@
     out = pl.pallas_call(
         functools.partial(analysis_kernel, n_lat, levels, parts),
         out_shape=jax.ShapeDtypeStruct((planes, depth, cols), BF16),
-        in_specs=[VMEM] * (7 + len(parts)),
+        in_specs=[VMEM] * (5 + sum(PLAN["pieces"]) + len(parts)),
         out_specs=HBM,
         scratch_shapes=[
             edge_type,
@@ -611,7 +639,7 @@
         ],
         compiler_params=PARAMS,
         name="analysis",
-    )(transform, halo, hi, lo, winds, done["pair"], done["odd"], *inners)
+    )(transform, halo, hi, lo, winds, *done["pair"], *done["odd"], *inners)
     return out.reshape(prior_state.shape)
 
 

time: 29.8 us -> 29.4 us (0.987)
  waiting for transfers between devices: 5.06 us -> 3.1 us
  starting transfers between devices: 13.4 us -> 14.9 us
    ppermute x7, waiting for transfers between devices: 5.06 us -> 3.1 us  [exchanged(): lax.ppermute(x, axis, [(i, i ^ step) for i in range(lax.axis_size(axis))])]
    ppermute x1, starting transfers between devices: 1.49 us -> 2.45 us  [exchanged_odd(): lax.ppermute(x, axis, [pair for i in range(1, count, 2) for pair in ((i,...]
    ppermute x7, starting transfers between devices: 11.9 us -> 12.4 us  [exchanged(): lax.ppermute(x, axis, [(i, i ^ step) for i in range(lax.axis_size(axis))])]
  transfers between devices with their start and end apart: 8 -> 8, of which waited for: 5 -> 5; matrix products, arithmetic and copies ran while one was open for 0% -> 0% of each run, Pallas kernels for 23% -> 24%
where the time goes in v5:
time: 29.4 us; the launch traced here: 29.3 us
  starting transfers between devices  14.9 us (51%)
  Pallas kernels  11 us (37%)
  waiting for transfers between devices  3.1 us (11%)
    ppermute x7, starting transfers between devices, exchanged(): lax.ppermute(x, axis, [(i, i ^ step) for i in range(lax.axis_size(axis))])  12.4 us
    pallas_call x1, Pallas kernels, per_device(): pl.pallas_call(functools.partial(filter_kernel, n_lon, levels, parts), ou...  4.02 us
    ppermute x7, waiting for transfers between devices, exchanged(): lax.ppermute(x, axis, [(i, i ^ step) for i in range(lax.axis_size(axis))])  3.1 us
    pallas_call x7, Pallas kernels, local(): pl.pallas_call(kernel, out_shape=out, in_specs=[VMEM] * len(operands), ou...  2.89 us
    ppermute x1, starting transfers between devices, exchanged_odd(): lax.ppermute(x, axis, [pair for i in range(1, count, 2) for pair in ((i,...  2.45 us
    pallas_call x1, Pallas kernels, per_device(): pl.pallas_call(functools.partial(observe_kernel, n_lon, levels), out_shap...  2.22 us
    pallas_call x1, Pallas kernels, per_device(): pl.pallas_call(functools.partial(analysis_kernel, n_lat, levels, parts),...  1.82 us
  transfers between devices with their start and end apart: 8, of which 5 were waited for; matrix products, arithmetic and copies ran while one was open for 0% of the time, Pallas kernels for 24%

profile of v5, /device:TPU:0, one launch (start us, length us, event | category | flops | bytes accessed | tf_op | source)
XLA Modules:
  0.0 29.3 jit_solution(11595727008363582052)
XLA Ops:
  0.0 0.0 copy-start
  0.0 0.0 copy-start.1
  0.0 2.2 %observe.1.full_ref = bf16[176,128]{1,0:T(8,128)(2,1)S(1)} custom-call(bf16[8,640,128]{2,1,0:T(8,128)(2,1)} %bitcast.5, f32[64,128]{1,0:T(8,128)} %bitcast.11, s32[1,64]{1,0:T(1,128)} %bitcast.16, s32[1,64]{1,0:T(1,128)} %bitcast.18, s32[4]{0:T(128)} %refs_0_.1), custom_call_target="tpu_custom_call" | custom-call | tf_op jit(solution)/shard_map/observe/pallas_call | solution.py:497
  2.2 0.5 %collective-permute-start = (bf16[176,128]{1,0:T(8,128)(2,1)S(1)}, bf16[176,128]{1,0:T(8,128)(2,1)S(1)}, u32[]{:S(2)}, u32[]{:S(2)}) collective-permute-start(bf16[176,128]{1,0:T(8,128)(2,1)S(1)} %observe.1.full_ref), channel_id=1, source_target_pairs={{0,1},{1,0},{2,3},{3,2},{4,5},{5,4},{6,7},{7,6},{8,9},{9,8},{10,11... | collective-permute-start | bytes 135176 | tf_op jit(solution)/shard_map/ppermute | solution.py:478
  2.8 0.0 copy-done
  2.8 0.7 %edge_columns.1 = (bf16[48,128]{1,0:T(8,128)(2,1)S(1)}, bf16[48,128]{1,0:T(8,128)(2,1)S(1)}) custom-call(bf16[8,640,128]{2,1,0:T(8,128)(2,1)S(1)} %bitcast.6), custom_call_target="tpu_custom_call" | custom-call | tf_op jit(solution)/shard_map/edge_columns/pallas_call | solution.py:517
  3.5 0.2 collective-permute-done.other_ref
  3.7 2.9 %collective-permute-start.1 = (bf16[96,128]{1,0:T(8,128)(2,1)S(1)}, bf16[96,128]{1,0:T(8,128)(2,1)S(1)}, u32[]{:S(2)}, u32[]{:S(2)}) collective-permute-start(bf16[96,128]{1,0:T(8,128)(2,1)S(1)} %half.1), channel_id=1, source_target_pairs={{0,8},{8,0},{16,24},{24,16},{1,9},{9,1},{17,25},{25,17},{2,10},{10... | collective-permute-start | bytes 73736 | tf_op jit(solution)/shard_map/ppermute | solution.py:478
  6.6 0.0 copy-done.1
  6.6 0.9 %inner.2.refs_8_.refs_7_ = f32[5,8,80,128]{3,2,1,0:T(8,128)S(1)} custom-call(bf16[8,640,128]{2,1,0:T(8,128)(2,1)S(1)} %bitcast.7, f32[64,128]{1,0:T(8,128)S(1)} %bitcast.12), custom_call_target="tpu_custom_call" | custom-call | tf_op jit(solution)/shard_map/inner/pallas_call | solution.py:517
  7.5 0.9 %collective-permute-done.1 = bf16[96,128]{1,0:T(8,128)(2,1)S(1)} collective-permute-done((bf16[96,128]{1,0:T(8,128)(2,1)S(1)}, bf16[96,128]{1,0:T(8,128)(2,1)S(1)}, u32[]{:S(2)}, u32[]{:S(2)}) %collective-permute-start.1) | collective-permute-done | bytes 24608 | tf_op jit(solution)/shard_map/ppermute | solution.py:478
  8.4 2.1 %collective-permute-start.2 = (bf16[96,128]{1,0:T(8,128)(2,1)S(1)}, bf16[96,128]{1,0:T(8,128)(2,1)S(1)}, u32[]{:S(2)}, u32[]{:S(2)}) collective-permute-start(bf16[96,128]{1,0:T(8,128)(2,1)S(1)} %add.9), channel_id=1, source_target_pairs={{0,16},{8,24},{16,0},{24,8},{1,17},{9,25},{17,1},{25,9},{2,18},{10... | collective-permute-start | bytes 73736 | tf_op jit(solution)/shard_map/ppermute | solution.py:478
  10.5 0.3 %edge_rows.2 = bf16[8,80,128]{2,1,0:T(8,128)(2,1)S(1)} custom-call(bf16[8,640,128]{2,1,0:T(8,128)(2,1)S(1)} %bitcast.8), custom_call_target="tpu_custom_call" | custom-call | tf_op jit(solution)/shard_map/edge_rows/pallas_call | solution.py:517
  10.8 0.3 %edge_rows.3 = bf16[8,80,128]{2,1,0:T(8,128)(2,1)S(1)} custom-call(bf16[8,640,128]{2,1,0:T(8,128)(2,1)S(1)} %bitcast.9), custom_call_target="tpu_custom_call" | custom-call | tf_op jit(solution)/shard_map/edge_rows/pallas_call | solution.py:517
  11.1 0.0 copy-start.6
  11.1 0.0 copy-start.2
  11.2 0.0 copy-start.3
  11.2 0.0 copy-start.4
  11.2 0.0 copy-start.5
  11.2 0.6 %inner.3.refs_9_.refs_8_ = f32[3,8,80,128]{3,2,1,0:T(8,128)S(1)} custom-call(bf16[8,640,128]{2,1,0:T(8,128)(2,1)S(1)} %bitcast.10, f32[64,128]{1,0:T(8,128)S(1)} %bitcast.13), custom_call_target="tpu_custom_call" | custom-call | tf_op jit(solution)/shard_map/inner/pallas_call | solution.py:517
  11.8 0.5 %collective-permute-done.2 = bf16[96,128]{1,0:T(8,128)(2,1)S(1)} collective-permute-done((bf16[96,128]{1,0:T(8,128)(2,1)S(1)}, bf16[96,128]{1,0:T(8,128)(2,1)S(1)}, u32[]{:S(2)}, u32[]{:S(2)}) %collective-permute-start.2) | collective-permute-done | bytes 24608 | tf_op jit(solution)/shard_map/ppermute | solution.py:478
  12.3 2.1 %collective-permute-start.3 = (bf16[144,128]{1,0:T(8,128)(2,1)S(1)}, bf16[144,128]{1,0:T(8,128)(2,1)S(1)}, u32[]{:S(2)}, u32[]{:S(2)}) collective-permute-start(bf16[144,128]{1,0:T(8,128)(2,1)S(1)} %pad_maximum_fusion), channel_id=1, source_target_pairs={{0,2},{1,3},{2,0},{3,1},{4,6},{5,7},{6,4},{7,5},{8,10},{9,11},{10,... | collective-permute-start | bytes 110600 | tf_op jit(solution)/shard_map/ppermute | solution.py:478
  14.5 1.5 %collective-permute-start.5 = (bf16[8,80,128]{2,1,0:T(8,128)(2,1)S(1)}, bf16[8,80,128]{2,1,0:T(8,128)(2,1)S(1)}, u32[]{:S(2)}, u32[]{:S(2)}) collective-permute-start(bf16[8,80,128]{2,1,0:T(8,128)(2,1)S(1)} %edge_rows.2), channel_id=1, source_target_pairs={{0,8},{8,0},{16,24},{24,16},{1,9},{9,1},{17,25},{25,17},{2,10},{10... | collective-permute-start | bytes 491528 | tf_op jit(solution)/shard_map/ppermute | solution.py:478
  16.0 0.4 %collective-permute-done.3 = bf16[144,128]{1,0:T(8,128)(2,1)S(1)} collective-permute-done((bf16[144,128]{1,0:T(8,128)(2,1)S(1)}, bf16[144,128]{1,0:T(8,128)(2,1)S(1)}, u32[]{:S(2)}, u32[]{:S(2)}) %collective-permute-start.3) | collective-permute-done | bytes 36896 | tf_op jit(solution)/shard_map/ppermute | solution.py:478
  16.4 3.2 %collective-permute-start.4 = (bf16[144,128]{1,0:T(8,128)(2,1)S(1)}, bf16[144,128]{1,0:T(8,128)(2,1)S(1)}, u32[]{:S(2)}, u32[]{:S(2)}) collective-permute-start(bf16[144,128]{1,0:T(8,128)(2,1)S(1)} %pad_maximum_fusion.1), channel_id=1, source_target_pairs={{0,4},{1,5},{2,6},{3,7},{4,0},{5,1},{6,2},{7,3},{8,12},{9,13},{10,... | collective-permute-start | bytes 110600 | tf_op jit(solution)/shard_map/ppermute | solution.py:478
  19.6 2.5 %collective-permute-start.7 = (bf16[8,80,128]{2,1,0:T(8,128)(2,1)S(1)}, bf16[8,80,128]{2,1,0:T(8,128)(2,1)S(1)}, u32[]{:S(2)}, u32[]{:S(2)}) collective-permute-start(bf16[8,80,128]{2,1,0:T(8,128)(2,1)S(1)} %edge_rows.3), channel_id=1, source_target_pairs={{8,16},{16,8},{24,0},{0,24},{9,17},{17,9},{25,1},{1,25},{10,18},{1... | collective-permute-start | bytes 491528 | tf_op jit(solution)/shard_map/ppermute | solution.py:483
  22.0 0.0 collective-permute-done.4.refs_1_
  22.1 0.0 collective-permute-done.5.refs_5_
  22.1 0.1 collective-permute-start.6
  22.2 0.0 copy-done.6
  22.2 0.1 copy.9.refs_6_
  22.3 1.1 %collective-permute-done.6.refs_4_ = bf16[192,128]{1,0:T(8,128)(2,1)S(1)} collective-permute-done((bf16[192,128]{1,0:T(8,128)(2,1)S(1)}, bf16[192,128]{1,0:T(8,128)(2,1)S(1)}, u32[]{:S(2)}, u32[]{:S(2)}) %collective-permute-start.6) | collective-permute-done | bytes 49184 | tf_op jit(solution)/shard_map/ppermute | solution.py:478
  23.4 0.0 copy-done.2
  23.4 0.0 copy-done.3
  23.4 0.0 copy-done.4
  23.4 0.0 copy-done.5
  23.4 4.0 %filter.1 = (f32[80,128]{1,0:T(8,128)S(1)}, f32[80,128]{1,0:T(8,128)S(1)}, bf16[8,80,768]{2,1,0:T(8,128)(2,1)S(1)}, bf16[8,80,768]{2,1,0:T(8,128)(2,1)S(1)}) custom-call(s32[4]{0:T(128)S(1)} %copy-done.2, f32[64]{0:T(128)S(1)} %copy-done.4, f32[64]{0:T(128)S(1)} %copy-done.5, bf16[96,128]{1,0:T(8,128)(2,1)S(1)} %slice.15.refs_3_, ...), custom_call_target="tpu_custom_call" | custom-call | flops 1000000000 | tf_op jit(solution)/shard_map/filter/pallas_call | solution.py:616
  27.4 0.0 collective-permute-done.7.refs_6_
  27.4 1.8 %analysis.1 = bf16[8,640,128]{2,1,0:T(8,128)(2,1)} custom-call(f32[80,128]{1,0:T(8,128)S(1)} %get-tuple-element.53.refs_0_, f32[80,128]{1,0:T(8,128)S(1)} %get-tuple-element.54.refs_1_, bf16[8,80,768]{2,1,0:T(8,128)(2,1)S(1)} %get-tuple-element.55.refs_2_, bf16[8,80,768]{2,1,0:T(8,128)(2,1)S(1)} %get-tuple-element.56.refs_3_, f32[64,128]{1,0:T(8,128)S(1)} %bitcast.15, ...), custom_call_target="tpu_custom_call" | custom-call | tf_op jit(solution)/shard_map/analysis/pallas_call | solution.py:628
  (10 shorter events, 0.1 us)
Async XLA Ops:
  0.0 2.8 %copy-start = (bf16[2,4,80,8,128]{4,3,2,1,0:T(8,128)(2,1)S(1)}, bf16[2,4,80,8,128]{4,3,2,1,0:T(8,128)(2,1)}, u32[]{:S(2)}) copy-start(bf16[2,4,80,8,128]{4,3,2,1,0:T(8,128)(2,1)} %param.8) | copy-start | bytes 3932164
  0.0 6.6 %copy-start.1 = (f32[2,4,8,128]{3,2,1,0:T(8,128)S(1)}, f32[2,4,8,128]{3,2,1,0:T(8,128)}, u32[]{:S(2)}) copy-start(f32[2,4,8,128]{3,2,1,0:T(8,128)} %param.9) | copy-start | bytes 98308
  2.2 1.4 %collective-permute-start = (bf16[176,128]{1,0:T(8,128)(2,1)S(1)}, bf16[176,128]{1,0:T(8,128)(2,1)S(1)}, u32[]{:S(2)}, u32[]{:S(2)}) collective-permute-start(bf16[176,128]{1,0:T(8,128)(2,1)S(1)} %observe.1.full_ref), channel_id=1, source_target_pairs={{0,1},{1,0},{2,3},{3,2},{4,5},{5,4},{6,7},{7,6},{8,9},{9,8},{10,11... | collective-permute-start | bytes 135176 | tf_op jit(solution)/shard_map/ppermute | solution.py:478
  3.7 4.7 %collective-permute-start.1 = (bf16[96,128]{1,0:T(8,128)(2,1)S(1)}, bf16[96,128]{1,0:T(8,128)(2,1)S(1)}, u32[]{:S(2)}, u32[]{:S(2)}) collective-permute-start(bf16[96,128]{1,0:T(8,128)(2,1)S(1)} %half.1), channel_id=1, source_target_pairs={{0,8},{8,0},{16,24},{24,16},{1,9},{9,1},{17,25},{25,17},{2,10},{10... | collective-permute-start | bytes 73736 | tf_op jit(solution)/shard_map/ppermute | solution.py:478
  8.4 3.9 %collective-permute-start.2 = (bf16[96,128]{1,0:T(8,128)(2,1)S(1)}, bf16[96,128]{1,0:T(8,128)(2,1)S(1)}, u32[]{:S(2)}, u32[]{:S(2)}) collective-permute-start(bf16[96,128]{1,0:T(8,128)(2,1)S(1)} %add.9), channel_id=1, source_target_pairs={{0,16},{8,24},{16,0},{24,8},{1,17},{9,25},{17,1},{25,9},{2,18},{10... | collective-permute-start | bytes 73736 | tf_op jit(solution)/shard_map/ppermute | solution.py:478
  11.1 11.0 %copy-start.6 = (s32[64,2]{0,1:T(2,128)S(1)}, s32[64,2]{0,1:T(2,128)}, u32[]{:S(2)}) copy-start(s32[64,2]{0,1:T(2,128)} %param.14) | copy-start | bytes 1540
  11.1 12.2 %copy-start.2 = (s32[4]{0:T(128)S(1)}, s32[4]{0:T(128)}, u32[]{:S(2)}) copy-start(s32[4]{0:T(128)} %refs_0_.1) | copy-start | bytes 52
  11.2 12.2 %copy-start.3 = (s32[64]{0:T(128)S(1)}, s32[64]{0:T(128)}, u32[]{:S(2)}) copy-start(s32[64]{0:T(128)} %param.10) | copy-start | bytes 772
  11.2 12.2 %copy-start.4 = (f32[64]{0:T(128)S(1)}, f32[64]{0:T(128)}, u32[]{:S(2)}) copy-start(f32[64]{0:T(128)} %refs_1_.1) | copy-start | bytes 772
  11.2 12.2 %copy-start.5 = (f32[64]{0:T(128)S(1)}, f32[64]{0:T(128)}, u32[]{:S(2)}) copy-start(f32[64]{0:T(128)} %refs_2_.1) | copy-start | bytes 772
  12.3 4.1 %collective-permute-start.3 = (bf16[144,128]{1,0:T(8,128)(2,1)S(1)}, bf16[144,128]{1,0:T(8,128)(2,1)S(1)}, u32[]{:S(2)}, u32[]{:S(2)}) collective-permute-start(bf16[144,128]{1,0:T(8,128)(2,1)S(1)} %pad_maximum_fusion), channel_id=1, source_target_pairs={{0,2},{1,3},{2,0},{3,1},{4,6},{5,7},{6,4},{7,5},{8,10},{9,11},{10,... | collective-permute-start | bytes 110600 | tf_op jit(solution)/shard_map/ppermute | solution.py:478
  14.5 7.6 %collective-permute-start.5 = (bf16[8,80,128]{2,1,0:T(8,128)(2,1)S(1)}, bf16[8,80,128]{2,1,0:T(8,128)(2,1)S(1)}, u32[]{:S(2)}, u32[]{:S(2)}) collective-permute-start(bf16[8,80,128]{2,1,0:T(8,128)(2,1)S(1)} %edge_rows.2), channel_id=1, source_target_pairs={{0,8},{8,0},{16,24},{24,16},{1,9},{9,1},{17,25},{25,17},{2,10},{10... | collective-permute-start | bytes 491528 | tf_op jit(solution)/shard_map/ppermute | solution.py:478
  16.4 5.6 %collective-permute-start.4 = (bf16[144,128]{1,0:T(8,128)(2,1)S(1)}, bf16[144,128]{1,0:T(8,128)(2,1)S(1)}, u32[]{:S(2)}, u32[]{:S(2)}) collective-permute-start(bf16[144,128]{1,0:T(8,128)(2,1)S(1)} %pad_maximum_fusion.1), channel_id=1, source_target_pairs={{0,4},{1,5},{2,6},{3,7},{4,0},{5,1},{6,2},{7,3},{8,12},{9,13},{10,... | collective-permute-start | bytes 110600 | tf_op jit(solution)/shard_map/ppermute | solution.py:478
  19.6 7.8 %collective-permute-start.7 = (bf16[8,80,128]{2,1,0:T(8,128)(2,1)S(1)}, bf16[8,80,128]{2,1,0:T(8,128)(2,1)S(1)}, u32[]{:S(2)}, u32[]{:S(2)}) collective-permute-start(bf16[8,80,128]{2,1,0:T(8,128)(2,1)S(1)} %edge_rows.3), channel_id=1, source_target_pairs={{8,16},{16,8},{24,0},{0,24},{9,17},{17,9},{25,1},{1,25},{10,18},{1... | collective-permute-start | bytes 491528 | tf_op jit(solution)/shard_map/ppermute | solution.py:483
  22.1 1.3 %collective-permute-start.6 = (bf16[192,128]{1,0:T(8,128)(2,1)S(1)}, bf16[192,128]{1,0:T(8,128)(2,1)S(1)}, u32[]{:S(2)}, u32[]{:S(2)}) collective-permute-start(bf16[192,128]{1,0:T(8,128)(2,1)S(1)} %join.1), channel_id=1, source_target_pairs={{0,1},{1,0},{2,3},{3,2},{4,5},{5,4},{6,7},{7,6},{8,9},{9,8},{10,11... | collective-permute-start | bytes 147464 | tf_op jit(solution)/shard_map/ppermute | solution.py:478

commit v6 on v5

--- a/solution.py
+++ b/solution.py
@@ -59,7 +59,7 @@
     ]
     for copy in large:
         copy.start()
-    for copy in small:
+    for copy in small[:3]:
         copy.wait()
     rows = courant_ref.shape[0] // (2 * levels)
     members = depth // rows
@@ -91,6 +91,7 @@
     far_col = jnp.where(from_west, cols - 1, jnp.where(from_east, 0, jnp.where(above, col, -1)))
     far_row = jnp.where(from_south, rows - 1, jnp.where(from_north, 0, row))
 
+    small[3].wait()
     down = iota((cols, LANES), 0)
     picked = jnp.dot(
         courant_ref[...], (down == col[:1]).astype(F32), precision=HIGHEST, preferred_element_type=F32
@@ -462,13 +463,12 @@
             else:
                 f = f + (north[r:] * has_north) * jnp.where(lat_even, near, far)
             split_store(f, edge_hi_ref, edge_lo_ref, p, 0 if r == 0 else cols)
-    for p in range(planes):
         for h_ref, l_ref, which in ((hi_ref, lo_ref, range(1, rows - 1)), (edge_hi_ref, edge_lo_ref, (0, rows - 1))):
             stacked = jnp.concatenate([h_ref[p], h_ref[p], l_ref[p]], axis=0)
             result = jnp.dot(terms, stacked, preferred_element_type=F32)
             for i, r in enumerate(which):
-                wide_ref[p % 2, pl.ds(r, members, stride=rows), :] = result[:, i * cols : (i + 1) * cols]
-        out_ref[p] = wide_ref[p % 2].astype(BF16)
+                wide_ref[p, pl.ds(r, members, stride=rows), :] = result[:, i * cols : (i + 1) * cols]
+        out_ref[p] = wide_ref[p].astype(BF16)
         pltpu.make_async_copy(out_ref.at[p], out_hbm.at[p], out_sem.at[p]).start()
     for p in range(planes):
         pltpu.make_async_copy(out_ref.at[p], out_hbm.at[p], out_sem.at[p]).wait()
@@ -634,7 +634,7 @@
             edge_type,
             edge_type,
             pltpu.VMEM((planes, depth, cols), BF16),
-            pltpu.VMEM((2, depth, cols), F32),
+            pltpu.VMEM((planes, depth, cols), F32),
             pltpu.SemaphoreType.DMA((planes,)),
         ],
         compiler_params=PARAMS,

time: 29.4 us -> 29.4 us (level)
  no operation moved by 1% of the time
where the time goes in v6:
time: 29.4 us; the launch traced here: 29.3 us
  starting transfers between devices  14.9 us (51%)
  Pallas kernels  11 us (37%)
  waiting for transfers between devices  3.1 us (11%)
    ppermute x7, starting transfers between devices, exchanged(): lax.ppermute(x, axis, [(i, i ^ step) for i in range(lax.axis_size(axis))])  12.4 us
    pallas_call x1, Pallas kernels, per_device(): pl.pallas_call(functools.partial(filter_kernel, n_lon, levels, parts), ou...  4.02 us
    ppermute x7, waiting for transfers between devices, exchanged(): lax.ppermute(x, axis, [(i, i ^ step) for i in range(lax.axis_size(axis))])  3.1 us
    pallas_call x7, Pallas kernels, local(): pl.pallas_call(kernel, out_shape=out, in_specs=[VMEM] * len(operands), ou...  2.89 us
    ppermute x1, starting transfers between devices, exchanged_odd(): lax.ppermute(x, axis, [pair for i in range(1, count, 2) for pair in ((i,...  2.45 us
    pallas_call x1, Pallas kernels, per_device(): pl.pallas_call(functools.partial(observe_kernel, n_lon, levels), out_shap...  2.22 us
    pallas_call x1, Pallas kernels, per_device(): pl.pallas_call(functools.partial(analysis_kernel, n_lat, levels, parts),...  1.82 us
  transfers between devices with their start and end apart: 8, of which 5 were waited for; matrix products, arithmetic and copies ran while one was open for 0% of the time, Pallas kernels for 24%

profile of v6, /device:TPU:0, one launch (start us, length us, event | category | flops | bytes accessed | tf_op | source)
XLA Modules:
  0.0 29.3 jit_solution(8103755632568275309)
XLA Ops:
  0.0 0.0 copy-start
  0.0 0.0 copy-start.1
  0.0 2.2 %observe.1.full_ref = bf16[176,128]{1,0:T(8,128)(2,1)S(1)} custom-call(bf16[8,640,128]{2,1,0:T(8,128)(2,1)} %bitcast.5, f32[64,128]{1,0:T(8,128)} %bitcast.11, s32[1,64]{1,0:T(1,128)} %bitcast.16, s32[1,64]{1,0:T(1,128)} %bitcast.18, s32[4]{0:T(128)} %refs_0_.1), custom_call_target="tpu_custom_call" | custom-call | tf_op jit(solution)/shard_map/observe/pallas_call | solution.py:497
  2.2 0.5 %collective-permute-start = (bf16[176,128]{1,0:T(8,128)(2,1)S(1)}, bf16[176,128]{1,0:T(8,128)(2,1)S(1)}, u32[]{:S(2)}, u32[]{:S(2)}) collective-permute-start(bf16[176,128]{1,0:T(8,128)(2,1)S(1)} %observe.1.full_ref), channel_id=1, source_target_pairs={{0,1},{1,0},{2,3},{3,2},{4,5},{5,4},{6,7},{7,6},{8,9},{9,8},{10,11... | collective-permute-start | bytes 135176 | tf_op jit(solution)/shard_map/ppermute | solution.py:478
  2.8 0.0 copy-done
  2.8 0.7 %edge_columns.1 = (bf16[48,128]{1,0:T(8,128)(2,1)S(1)}, bf16[48,128]{1,0:T(8,128)(2,1)S(1)}) custom-call(bf16[8,640,128]{2,1,0:T(8,128)(2,1)S(1)} %bitcast.6), custom_call_target="tpu_custom_call" | custom-call | tf_op jit(solution)/shard_map/edge_columns/pallas_call | solution.py:517
  3.5 0.2 collective-permute-done.other_ref
  3.7 2.9 %collective-permute-start.1 = (bf16[96,128]{1,0:T(8,128)(2,1)S(1)}, bf16[96,128]{1,0:T(8,128)(2,1)S(1)}, u32[]{:S(2)}, u32[]{:S(2)}) collective-permute-start(bf16[96,128]{1,0:T(8,128)(2,1)S(1)} %half.1), channel_id=1, source_target_pairs={{0,8},{8,0},{16,24},{24,16},{1,9},{9,1},{17,25},{25,17},{2,10},{10... | collective-permute-start | bytes 73736 | tf_op jit(solution)/shard_map/ppermute | solution.py:478
  6.6 0.0 copy-done.1
  6.6 0.9 %inner.2.refs_8_.refs_7_ = f32[5,8,80,128]{3,2,1,0:T(8,128)S(1)} custom-call(bf16[8,640,128]{2,1,0:T(8,128)(2,1)S(1)} %bitcast.7, f32[64,128]{1,0:T(8,128)S(1)} %bitcast.12), custom_call_target="tpu_custom_call" | custom-call | tf_op jit(solution)/shard_map/inner/pallas_call | solution.py:517
  7.5 0.9 %collective-permute-done.1 = bf16[96,128]{1,0:T(8,128)(2,1)S(1)} collective-permute-done((bf16[96,128]{1,0:T(8,128)(2,1)S(1)}, bf16[96,128]{1,0:T(8,128)(2,1)S(1)}, u32[]{:S(2)}, u32[]{:S(2)}) %collective-permute-start.1) | collective-permute-done | bytes 24608 | tf_op jit(solution)/shard_map/ppermute | solution.py:478
  8.4 2.1 %collective-permute-start.2 = (bf16[96,128]{1,0:T(8,128)(2,1)S(1)}, bf16[96,128]{1,0:T(8,128)(2,1)S(1)}, u32[]{:S(2)}, u32[]{:S(2)}) collective-permute-start(bf16[96,128]{1,0:T(8,128)(2,1)S(1)} %add.9), channel_id=1, source_target_pairs={{0,16},{8,24},{16,0},{24,8},{1,17},{9,25},{17,1},{25,9},{2,18},{10... | collective-permute-start | bytes 73736 | tf_op jit(solution)/shard_map/ppermute | solution.py:478
  10.5 0.3 %edge_rows.2 = bf16[8,80,128]{2,1,0:T(8,128)(2,1)S(1)} custom-call(bf16[8,640,128]{2,1,0:T(8,128)(2,1)S(1)} %bitcast.8), custom_call_target="tpu_custom_call" | custom-call | tf_op jit(solution)/shard_map/edge_rows/pallas_call | solution.py:517
  10.8 0.3 %edge_rows.3 = bf16[8,80,128]{2,1,0:T(8,128)(2,1)S(1)} custom-call(bf16[8,640,128]{2,1,0:T(8,128)(2,1)S(1)} %bitcast.9), custom_call_target="tpu_custom_call" | custom-call | tf_op jit(solution)/shard_map/edge_rows/pallas_call | solution.py:517
  11.1 0.0 copy-start.6
  11.1 0.0 copy-start.2
  11.2 0.0 copy-start.3
  11.2 0.0 copy-start.4
  11.2 0.0 copy-start.5
  11.2 0.6 %inner.3.refs_9_.refs_8_ = f32[3,8,80,128]{3,2,1,0:T(8,128)S(1)} custom-call(bf16[8,640,128]{2,1,0:T(8,128)(2,1)S(1)} %bitcast.10, f32[64,128]{1,0:T(8,128)S(1)} %bitcast.13), custom_call_target="tpu_custom_call" | custom-call | tf_op jit(solution)/shard_map/inner/pallas_call | solution.py:517
  11.8 0.5 %collective-permute-done.2 = bf16[96,128]{1,0:T(8,128)(2,1)S(1)} collective-permute-done((bf16[96,128]{1,0:T(8,128)(2,1)S(1)}, bf16[96,128]{1,0:T(8,128)(2,1)S(1)}, u32[]{:S(2)}, u32[]{:S(2)}) %collective-permute-start.2) | collective-permute-done | bytes 24608 | tf_op jit(solution)/shard_map/ppermute | solution.py:478
  12.3 2.1 %collective-permute-start.3 = (bf16[144,128]{1,0:T(8,128)(2,1)S(1)}, bf16[144,128]{1,0:T(8,128)(2,1)S(1)}, u32[]{:S(2)}, u32[]{:S(2)}) collective-permute-start(bf16[144,128]{1,0:T(8,128)(2,1)S(1)} %pad_maximum_fusion), channel_id=1, source_target_pairs={{0,2},{1,3},{2,0},{3,1},{4,6},{5,7},{6,4},{7,5},{8,10},{9,11},{10,... | collective-permute-start | bytes 110600 | tf_op jit(solution)/shard_map/ppermute | solution.py:478
  14.5 1.5 %collective-permute-start.5 = (bf16[8,80,128]{2,1,0:T(8,128)(2,1)S(1)}, bf16[8,80,128]{2,1,0:T(8,128)(2,1)S(1)}, u32[]{:S(2)}, u32[]{:S(2)}) collective-permute-start(bf16[8,80,128]{2,1,0:T(8,128)(2,1)S(1)} %edge_rows.2), channel_id=1, source_target_pairs={{0,8},{8,0},{16,24},{24,16},{1,9},{9,1},{17,25},{25,17},{2,10},{10... | collective-permute-start | bytes 491528 | tf_op jit(solution)/shard_map/ppermute | solution.py:478
  16.0 0.4 %collective-permute-done.3 = bf16[144,128]{1,0:T(8,128)(2,1)S(1)} collective-permute-done((bf16[144,128]{1,0:T(8,128)(2,1)S(1)}, bf16[144,128]{1,0:T(8,128)(2,1)S(1)}, u32[]{:S(2)}, u32[]{:S(2)}) %collective-permute-start.3) | collective-permute-done | bytes 36896 | tf_op jit(solution)/shard_map/ppermute | solution.py:478
  16.4 3.2 %collective-permute-start.4 = (bf16[144,128]{1,0:T(8,128)(2,1)S(1)}, bf16[144,128]{1,0:T(8,128)(2,1)S(1)}, u32[]{:S(2)}, u32[]{:S(2)}) collective-permute-start(bf16[144,128]{1,0:T(8,128)(2,1)S(1)} %pad_maximum_fusion.1), channel_id=1, source_target_pairs={{0,4},{1,5},{2,6},{3,7},{4,0},{5,1},{6,2},{7,3},{8,12},{9,13},{10,... | collective-permute-start | bytes 110600 | tf_op jit(solution)/shard_map/ppermute | solution.py:478
  19.6 2.5 %collective-permute-start.7 = (bf16[8,80,128]{2,1,0:T(8,128)(2,1)S(1)}, bf16[8,80,128]{2,1,0:T(8,128)(2,1)S(1)}, u32[]{:S(2)}, u32[]{:S(2)}) collective-permute-start(bf16[8,80,128]{2,1,0:T(8,128)(2,1)S(1)} %edge_rows.3), channel_id=1, source_target_pairs={{8,16},{16,8},{24,0},{0,24},{9,17},{17,9},{25,1},{1,25},{10,18},{1... | collective-permute-start | bytes 491528 | tf_op jit(solution)/shard_map/ppermute | solution.py:483
  22.0 0.0 collective-permute-done.4.refs_1_
  22.1 0.0 collective-permute-done.5.refs_5_
  22.1 0.1 collective-permute-start.6
  22.2 0.0 copy-done.6
  22.2 0.1 copy.9.refs_6_
  22.3 1.1 %collective-permute-done.6.refs_4_ = bf16[192,128]{1,0:T(8,128)(2,1)S(1)} collective-permute-done((bf16[192,128]{1,0:T(8,128)(2,1)S(1)}, bf16[192,128]{1,0:T(8,128)(2,1)S(1)}, u32[]{:S(2)}, u32[]{:S(2)}) %collective-permute-start.6) | collective-permute-done | bytes 49184 | tf_op jit(solution)/shard_map/ppermute | solution.py:478
  23.4 0.0 copy-done.2
  23.4 0.0 copy-done.3
  23.4 0.0 copy-done.4
  23.4 0.0 copy-done.5
  23.4 4.0 %filter.1 = (f32[80,128]{1,0:T(8,128)S(1)}, f32[80,128]{1,0:T(8,128)S(1)}, bf16[8,80,768]{2,1,0:T(8,128)(2,1)S(1)}, bf16[8,80,768]{2,1,0:T(8,128)(2,1)S(1)}) custom-call(s32[4]{0:T(128)S(1)} %copy-done.2, f32[64]{0:T(128)S(1)} %copy-done.4, f32[64]{0:T(128)S(1)} %copy-done.5, bf16[96,128]{1,0:T(8,128)(2,1)S(1)} %slice.15.refs_3_, ...), custom_call_target="tpu_custom_call" | custom-call | flops 1000000000 | tf_op jit(solution)/shard_map/filter/pallas_call | solution.py:616
  27.4 0.0 collective-permute-done.7.refs_6_
  27.4 1.8 %analysis.1 = bf16[8,640,128]{2,1,0:T(8,128)(2,1)} custom-call(f32[80,128]{1,0:T(8,128)S(1)} %get-tuple-element.53.refs_0_, f32[80,128]{1,0:T(8,128)S(1)} %get-tuple-element.54.refs_1_, bf16[8,80,768]{2,1,0:T(8,128)(2,1)S(1)} %get-tuple-element.55.refs_2_, bf16[8,80,768]{2,1,0:T(8,128)(2,1)S(1)} %get-tuple-element.56.refs_3_, f32[64,128]{1,0:T(8,128)S(1)} %bitcast.15, ...), custom_call_target="tpu_custom_call" | custom-call | tf_op jit(solution)/shard_map/analysis/pallas_call | solution.py:628
  (10 shorter events, 0.1 us)
Async XLA Ops:
  0.0 2.8 %copy-start = (bf16[2,4,80,8,128]{4,3,2,1,0:T(8,128)(2,1)S(1)}, bf16[2,4,80,8,128]{4,3,2,1,0:T(8,128)(2,1)}, u32[]{:S(2)}) copy-start(bf16[2,4,80,8,128]{4,3,2,1,0:T(8,128)(2,1)} %param.8) | copy-start | bytes 3932164
  0.0 6.6 %copy-start.1 = (f32[2,4,8,128]{3,2,1,0:T(8,128)S(1)}, f32[2,4,8,128]{3,2,1,0:T(8,128)}, u32[]{:S(2)}) copy-start(f32[2,4,8,128]{3,2,1,0:T(8,128)} %param.9) | copy-start | bytes 98308
  2.2 1.4 %collective-permute-start = (bf16[176,128]{1,0:T(8,128)(2,1)S(1)}, bf16[176,128]{1,0:T(8,128)(2,1)S(1)}, u32[]{:S(2)}, u32[]{:S(2)}) collective-permute-start(bf16[176,128]{1,0:T(8,128)(2,1)S(1)} %observe.1.full_ref), channel_id=1, source_target_pairs={{0,1},{1,0},{2,3},{3,2},{4,5},{5,4},{6,7},{7,6},{8,9},{9,8},{10,11... | collective-permute-start | bytes 135176 | tf_op jit(solution)/shard_map/ppermute | solution.py:478
  3.7 4.7 %collective-permute-start.1 = (bf16[96,128]{1,0:T(8,128)(2,1)S(1)}, bf16[96,128]{1,0:T(8,128)(2,1)S(1)}, u32[]{:S(2)}, u32[]{:S(2)}) collective-permute-start(bf16[96,128]{1,0:T(8,128)(2,1)S(1)} %half.1), channel_id=1, source_target_pairs={{0,8},{8,0},{16,24},{24,16},{1,9},{9,1},{17,25},{25,17},{2,10},{10... | collective-permute-start | bytes 73736 | tf_op jit(solution)/shard_map/ppermute | solution.py:478
  8.4 3.9 %collective-permute-start.2 = (bf16[96,128]{1,0:T(8,128)(2,1)S(1)}, bf16[96,128]{1,0:T(8,128)(2,1)S(1)}, u32[]{:S(2)}, u32[]{:S(2)}) collective-permute-start(bf16[96,128]{1,0:T(8,128)(2,1)S(1)} %add.9), channel_id=1, source_target_pairs={{0,16},{8,24},{16,0},{24,8},{1,17},{9,25},{17,1},{25,9},{2,18},{10... | collective-permute-start | bytes 73736 | tf_op jit(solution)/shard_map/ppermute | solution.py:478
  11.1 11.0 %copy-start.6 = (s32[64,2]{0,1:T(2,128)S(1)}, s32[64,2]{0,1:T(2,128)}, u32[]{:S(2)}) copy-start(s32[64,2]{0,1:T(2,128)} %param.14) | copy-start | bytes 1540
  11.1 12.2 %copy-start.2 = (s32[4]{0:T(128)S(1)}, s32[4]{0:T(128)}, u32[]{:S(2)}) copy-start(s32[4]{0:T(128)} %refs_0_.1) | copy-start | bytes 52
  11.2 12.2 %copy-start.3 = (s32[64]{0:T(128)S(1)}, s32[64]{0:T(128)}, u32[]{:S(2)}) copy-start(s32[64]{0:T(128)} %param.10) | copy-start | bytes 772
  11.2 12.2 %copy-start.4 = (f32[64]{0:T(128)S(1)}, f32[64]{0:T(128)}, u32[]{:S(2)}) copy-start(f32[64]{0:T(128)} %refs_1_.1) | copy-start | bytes 772
  11.2 12.2 %copy-start.5 = (f32[64]{0:T(128)S(1)}, f32[64]{0:T(128)}, u32[]{:S(2)}) copy-start(f32[64]{0:T(128)} %refs_2_.1) | copy-start | bytes 772
  12.3 4.1 %collective-permute-start.3 = (bf16[144,128]{1,0:T(8,128)(2,1)S(1)}, bf16[144,128]{1,0:T(8,128)(2,1)S(1)}, u32[]{:S(2)}, u32[]{:S(2)}) collective-permute-start(bf16[144,128]{1,0:T(8,128)(2,1)S(1)} %pad_maximum_fusion), channel_id=1, source_target_pairs={{0,2},{1,3},{2,0},{3,1},{4,6},{5,7},{6,4},{7,5},{8,10},{9,11},{10,... | collective-permute-start | bytes 110600 | tf_op jit(solution)/shard_map/ppermute | solution.py:478
  14.5 7.6 %collective-permute-start.5 = (bf16[8,80,128]{2,1,0:T(8,128)(2,1)S(1)}, bf16[8,80,128]{2,1,0:T(8,128)(2,1)S(1)}, u32[]{:S(2)}, u32[]{:S(2)}) collective-permute-start(bf16[8,80,128]{2,1,0:T(8,128)(2,1)S(1)} %edge_rows.2), channel_id=1, source_target_pairs={{0,8},{8,0},{16,24},{24,16},{1,9},{9,1},{17,25},{25,17},{2,10},{10... | collective-permute-start | bytes 491528 | tf_op jit(solution)/shard_map/ppermute | solution.py:478
  16.4 5.6 %collective-permute-start.4 = (bf16[144,128]{1,0:T(8,128)(2,1)S(1)}, bf16[144,128]{1,0:T(8,128)(2,1)S(1)}, u32[]{:S(2)}, u32[]{:S(2)}) collective-permute-start(bf16[144,128]{1,0:T(8,128)(2,1)S(1)} %pad_maximum_fusion.1), channel_id=1, source_target_pairs={{0,4},{1,5},{2,6},{3,7},{4,0},{5,1},{6,2},{7,3},{8,12},{9,13},{10,... | collective-permute-start | bytes 110600 | tf_op jit(solution)/shard_map/ppermute | solution.py:478
  19.6 7.8 %collective-permute-start.7 = (bf16[8,80,128]{2,1,0:T(8,128)(2,1)S(1)}, bf16[8,80,128]{2,1,0:T(8,128)(2,1)S(1)}, u32[]{:S(2)}, u32[]{:S(2)}) collective-permute-start(bf16[8,80,128]{2,1,0:T(8,128)(2,1)S(1)} %edge_rows.3), channel_id=1, source_target_pairs={{8,16},{16,8},{24,0},{0,24},{9,17},{17,9},{25,1},{1,25},{10,18},{1... | collective-permute-start | bytes 491528 | tf_op jit(solution)/shard_map/ppermute | solution.py:483
  22.1 1.3 %collective-permute-start.6 = (bf16[192,128]{1,0:T(8,128)(2,1)S(1)}, bf16[192,128]{1,0:T(8,128)(2,1)S(1)}, u32[]{:S(2)}, u32[]{:S(2)}) collective-permute-start(bf16[192,128]{1,0:T(8,128)(2,1)S(1)} %join.1), channel_id=1, source_target_pairs={{0,1},{1,0},{2,3},{3,2},{4,5},{5,4},{6,7},{7,6},{8,9},{9,8},{10,11... | collective-permute-start | bytes 147464 | tf_op jit(solution)/shard_map/ppermute | solution.py:478
